TPU v7x, 32 devices: a whole 2x2x4 slice. The times are simulated.
32 devices in a mesh: groups: 2 (over x), series: 16 (over z, y, core).
Axes of the slice: x: 2, y: 2, z: 4, core: 2. Of those that a mesh axis runs over, the one named last changes fastest.
Arguments:
- series_data: bfloat16 [65536, 1024], P(('groups', 'series')), parts along dimension 0, may hold values from -90 to 90
- sketch_matrix: bfloat16 [2048, 256], P(('groups', 'series')), parts along dimension 0, may hold values from -0.1875 to 0.1875
Outputs:
- range_basis: bfloat16 [65536, 256], P(('groups', 'series')), parts along dimension 0
- coefficients: bfloat16 [2048, 256], P(('groups', 'series')), parts along dimension 0
There are 2 independent parts, one for each index of `groups`. A program takes and returns all parts, laid end to end along the dimension named above; each array names one. Nothing has to cross between parts.
All inputs are finite; a program needn't handle non-finite values.
Results may differ from a plain program's by a relative error of at most 0.0054.
Values may be sent and summed in bfloat16 or wider, within the bound.
No kernel may reach another device: no remote copies, remote signals or barrier semaphores. Data moves between devices by JAX's collectives and lax.ppermute only.
A program may use at most 64 MiB of HBM per device.

v0:
```python
import math

import jax
import jax.numpy as jnp
from jax import lax
from jax.sharding import PartitionSpec as P


def orthonormal(panel_rows, rows_total):
    partial_gram = jnp.dot(
        panel_rows.T,
        panel_rows,
        precision=lax.Precision.HIGHEST,
        preferred_element_type=jnp.float32,
    )
    gram_sum = lax.psum(partial_gram, "series") / rows_total
    lower_factor = jnp.linalg.cholesky(gram_sum)
    identity_k = jnp.eye(panel_rows.shape[1], dtype=jnp.float32)
    inverse = jax.scipy.linalg.solve_triangular(lower_factor, identity_k, lower=True)
    return jnp.dot(
        panel_rows, inverse.T, precision=lax.Precision.HIGHEST, preferred_element_type=jnp.float32
    ).astype(jnp.bfloat16)


def body(series_data, sketch_matrix):
    devices_here = lax.axis_size("series")
    rows_total = series_data.shape[0] * devices_here
    local_steps = sketch_matrix.shape[0]
    time_steps = local_steps * devices_here
    factor = math.sqrt(time_steps) / rows_total

    def accumulate(portion):
        return jnp.dot(series_data, portion, preferred_element_type=jnp.float32)

    sketch = accumulate(lax.all_gather(sketch_matrix, "series", axis=0, tiled=True))
    basis = orthonormal(sketch, rows_total)
    columns = series_data
    summed = lax.dot_general(
        columns, basis, (((0,), (0,)), ((), ())), preferred_element_type=jnp.float32
    )
    back_rows = lax.psum_scatter(summed * factor, "series", scatter_dimension=0, tiled=True).astype(
        jnp.bfloat16
    )
    power = accumulate(lax.all_gather(back_rows, "series", axis=0, tiled=True))
    range_basis = orthonormal(power, rows_total)
    columns = series_data
    summed = lax.dot_general(
        columns, range_basis, (((0,), (0,)), ((), ())), preferred_element_type=jnp.float32
    )
    coefficients = lax.psum_scatter(
        summed * factor, "series", scatter_dimension=0, tiled=True
    ).astype(jnp.bfloat16)
    return (range_basis, coefficients)


def solution(mesh):
    in_specs = (P(("groups", "series"), None), P(("groups", "series"), None))
    out_specs = (P(("groups", "series"), None), P(("groups", "series"), None))
    return jax.shard_map(body, mesh=mesh, in_specs=in_specs, out_specs=out_specs, check_vma=False)
```

profile of v0, /device:TPU:0, one launch (start us, length us, event | category | flops | bytes accessed | tf_op | source)
XLA Modules:
  0.0 501.7 jit_solution(1863021078401241186)
XLA Ops:
  7.2 24.8 %all_gather.6 = bf16[1024,256]{1,0:T(8,128)(2,1)S(1)} all-gather(bf16[64,256]{1,0:T(8,128)(2,1)} %param.6), channel_id=1, replica_groups=mesh['groups'=2,'series'=16] {'series'}, dimensions={0}, use_global_device_ids=true | all-gather | bytes 557056 | tf_op jit(solution)/shard_map/all_gather | solution.py:35
  32.0 3.4 fusion.29
  35.4 4.2 fusion.30
  39.6 0.6 reduce-scatter.7.cloned.1.call-start
  40.2 85.6 %all-reduce.4.cloned.1.call-done = f32[256,256]{0,1:T(8,128)} async-done(((f32[256,256]{0,1:T(8,128)}), f32[256,256]{0,1:T(8,128)}) %all-reduce.4.cloned.1.call-update) | async-done | bytes 262160 | tf_op jit(solution)/shard_map/psum | solution.py:16
  125.8 1.0 broadcast_multiply_fusion.1
  127.0 1.0 fusion.9
  128.0 11.7 %cholesky.130 = f32[128,128]{1,0:T(8,128)S(1)} custom-call(f32[128,128]{1,0:T(8,128)S(1)} %cholesky.194), custom_call_target="Cholesky" | custom-call | tf_op jit(solution)/shard_map/jit(cholesky)/cholesky | solution.py:17
  139.7 9.8 %custom-call.13 = f32[1,128,128]{1,2,0:T(8,128)S(1)} custom-call(f32[1,128,128]{2,1,0:T(8,128)S(1)} %get-tuple-element.53), custom_call_target="InvertDiagBlocksLowerTriangular" | custom-call | tf_op jit(solution)/shard_map/jit(cholesky)/cholesky | solution.py:17
  150.0 11.7 %cholesky.147 = f32[128,128]{1,0:T(8,128)S(1)} custom-call(f32[128,128]{1,0:T(8,128)S(1)} %convolution_subtract_fusion.3), custom_call_target="Cholesky" | custom-call | tf_op jit(solution)/shard_map/jit(cholesky)/cholesky | solution.py:17
  161.8 0.7 compare_reduce_fusion.2
  164.0 4.3 while.4
  164.2 0.6 fusion.57
  164.8 1.4 bitcast_dynamic-update-slice_fusion.4
  166.2 0.6 fusion.57
  166.8 1.4 bitcast_dynamic-update-slice_fusion.4
  168.3 19.7 %custom-call.14 = f32[2,128,128]{1,2,0:T(8,128)S(1)} custom-call(f32[2,128,128]{2,1,0:T(8,128)S(1)} %get-tuple-element.18), custom_call_target="InvertDiagBlocksLowerTriangular" | custom-call | tf_op jit(solution)/shard_map/jit(_solve_triangular)/triangular_solve | solution.py:19
  188.0 0.3 fusion.13
  188.8 1.8 convolution_convert_fusion.1
  190.7 1.3 fusion.1
  192.0 1.3 copy.23
  193.4 58.0 %reduce-scatter.7.cloned.1.call-done = f32[64,256]{1,0:T(8,128)} async-done(((f32[1024,256]{1,0:T(8,128)}), f32[64,256]{1,0:T(8,128)}) %reduce-scatter.7.cloned.1.call-update) | async-done | bytes 65552 | tf_op jit(solution)/shard_map/reduce_scatter | solution.py:41
  251.3 0.8 convert_element_type.20
  252.2 20.9 %all_gather.7 = bf16[1024,256]{1,0:T(8,128)(2,1)S(1)} all-gather(bf16[64,256]{1,0:T(8,128)(2,1)S(1)} %convert_element_type.20), channel_id=1, replica_groups=mesh['groups'=2,'series'=16] {'series'}, dimensions={0}, use_global_device_ids=true | all-gather | bytes 557056 | tf_op jit(solution)/shard_map/all_gather | solution.py:44
  273.0 3.5 fusion.31
  276.5 2.6 fusion.32
  279.4 86.0 %all-reduce.6.cloned.1.call-done = f32[256,256]{0,1:T(8,128)} async-done(((f32[256,256]{0,1:T(8,128)}), f32[256,256]{0,1:T(8,128)}) %all-reduce.6.cloned.1.call-update) | async-done | bytes 262160 | tf_op jit(solution)/shard_map/psum | solution.py:16
  365.4 1.0 broadcast_multiply_fusion
  366.5 1.0 fusion.8
  367.5 11.7 %cholesky.164 = f32[128,128]{1,0:T(8,128)S(1)} custom-call(f32[128,128]{1,0:T(8,128)S(1)} %cholesky.197), custom_call_target="Cholesky" | custom-call | tf_op jit(solution)/shard_map/jit(cholesky)/cholesky | solution.py:17
  379.3 9.8 %custom-call.15 = f32[1,128,128]{1,2,0:T(8,128)S(1)} custom-call(f32[1,128,128]{2,1,0:T(8,128)S(1)} %get-tuple-element.49), custom_call_target="InvertDiagBlocksLowerTriangular" | custom-call | tf_op jit(solution)/shard_map/jit(cholesky)/cholesky | solution.py:17
  389.6 11.7 %cholesky.181 = f32[128,128]{1,0:T(8,128)S(1)} custom-call(f32[128,128]{1,0:T(8,128)S(1)} %convolution_subtract_fusion.2), custom_call_target="Cholesky" | custom-call | tf_op jit(solution)/shard_map/jit(cholesky)/cholesky | solution.py:17
  401.3 0.7 compare_reduce_fusion
  402.0 0.6 compare_reduce_fusion.1
  404.1 4.4 while.5
  404.4 0.6 fusion.58
  404.9 1.4 bitcast_dynamic-update-slice_fusion.5
  406.4 0.6 fusion.58
  407.0 1.4 bitcast_dynamic-update-slice_fusion.5
  408.4 19.7 %custom-call.16 = f32[2,128,128]{1,2,0:T(8,128)S(1)} custom-call(f32[2,128,128]{2,1,0:T(8,128)S(1)} %get-tuple-element.19), custom_call_target="InvertDiagBlocksLowerTriangular" | custom-call | tf_op jit(solution)/shard_map/jit(_solve_triangular)/triangular_solve | solution.py:19
  428.1 0.3 fusion.11
  428.7 0.3 fusion.16
  429.0 3.4 convolution_convert_fusion
  432.5 1.3 fusion
  433.8 1.3 copy.25
  435.2 58.0 %reduce-scatter.9.cloned.1.call-done = f32[64,256]{1,0:T(8,128)} async-done(((f32[1024,256]{1,0:T(8,128)}), f32[64,256]{1,0:T(8,128)}) %reduce-scatter.9.cloned.1.call-update) | async-done | bytes 65552
  493.2 0.9 copy.26
  494.1 0.7 copy.20
  (41 shorter events, 2.8 us)
Async XLA Ops:
  7.2 118.7 %all-reduce.4.cloned.1.call-start = ((), (), s32[]{:S(2)}) async-start(), calls=%async_computation.2 | async-start | bytes 524288 | tf_op jit(solution)/shard_map/psum | solution.py:16
  39.6 211.7 %reduce-scatter.7.cloned.1.call-start = ((), (), s32[]{:S(2)}) async-start(), calls=%async_computation.4 | async-start | bytes 1114112 | tf_op jit(solution)/shard_map/reduce_scatter | solution.py:41
  187.9 2.8 copy-start.1
  193.3 172.1 %all-reduce.6.cloned.1.call-start = ((), (), s32[]{:S(2)}) async-start(), calls=%async_computation.3 | async-start | bytes 524288 | tf_op jit(solution)/shard_map/psum | solution.py:16
  279.1 214.1 %reduce-scatter.9.cloned.1.call-start = ((), (), s32[]{:S(2)}) async-start(), calls=%async_computation.5 | async-start | bytes 1114112
  428.1 4.4 copy-start.2
  432.5 1.3 copy-start
Sparse Core Ops, SparseCore 0:
  39.8 86.0 all-reduce.3
  193.4 57.8 reduce-scatter.6
  279.3 86.0 all-reduce.5
  435.3 57.8 reduce-scatter.8
where the time goes:
time: 506 us; the launch traced here: 502 us
  waiting for transfers between devices  288 us (57%)
  other arithmetic  113 us (22%)
  blocking collectives  45.7 us (9%)
  matrix products  24.2 us (5%)
  between operations  17 us (3%)
  local copies, waits for them, and re-layouts  12.8 us (3%)
    psum x2, waiting for transfers between devices, orthonormal(): gram_sum = lax.psum(partial_gram, 'series') / rows_total  172 us
    another operation x13, other arithmetic, orthonormal(): lower_factor = jnp.linalg.cholesky(gram_sum)  68.7 us
    unnamed x5, waiting for transfers between devices  58.1 us
    reduce_scatter x1, waiting for transfers between devices, body(): lax.psum_scatter(summed * factor, 'series', scatter_dimension=0, tiled=True)  58 us
    another operation x5, other arithmetic, orthonormal(): jax.scipy.linalg.solve_triangular(lower_factor, identity_k, lower=True)  39.4 us
    all_gather x1, blocking collectives, body(): lax.all_gather(sketch_matrix, 'series', axis=0, tiled=True)  24.8 us
    all_gather x1, blocking collectives, body(): power = accumulate(lax.all_gather(back_rows, 'series', axis=0, tiled=True))  20.9 us
  transfers between devices with their start and end apart: 4, of which 4 were waited for; matrix products, arithmetic and copies ran while one was open for 0% of the time, Pallas kernels for 0%

commit v1 on v0

v1 whole, which is shorter than its diff:
```python
import math

import jax
import jax.numpy as jnp
from jax import lax
from jax.sharding import PartitionSpec as P

AXIS = "series"
EDGE = 256
CHAINS = 2


def exchange(value, distance):
    n = lax.axis_size(AXIS)
    return lax.ppermute(value, AXIS, [(i, i ^ distance) for i in range(n)])


def piece(value, index, count):
    rows = value.shape[0] // count
    return lax.dynamic_slice_in_dim(value, index * rows, rows, 0)


def scatter_stage(value, low, count):
    me = (lax.axis_index(AXIS) >> low) & (count - 1)
    got = [exchange(piece(value, me ^ k, count), k << low) for k in range(1, count)]
    total = piece(value, me, count)
    for item in got:
        total = total + item
    return total


def gather_stage(value, low, count):
    me = (lax.axis_index(AXIS) >> low) & (count - 1)
    got = [value] + [exchange(value, k << low) for k in range(1, count)]
    if count == 2:
        return jnp.where(me == 0, jnp.concatenate(got), jnp.concatenate(got[::-1]))
    rows = value.shape[0]
    out = jnp.zeros((count * rows,) + value.shape[1:], value.dtype)
    for k in range(count):
        out = lax.dynamic_update_slice_in_dim(out, got[k], (me ^ k) * rows, 0)
    return out


def stages():
    n = lax.axis_size(AXIS)
    return [(0, 2), (1, 2), (2, n // 4)]


def sum_everywhere(value):
    for low, count in stages():
        value = scatter_stage(value, low, count)
    for low, count in reversed(stages()):
        value = gather_stage(value, low, count)
    return value


def gather_rows(value):
    for low, count in stages():
        value = gather_stage(value, low, count)
    return value


def exact(a, b, contract):
    return lax.dot_general(
        a.astype(jnp.float32),
        b.astype(jnp.float32),
        ((contract[0], contract[1]), ((), ())),
        precision=lax.Precision.HIGHEST,
        preferred_element_type=jnp.float32,
    )


def inverse_factor(gram):
    lower_factor = jnp.linalg.cholesky(gram)
    identity_k = jnp.eye(gram.shape[0], dtype=jnp.float32)
    return jax.scipy.linalg.solve_triangular(lower_factor, identity_k, lower=True)


def body(series_data, sketch_matrix):
    devices_here = lax.axis_size(AXIS)
    rows_total = series_data.shape[0] * devices_here
    local_steps = sketch_matrix.shape[0]
    time_steps = local_steps * devices_here
    factor = math.sqrt(time_steps) / rows_total
    nb = time_steps // EDGE

    sketch_all = gather_rows(sketch_matrix)

    blocks = []
    for i in range(nb):
        row = lax.dot_general(
            series_data[:, i * EDGE : (i + 1) * EDGE],
            series_data[:, : (i + 1) * EDGE],
            (((0,), (0,)), ((), ())),
            preferred_element_type=jnp.float32,
        )
        blocks += [row[:, j * EDGE : (j + 1) * EDGE] for j in range(i + 1)]
    per = len(blocks) // CHAINS
    summed = [
        sum_everywhere(jnp.concatenate(blocks[c * per : (c + 1) * per])) for c in range(CHAINS)
    ]
    flat = [s[k * EDGE : (k + 1) * EDGE] for s in summed for k in range(per)]
    at = lambda i, j: flat[i * (i + 1) // 2 + j] if j <= i else flat[j * (j + 1) // 2 + i].T
    moment = jnp.concatenate(
        [jnp.concatenate([at(i, j) for j in range(nb)], axis=1) for i in range(nb)]
    )

    y = exact(moment, sketch_all, ((1,), (0,)))
    inverse = inverse_factor(exact(sketch_all, y, ((0,), (0,))) / rows_total)
    back = (exact(y, inverse, ((1,), (1,))) * factor).astype(jnp.bfloat16)
    z = exact(moment, back, ((1,), (0,)))
    inverse2 = inverse_factor(exact(back, z, ((0,), (0,))) / rows_total)
    power = jnp.dot(series_data, back, preferred_element_type=jnp.float32)
    range_basis = exact(power, inverse2, ((1,), (1,))).astype(jnp.bfloat16)
    mine = lax.dynamic_slice_in_dim(z, lax.axis_index(AXIS) * local_steps, local_steps, 0)
    coefficients = (exact(mine, inverse2, ((1,), (1,))) * factor).astype(jnp.bfloat16)
    return (range_basis, coefficients)


def solution(mesh):
    in_specs = (P(("groups", "series"), None), P(("groups", "series"), None))
    out_specs = (P(("groups", "series"), None), P(("groups", "series"), None))
    return jax.shard_map(body, mesh=mesh, in_specs=in_specs, out_specs=out_specs, check_vma=False)
```

time: 506 us -> 259 us (0.51)
  waiting for transfers between devices: 288 us -> 23.8 us
  blocking collectives: 45.7 us -> 0 us
  starting transfers between devices: 0.9 us -> 29 us
  local copies, waits for them, and re-layouts: 12.8 us -> 39.5 us
  between operations: 17 us -> 4.33 us
  other arithmetic: 113 us -> 125 us
  matrix products: 24.2 us -> 33.1 us
    psum x2 -> x0, waiting for transfers between devices: 172 us -> none  [orthonormal(): gram_sum = lax.psum(partial_gram, 'series') / rows_total]
    unnamed x5 -> x0, waiting for transfers between devices: 58.1 us -> none
    reduce_scatter x1 -> x0, waiting for transfers between devices: 58 us -> none  [body(): lax.psum_scatter(summed * factor, 'series', scatter_dimension=0, tiled=True)]
    all_gather x2 -> x0, blocking collectives: 45.7 us -> none  [the longest x1 24.8 us: body(): lax.all_gather(sketch_matrix, 'series', axis=0, tiled=True)]
    ppermute x0 -> x25, starting transfers between devices: none -> 29 us  [exchange(): return lax.ppermute(value, AXIS, [(i, i ^ distance) for i in range(n)])]
    ppermute x0 -> x25, waiting for transfers between devices: none -> 23.8 us  [exchange(): return lax.ppermute(value, AXIS, [(i, i ^ distance) for i in range(n)])]
    dynamic_update_slice x0 -> x11, local copies, waits for them, and re-layouts: none -> 10.4 us  [gather_stage(): out = lax.dynamic_update_slice_in_dim(out, got[k], (me ^ k) * rows, 0)]
    concatenate x0 -> x3, other arithmetic: none -> 8.44 us  [the longest x1 5.83 us: body(): jnp.concatenate([jnp.concatenate([at(i, j) for j in range(nb)], axis=1) f...]
  transfers between devices with their start and end apart: 4 -> 25, of which waited for: 4 -> 9; matrix products, arithmetic and copies ran while one was open for 0% -> 9% of each run, Pallas kernels for 0% -> 0%
where the time goes in v1:
time: 259 us; the launch traced here: 254 us
  other arithmetic  125 us (48%)
  local copies, waits for them, and re-layouts  39.5 us (15%)
  matrix products  33.1 us (13%)
  starting transfers between devices  29 us (11%)
  waiting for transfers between devices  23.8 us (9%)
  between operations  4.33 us (2%)
    another operation x13, other arithmetic, inverse_factor(): lower_factor = jnp.linalg.cholesky(gram)  69.6 us
    another operation x5, other arithmetic, inverse_factor(): jax.scipy.linalg.solve_triangular(lower_factor, identity_k, lower=True)  41.9 us
    ppermute x25, starting transfers between devices, exchange(): return lax.ppermute(value, AXIS, [(i, i ^ distance) for i in range(n)])  29 us
    ppermute x25, waiting for transfers between devices, exchange(): return lax.ppermute(value, AXIS, [(i, i ^ distance) for i in range(n)])  23.8 us
    dot_general x7, matrix products, exact(): lax.dot_general(a.astype(jnp.float32), b.astype(jnp.float32), ((contract[...  14.8 us
    dynamic_update_slice x11, local copies, waits for them, and re-layouts, gather_stage(): out = lax.dynamic_update_slice_in_dim(out, got[k], (me ^ k) * rows, 0)  10.4 us
    another operation x15, local copies, waits for them, and re-layouts, inverse_factor(): jax.scipy.linalg.solve_triangular(lower_factor, identity_k, lower=True)  9.76 us
    dot_general x4, matrix products, body(): lax.dot_general(series_data[:, i * EDGE:(i + 1) * EDGE], series_data[:, :...  9.71 us
  transfers between devices with their start and end apart: 25, of which 9 were waited for; matrix products, arithmetic and copies ran while one was open for 9% of the time, Pallas kernels for 0%

profile of v1, /device:TPU:0, one launch (start us, length us, event | category | flops | bytes accessed | tf_op | source)
XLA Modules:
  0.0 254.3 jit_solution(12275798698400324003)
XLA Ops:
  0.6 2.8 %fusion.2 = f32[256,512]{1,0:T(8,128)S(1)} fusion(bf16[2048,1024]{1,0:T(8,128)(2,1)} %param.5), kind=kOutput, calls=%fused_computation.8 | convolution fusion | flops 536870912 | bytes 3670016 | tf_op jit(solution)/shard_map/dot_general | solution.py:91
  3.4 2.1 convolution_dynamic-update-slice_fusion
  9.9 3.8 %fusion.6 = f32[256,1024]{1,0:T(8,128)S(1)} fusion(bf16[2048,1024]{1,0:T(8,128)(2,1)} %param.5), kind=kOutput, calls=%fused_computation.25 | convolution fusion | flops 1073741824 | bytes 6291456 | tf_op jit(solution)/shard_map/dot_general | solution.py:91
  17.3 2.8 %collective-permute-start.21 = (bf16[128,256]{1,0:T(8,128)(2,1)}, bf16[128,256]{1,0:T(8,128)(2,1)}, u32[]{:S(2)}, u32[]{:S(2)}) collective-permute-start(bf16[128,256]{1,0:T(8,128)(2,1)} %maximum_select_fusion.4), channel_id=1, source_target_pairs={{0,2},{1,3},{2,0},{3,1},{4,6},{5,7},{6,4},{7,5},{8,10},{9,11},{10,... | collective-permute-start | bytes 196616 | tf_op jit(solution)/shard_map/ppermute | solution.py:15
  21.5 2.1 collective-permute-start.11
  23.6 7.3 %collective-permute-done.1 = f32[320,256]{1,0:T(8,128)S(1)} collective-permute-done((f32[320,256]{1,0:T(8,128)S(1)}, f32[320,256]{1,0:T(8,128)S(1)}, u32[]{:S(2)}, u32[]{:S(2)}) %collective-permute-start.1) | collective-permute-done | bytes 327712 | tf_op jit(solution)/shard_map/ppermute | solution.py:15
  30.9 1.6 collective-permute-start.2
  32.6 2.6 %collective-permute-start.3 = (f32[80,256]{1,0:T(8,128)S(1)}, f32[80,256]{1,0:T(8,128)S(1)}, u32[]{:S(2)}, u32[]{:S(2)}) collective-permute-start(f32[80,256]{1,0:T(8,128)S(1)} %get-tuple-element.62), channel_id=1, source_target_pairs={{0,8},{1,9},{2,10},{3,11},{4,12},{5,13},{6,14},{7,15},{8,0},{9,1},... | collective-permute-start | bytes 245768 | tf_op jit(solution)/shard_map/ppermute | solution.py:15
  35.4 1.4 collective-permute-done.11
  36.8 2.9 %collective-permute-done.3 = f32[80,256]{1,0:T(8,128)S(1)} collective-permute-done((f32[80,256]{1,0:T(8,128)S(1)}, f32[80,256]{1,0:T(8,128)S(1)}, u32[]{:S(2)}, u32[]{:S(2)}) %collective-permute-start.3) | collective-permute-done | bytes 81952 | tf_op jit(solution)/shard_map/ppermute | solution.py:15
  39.7 2.0 collective-permute-done.4
  41.8 1.8 collective-permute-start.6
  43.6 2.6 %collective-permute-start.7 = (f32[80,256]{1,0:T(8,128)S(1)}, f32[80,256]{1,0:T(8,128)S(1)}, u32[]{:S(2)}, u32[]{:S(2)}) collective-permute-start(f32[80,256]{1,0:T(8,128)S(1)} %add_add_fusion.1), channel_id=1, source_target_pairs={{0,12},{1,13},{2,14},{3,15},{4,8},{5,9},{6,10},{7,11},{8,4},{9,5},... | collective-permute-start | bytes 245768 | tf_op jit(solution)/shard_map/ppermute | solution.py:15
  48.4 1.4 collective-permute-start.13
  51.2 2.7 %collective-permute-start.14 = (f32[80,256]{1,0:T(8,128)S(1)}, f32[80,256]{1,0:T(8,128)S(1)}, u32[]{:S(2)}, u32[]{:S(2)}) collective-permute-start(f32[80,256]{1,0:T(8,128)S(1)} %get-tuple-element.64), channel_id=1, source_target_pairs={{0,12},{1,13},{2,14},{3,15},{4,8},{5,9},{6,10},{7,11},{8,4},{9,5},... | collective-permute-start | bytes 245768 | tf_op jit(solution)/shard_map/ppermute | solution.py:15
  56.8 1.4 collective-permute-start.8
  58.2 1.6 constant_dynamic-update-slice_fusion.5
  59.9 2.1 collective-permute-start.15
  62.4 2.1 collective-permute-start.17
  72.6 2.0 collective-permute-start.24
  74.6 1.7 collective-permute-done.23
  76.3 6.3 %collective-permute-done.18 = f32[320,256]{0,1:T(8,128)S(1)} collective-permute-done((f32[320,256]{0,1:T(8,128)S(1)}, f32[320,256]{0,1:T(8,128)S(1)}, u32[]{:S(2)}, u32[]{:S(2)}) %collective-permute-start.18) | collective-permute-done | bytes 327712 | tf_op jit(solution)/shard_map/ppermute | solution.py:15
  85.2 2.5 %pad_maximum_fusion.1 = (f32[1280,256]{0,1:T(8,128)}, f32[1280,256]{0,1:T(8,128)S(1)}) fusion(f32[640,256]{0,1:T(8,128)S(1)} %maximum_select_fusion.2, f32[640,256]{0,1:T(8,128)} %collective-permute-done.19), kind=kLoop, calls=%fused_computation.13 | loop fusion | flops 655360 | bytes 3932160 | tf_op jit(solution)/shard_map/concatenate | solution.py:36
  88.2 1.7 copy.15
  92.0 1.9 copy.18
  93.8 1.8 copy.28
  96.5 1.8 copy.19
  98.3 5.8 %maximum_maximum_fusion = f32[1024,1024]{1,0:T(8,128)S(1)} fusion(f32[256,256]{1,0:T(8,128)S(1)} %copy-done.5, f32[256,256]{1,0:T(8,128)S(1)} %copy-done.6, f32[256,256]{1,0:T(8,128)} %get-tuple-element.54, f32[256,256]{1,0:T(8,128)S(1)} %get-tuple-element.55, f32[256,256]{1,0:T(8,128)} %copy.19, f32[256,256]{1,0:T(8,128)} %get-tuple-element.53, ...), kind=kLoop, calls=%fused_computation.4 | loop fusion | flops 12582912 | bytes 8388608 | tf_op jit(solution)/shard_map/concatenate | solution.py:104
  104.1 2.0 fusion.39
  107.4 11.7 %cholesky.130 = f32[128,128]{1,0:T(8,128)S(1)} custom-call(f32[128,128]{1,0:T(8,128)S(1)} %cholesky.194), custom_call_target="Cholesky" | custom-call | tf_op jit(solution)/shard_map/jit(cholesky)/cholesky | solution.py:74
  119.2 9.8 %custom-call.13 = f32[1,128,128]{1,2,0:T(8,128)S(1)} custom-call(f32[1,128,128]{2,1,0:T(8,128)S(1)} %get-tuple-element.73), custom_call_target="InvertDiagBlocksLowerTriangular" | custom-call | tf_op jit(solution)/shard_map/jit(cholesky)/cholesky | solution.py:74
  129.4 11.9 %cholesky.147 = f32[128,128]{1,0:T(8,128)S(1)} custom-call(f32[128,128]{1,0:T(8,128)S(1)} %convolution_subtract_fusion.3), custom_call_target="Cholesky" | custom-call | tf_op jit(solution)/shard_map/jit(cholesky)/cholesky | solution.py:74
  143.4 4.0 %while.4 = (s32[]{:T(128)}, f32[256,256]{1,0:T(8,128)S(1)}, s32[2,2]{1,0:T(2,128)S(1)}, f32[2,128,128]{2,1,0:T(8,128)S(1)}, s32[]{:T(128)}) while((s32[]{:T(128)}, f32[256,256]{1,0:T(8,128)S(1)}, s32[2,2]{1,0:T(2,128)S(1)}, f32[2,128,128]{2,1,0:T(8,128)S(1)}, s32[]{:T(128)}) %tuple.66), condition=%wide.while_cond, body=%wide.while_body.sunk | while | flops 2 | bytes 131181 | solution.py:76
  144.1 1.4 bitcast_dynamic-update-slice_fusion.4
  146.0 1.4 bitcast_dynamic-update-slice_fusion.4
  147.4 19.7 %custom-call.14 = f32[2,128,128]{1,2,0:T(8,128)S(1)} custom-call(f32[2,128,128]{2,1,0:T(8,128)S(1)} %get-tuple-element.18), custom_call_target="InvertDiagBlocksLowerTriangular" | custom-call | tf_op jit(solution)/shard_map/jit(_solve_triangular)/triangular_solve | solution.py:76
  169.1 4.4 %fusion.41 = f32[1024,256]{1,0:T(8,128)S(1)} fusion(f32[1024,1024]{1,0:T(8,128)} %copy-done, bf16[1024,256]{1,0:T(8,128)(2,1)S(1)} %fusion.4), kind=kOutput, calls=%fused_computation.126 | convolution fusion | flops 3221225472 | bytes 5767168 | tf_op jit(solution)/shard_map/dot_general | solution.py:64
  173.4 2.7 %fusion.40 = f32[256,2048]{1,0:T(8,128)} fusion(bf16[1024,256]{1,0:T(8,128)(2,1)S(1)} %fusion.4, bf16[2048,1024]{1,0:T(8,128)(2,1)S(1)} %copy-done.14), kind=kOutput, calls=%fused_computation.125 | convolution fusion | flops 1073741824 | bytes 6815744 | tf_op jit(solution)/shard_map/dot_general | solution.py:113
  178.0 11.7 %cholesky.164 = f32[128,128]{1,0:T(8,128)S(1)} custom-call(f32[128,128]{1,0:T(8,128)S(1)} %cholesky.197), custom_call_target="Cholesky" | custom-call | tf_op jit(solution)/shard_map/jit(cholesky)/cholesky | solution.py:74
  190.5 10.0 %custom-call.15 = f32[1,128,128]{1,2,0:T(8,128)S(1)} custom-call(f32[1,128,128]{2,1,0:T(8,128)S(1)} %get-tuple-element.69), custom_call_target="InvertDiagBlocksLowerTriangular" | custom-call | tf_op jit(solution)/shard_map/jit(cholesky)/cholesky | solution.py:74
  200.5 1.7 constant_dynamic-update-slice_fusion
  203.3 11.7 %cholesky.181 = f32[128,128]{1,0:T(8,128)S(1)} custom-call(f32[128,128]{1,0:T(8,128)S(1)} %convolution_subtract_fusion.2), custom_call_target="Cholesky" | custom-call | tf_op jit(solution)/shard_map/jit(cholesky)/cholesky | solution.py:74
  218.3 1.7 select_select_fusion
  220.0 5.8 %while.5 = (s32[]{:T(128)}, f32[256,256]{1,0:T(8,128)}, s32[2,2]{1,0:T(2,128)S(1)}, f32[2,128,128]{2,1,0:T(8,128)S(1)}, s32[]{:T(128)}) while((s32[]{:T(128)}, f32[256,256]{1,0:T(8,128)}, s32[2,2]{1,0:T(2,128)S(1)}, f32[2,128,128]{2,1,0:T(8,128)S(1)}, s32[]{:T(128)}) %tuple.72), condition=%wide.while_cond.clone, body=%wide.while_body.clone.sunk | while | flops 2 | bytes 131181 | solution.py:76
  220.6 2.3 bitcast_dynamic-update-slice_fusion.5
  223.5 2.3 bitcast_dynamic-update-slice_fusion.5
  226.5 20.5 %custom-call.16 = f32[2,128,128]{1,2,0:T(8,128)S(1)} custom-call(f32[2,128,128]{2,1,0:T(8,128)} %copy-done.11), custom_call_target="InvertDiagBlocksLowerTriangular" | custom-call | tf_op jit(solution)/shard_map/jit(_solve_triangular)/triangular_solve | solution.py:76
  249.7 4.4 %convolution_convert_fusion = bf16[2048,256]{1,0:T(8,128)(2,1)} fusion(f32[256,2048]{1,0:T(8,128)S(1)} %copy-done.2, f32[128,256]{1,0:T(8,128)S(1)} %fusion.22, f32[128,256]{1,0:T(8,128)S(1)} %fusion.17), kind=kOutput, calls=%fused_computation.7 | convolution fusion | flops 1611202560 | bytes 3407872 | tf_op jit(solution)/shard_map/dot_general | solution.py:64
  (159 shorter events, 46.4 us)
Async XLA Ops:
  0.6 4.9 %copy-start.13 = (bf16[2048,1024]{1,0:T(8,128)(2,1)S(1)}, bf16[2048,1024]{1,0:T(8,128)(2,1)}, u32[]{:S(2)}) copy-start(bf16[2048,1024]{1,0:T(8,128)(2,1)} %param.5) | copy-start | bytes 12582916
  6.6 0.9 copy-start.10
  9.5 10.6 %collective-permute-start = (f32[640,256]{1,0:T(8,128)}, f32[640,256]{1,0:T(8,128)S(1)}, u32[]{:S(2)}, u32[]{:S(2)}) collective-permute-start(f32[640,256]{1,0:T(8,128)} %constant_dynamic-slice_fusion.11), channel_id=1, source_target_pairs={{0,1},{1,0},{2,3},{3,2},{4,5},{5,4},{6,7},{7,6},{8,9},{9,8},{10,11... | collective-permute-start | bytes 1966088 | tf_op jit(solution)/shard_map/ppermute | solution.py:15
  13.8 1.1 copy-start.12
  14.8 5.5 %collective-permute-start.10 = (f32[640,256]{1,0:T(8,128)}, f32[640,256]{1,0:T(8,128)}, u32[]{:S(2)}, u32[]{:S(2)}) collective-permute-start(f32[640,256]{1,0:T(8,128)} %constant_dynamic-slice_fusion.6), channel_id=1, source_target_pairs={{0,1},{1,0},{2,3},{3,2},{4,5},{5,4},{6,7},{7,6},{8,9},{9,8},{10,11... | collective-permute-start | bytes 1966088 | tf_op jit(solution)/shard_map/ppermute | solution.py:15
  14.8 1.8 collective-permute-start.20
  17.3 40.9 %collective-permute-start.21 = (bf16[128,256]{1,0:T(8,128)(2,1)}, bf16[128,256]{1,0:T(8,128)(2,1)}, u32[]{:S(2)}, u32[]{:S(2)}) collective-permute-start(bf16[128,256]{1,0:T(8,128)(2,1)} %maximum_select_fusion.4), channel_id=1, source_target_pairs={{0,2},{1,3},{2,0},{3,1},{4,6},{5,7},{6,4},{7,5},{8,10},{9,11},{10,... | collective-permute-start | bytes 196616 | tf_op jit(solution)/shard_map/ppermute | solution.py:15
  20.2 10.7 %collective-permute-start.1 = (f32[320,256]{1,0:T(8,128)S(1)}, f32[320,256]{1,0:T(8,128)S(1)}, u32[]{:S(2)}, u32[]{:S(2)}) collective-permute-start(f32[320,256]{1,0:T(8,128)S(1)} %constant_dynamic-slice_fusion.10), channel_id=1, source_target_pairs={{0,2},{1,3},{2,0},{3,1},{4,6},{5,7},{6,4},{7,5},{8,10},{9,11},{10,... | collective-permute-start | bytes 983048 | tf_op jit(solution)/shard_map/ppermute | solution.py:15
  21.5 15.2 %collective-permute-start.11 = (f32[320,256]{1,0:T(8,128)S(1)}, f32[320,256]{1,0:T(8,128)S(1)}, u32[]{:S(2)}, u32[]{:S(2)}) collective-permute-start(f32[320,256]{1,0:T(8,128)S(1)} %constant_dynamic-slice_fusion.5), channel_id=1, source_target_pairs={{0,2},{1,3},{2,0},{3,1},{4,6},{5,7},{6,4},{7,5},{8,10},{9,11},{10,... | collective-permute-start | bytes 983048 | tf_op jit(solution)/shard_map/ppermute | solution.py:15
  30.9 5.9 %collective-permute-start.2 = (f32[80,256]{1,0:T(8,128)S(1)}, f32[80,256]{1,0:T(8,128)S(1)}, u32[]{:S(2)}, u32[]{:S(2)}) collective-permute-start(f32[80,256]{1,0:T(8,128)S(1)} %get-tuple-element.60), channel_id=1, source_target_pairs={{0,4},{1,5},{2,6},{3,7},{4,0},{5,1},{6,2},{7,3},{8,12},{9,13},{10,... | collective-permute-start | bytes 245768 | tf_op jit(solution)/shard_map/ppermute | solution.py:15
  32.6 7.1 %collective-permute-start.3 = (f32[80,256]{1,0:T(8,128)S(1)}, f32[80,256]{1,0:T(8,128)S(1)}, u32[]{:S(2)}, u32[]{:S(2)}) collective-permute-start(f32[80,256]{1,0:T(8,128)S(1)} %get-tuple-element.62), channel_id=1, source_target_pairs={{0,8},{1,9},{2,10},{3,11},{4,12},{5,13},{6,14},{7,15},{8,0},{9,1},... | collective-permute-start | bytes 245768 | tf_op jit(solution)/shard_map/ppermute | solution.py:15
  35.2 6.5 %collective-permute-start.4 = (f32[80,256]{1,0:T(8,128)S(1)}, f32[80,256]{1,0:T(8,128)S(1)}, u32[]{:S(2)}, u32[]{:S(2)}) collective-permute-start(f32[80,256]{1,0:T(8,128)S(1)} %get-tuple-element.61), channel_id=1, source_target_pairs={{0,12},{1,13},{2,14},{3,15},{4,8},{5,9},{6,10},{7,11},{8,4},{9,5},... | collective-permute-start | bytes 245768 | tf_op jit(solution)/shard_map/ppermute | solution.py:15
  41.7 6.7 %collective-permute-start.5 = (f32[80,256]{1,0:T(8,128)S(1)}, f32[80,256]{1,0:T(8,128)S(1)}, u32[]{:S(2)}, u32[]{:S(2)}) collective-permute-start(f32[80,256]{1,0:T(8,128)S(1)} %add_add_fusion.1), channel_id=1, source_target_pairs={{0,4},{1,5},{2,6},{3,7},{4,0},{5,1},{6,2},{7,3},{8,12},{9,13},{10,... | collective-permute-start | bytes 245768 | tf_op jit(solution)/shard_map/ppermute | solution.py:15
  41.8 9.4 %collective-permute-start.6 = (f32[80,256]{1,0:T(8,128)S(1)}, f32[80,256]{1,0:T(8,128)S(1)}, u32[]{:S(2)}, u32[]{:S(2)}) collective-permute-start(f32[80,256]{1,0:T(8,128)S(1)} %add_add_fusion.1), channel_id=1, source_target_pairs={{0,8},{1,9},{2,10},{3,11},{4,12},{5,13},{6,14},{7,15},{8,0},{9,1},... | collective-permute-start | bytes 245768 | tf_op jit(solution)/shard_map/ppermute | solution.py:15
  43.6 11.7 %collective-permute-start.7 = (f32[80,256]{1,0:T(8,128)S(1)}, f32[80,256]{1,0:T(8,128)S(1)}, u32[]{:S(2)}, u32[]{:S(2)}) collective-permute-start(f32[80,256]{1,0:T(8,128)S(1)} %add_add_fusion.1), channel_id=1, source_target_pairs={{0,12},{1,13},{2,14},{3,15},{4,8},{5,9},{6,10},{7,11},{8,4},{9,5},... | collective-permute-start | bytes 245768 | tf_op jit(solution)/shard_map/ppermute | solution.py:15
  46.2 13.7 %collective-permute-start.12 = (f32[80,256]{1,0:T(8,128)S(1)}, f32[80,256]{1,0:T(8,128)S(1)}, u32[]{:S(2)}, u32[]{:S(2)}) collective-permute-start(f32[80,256]{1,0:T(8,128)S(1)} %get-tuple-element.63), channel_id=1, source_target_pairs={{0,4},{1,5},{2,6},{3,7},{4,0},{5,1},{6,2},{7,3},{8,12},{9,13},{10,... | collective-permute-start | bytes 245768 | tf_op jit(solution)/shard_map/ppermute | solution.py:15
  48.4 11.5 %collective-permute-start.13 = (f32[80,256]{1,0:T(8,128)S(1)}, f32[80,256]{1,0:T(8,128)S(1)}, u32[]{:S(2)}, u32[]{:S(2)}) collective-permute-start(f32[80,256]{1,0:T(8,128)S(1)} %get-tuple-element.65), channel_id=1, source_target_pairs={{0,8},{1,9},{2,10},{3,11},{4,12},{5,13},{6,14},{7,15},{8,0},{9,1},... | collective-permute-start | bytes 245768 | tf_op jit(solution)/shard_map/ppermute | solution.py:15
  51.2 8.7 %collective-permute-start.14 = (f32[80,256]{1,0:T(8,128)S(1)}, f32[80,256]{1,0:T(8,128)S(1)}, u32[]{:S(2)}, u32[]{:S(2)}) collective-permute-start(f32[80,256]{1,0:T(8,128)S(1)} %get-tuple-element.64), channel_id=1, source_target_pairs={{0,12},{1,13},{2,14},{3,15},{4,8},{5,9},{6,10},{7,11},{8,4},{9,5},... | collective-permute-start | bytes 245768 | tf_op jit(solution)/shard_map/ppermute | solution.py:15
  56.8 7.8 %collective-permute-start.8 = (f32[320,256]{0,1:T(8,128)S(1)}, f32[320,256]{0,1:T(8,128)S(1)}, u32[]{:S(2)}, u32[]{:S(2)}) collective-permute-start(f32[320,256]{0,1:T(8,128)S(1)} %dynamic_update_slice.39), channel_id=1, source_target_pairs={{0,2},{1,3},{2,0},{3,1},{4,6},{5,7},{6,4},{7,5},{8,10},{9,11},{10,... | collective-permute-start | bytes 983048 | tf_op jit(solution)/shard_map/ppermute | solution.py:15
  59.9 14.7 %collective-permute-start.22 = (bf16[256,256]{1,0:T(8,128)(2,1)}, bf16[256,256]{1,0:T(8,128)(2,1)S(1)}, u32[]{:S(2)}, u32[]{:S(2)}) collective-permute-start(bf16[256,256]{1,0:T(8,128)(2,1)} %get-tuple-element.37), channel_id=1, source_target_pairs={{0,4},{1,5},{2,6},{3,7},{4,0},{5,1},{6,2},{7,3},{8,12},{9,13},{10,... | collective-permute-start | bytes 393224 | tf_op jit(solution)/shard_map/ppermute | solution.py:15
  59.9 6.3 %collective-permute-start.15 = (f32[80,256]{1,0:T(8,128)S(1)}, f32[80,256]{1,0:T(8,128)S(1)}, u32[]{:S(2)}, u32[]{:S(2)}) collective-permute-start(f32[80,256]{1,0:T(8,128)S(1)} %add_add_fusion), channel_id=1, source_target_pairs={{0,4},{1,5},{2,6},{3,7},{4,0},{5,1},{6,2},{7,3},{8,12},{9,13},{10,... | collective-permute-start | bytes 245768 | tf_op jit(solution)/shard_map/ppermute | solution.py:15
  62.0 6.4 %collective-permute-start.16 = (f32[80,256]{1,0:T(8,128)S(1)}, f32[80,256]{1,0:T(8,128)S(1)}, u32[]{:S(2)}, u32[]{:S(2)}) collective-permute-start(f32[80,256]{1,0:T(8,128)S(1)} %add_add_fusion), channel_id=1, source_target_pairs={{0,8},{1,9},{2,10},{3,11},{4,12},{5,13},{6,14},{7,15},{8,0},{9,1},... | collective-permute-start | bytes 245768 | tf_op jit(solution)/shard_map/ppermute | solution.py:15
  62.4 7.5 %collective-permute-start.17 = (f32[80,256]{1,0:T(8,128)S(1)}, f32[80,256]{1,0:T(8,128)S(1)}, u32[]{:S(2)}, u32[]{:S(2)}) collective-permute-start(f32[80,256]{1,0:T(8,128)S(1)} %add_add_fusion), channel_id=1, source_target_pairs={{0,12},{1,13},{2,14},{3,15},{4,8},{5,9},{6,10},{7,11},{8,4},{9,5},... | collective-permute-start | bytes 245768 | tf_op jit(solution)/shard_map/ppermute | solution.py:15
  64.9 18.1 %collective-permute-start.9 = (f32[640,256]{0,1:T(8,128)S(1)}, f32[640,256]{0,1:T(8,128)S(1)}, u32[]{:S(2)}, u32[]{:S(2)}) collective-permute-start(f32[640,256]{0,1:T(8,128)S(1)} %maximum_select_fusion.1), channel_id=1, source_target_pairs={{0,1},{1,0},{2,3},{3,2},{4,5},{5,4},{6,7},{7,6},{8,9},{9,8},{10,11... | collective-permute-start | bytes 1966088 | tf_op jit(solution)/shard_map/ppermute | solution.py:15
  66.2 10.1 %collective-permute-start.23 = (bf16[256,256]{1,0:T(8,128)(2,1)}, bf16[256,256]{1,0:T(8,128)(2,1)S(1)}, u32[]{:S(2)}, u32[]{:S(2)}) collective-permute-start(bf16[256,256]{1,0:T(8,128)(2,1)} %get-tuple-element.37), channel_id=1, source_target_pairs={{0,8},{1,9},{2,10},{3,11},{4,12},{5,13},{6,14},{7,15},{8,0},{9,1},... | collective-permute-start | bytes 393224 | tf_op jit(solution)/shard_map/ppermute | solution.py:15
  71.3 11.3 %collective-permute-start.18 = (f32[320,256]{0,1:T(8,128)S(1)}, f32[320,256]{0,1:T(8,128)S(1)}, u32[]{:S(2)}, u32[]{:S(2)}) collective-permute-start(f32[320,256]{0,1:T(8,128)S(1)} %dynamic_update_slice.43), channel_id=1, source_target_pairs={{0,2},{1,3},{2,0},{3,1},{4,6},{5,7},{6,4},{7,5},{8,10},{9,11},{10,... | collective-permute-start | bytes 983048 | tf_op jit(solution)/shard_map/ppermute | solution.py:15
  72.6 10.3 %collective-permute-start.24 = (bf16[256,256]{1,0:T(8,128)(2,1)}, bf16[256,256]{1,0:T(8,128)(2,1)S(1)}, u32[]{:S(2)}, u32[]{:S(2)}) collective-permute-start(bf16[256,256]{1,0:T(8,128)(2,1)} %get-tuple-element.37), channel_id=1, source_target_pairs={{0,12},{1,13},{2,14},{3,15},{4,8},{5,9},{6,10},{7,11},{8,4},{9,5},... | collective-permute-start | bytes 393224 | tf_op jit(solution)/shard_map/ppermute | solution.py:15
  82.9 2.3 collective-permute-start.19
  90.1 1.1 copy-start.1
  90.1 1.2 copy-start.7
  90.1 1.4 copy-start.8
  91.9 6.3 %copy-start.3 = (f32[256,256]{1,0:T(8,128)S(1)}, f32[256,256]{1,0:T(8,128)}, u32[]{:S(2)}) copy-start(f32[256,256]{1,0:T(8,128)} %get-tuple-element.43) | copy-start | bytes 786436
  91.9 6.3 %copy-start.4 = (f32[256,256]{1,0:T(8,128)S(1)}, f32[256,256]{1,0:T(8,128)}, u32[]{:S(2)}) copy-start(f32[256,256]{1,0:T(8,128)} %get-tuple-element.44) | copy-start | bytes 786436
  92.0 6.3 %copy-start.5 = (f32[256,256]{1,0:T(8,128)S(1)}, f32[256,256]{1,0:T(8,128)}, u32[]{:S(2)}) copy-start(f32[256,256]{1,0:T(8,128)} %get-tuple-element.51) | copy-start | bytes 786436
  92.0 6.3 %copy-start.6 = (f32[256,256]{1,0:T(8,128)S(1)}, f32[256,256]{1,0:T(8,128)}, u32[]{:S(2)}) copy-start(f32[256,256]{1,0:T(8,128)} %get-tuple-element.52) | copy-start | bytes 786436
  104.1 2.1 copy-start
  169.0 4.4 %copy-start.14 = (bf16[2048,1024]{1,0:T(8,128)(2,1)S(1)}, bf16[2048,1024]{1,0:T(8,128)(2,1)}, u32[]{:S(2)}) copy-start(bf16[2048,1024]{1,0:T(8,128)(2,1)} %param.5) | copy-start | bytes 12582916
  177.3 0.7 copy-start.9
  178.0 71.7 %copy-start.2 = (f32[256,2048]{1,0:T(8,128)S(1)}, f32[256,2048]{1,0:T(8,128)}, u32[]{:S(2)}) copy-start(f32[256,2048]{1,0:T(8,128)} %fusion.40) | copy-start | bytes 6291460
  225.8 0.7 copy-start.11

commit v2 on v1

v2 whole, which is shorter than its diff:
```python
import functools
import math

import jax
import jax.numpy as jnp
from jax import lax
from jax.experimental import pallas as pl
from jax.experimental.pallas import tpu as pltpu
from jax.sharding import PartitionSpec as P

AXIS = "series"
EDGE = 256
HALF = 128
PIVOTS = 32
CHAINS = 2
F32 = jnp.float32
BF16 = jnp.bfloat16


def exchange(value, distance):
    n = lax.axis_size(AXIS)
    return lax.ppermute(value, AXIS, [(i, i ^ distance) for i in range(n)])


def piece(value, index, count):
    rows = value.shape[0] // count
    return lax.dynamic_slice_in_dim(value, index * rows, rows, 0)


def scatter_stage(value, low, count):
    me = (lax.axis_index(AXIS) >> low) & (count - 1)
    got = [exchange(piece(value, me ^ k, count), k << low) for k in range(1, count)]
    total = piece(value, me, count)
    for item in got:
        total = total + item
    return total


def gather_stage(value, low, count):
    me = (lax.axis_index(AXIS) >> low) & (count - 1)
    got = [value] + [exchange(value, k << low) for k in range(1, count)]
    if count == 2:
        return jnp.where(me == 0, jnp.concatenate(got), jnp.concatenate(got[::-1]))
    rows = value.shape[0]
    out = jnp.zeros((count * rows,) + value.shape[1:], value.dtype)
    for k in range(count):
        out = lax.dynamic_update_slice_in_dim(out, got[k], (me ^ k) * rows, 0)
    return out


def stages():
    n = lax.axis_size(AXIS)
    return [(0, 2), (1, 2), (2, n // 4)]


def sum_everywhere(value):
    for low, count in stages():
        value = scatter_stage(value, low, count)
    for low, count in reversed(stages()):
        value = gather_stage(value, low, count)
    return value


def gather_rows(value):
    for low, count in stages():
        value = gather_stage(value, low, count)
    return value


def layout(time_steps):
    nb = time_steps // EDGE
    off = [(i, j) for i in range(nb) for j in range(i)]
    chains = [[] for _ in range(CHAINS)]
    for k, ij in enumerate(off):
        chains[k * CHAINS // len(off)].append(ij)
    for i in range(nb):
        chains[i * CHAINS // nb].append((i, i))
    return chains


def chain_rows(chain):
    return sum(EDGE if i != j else EDGE * 3 // 4 for i, j in chain)


def three(value):
    high = value.astype(BF16)
    rest = value - high.astype(F32)
    mid = rest.astype(BF16)
    low = (rest - mid.astype(F32)).astype(BF16)
    return high, mid, low


def product(a, b, contract=((1,), (0,)), precision=None):
    return lax.dot_general(
        a, b, (contract, ((), ())), precision=precision, preferred_element_type=F32
    )


def moment_kernel(chains, a_ref, *out_refs):
    for chain, out in zip(chains, out_refs):
        row = 0
        for i, j in chain:
            left = a_ref[:, i * EDGE : (i + 1) * EDGE]
            block = product(left, a_ref[:, j * EDGE : (j + 1) * EDGE], ((0,), (0,)))
            if i != j:
                out[row : row + EDGE, :] = block
                row += EDGE
            else:
                out[row : row + HALF, :HALF] = block[:HALF, :HALF]
                out[row : row + HALF, HALF:] = block[HALF:, HALF:]
                out[row + HALF : row + HALF + HALF // 2, :HALF] = block[HALF : HALF + HALF // 2, :HALF]
                out[row + HALF : row + HALF + HALF // 2, HALF:] = block[HALF + HALF // 2 :, :HALF]
                row += EDGE * 3 // 4


def unpack(chains, refs, store):
    for chain, ref in zip(chains, refs):
        row = 0
        for i, j in chain:
            if i != j:
                block = ref[row : row + EDGE, :]
                row += EDGE
                store(i, j, block)
                store(j, i, block.T)
            else:
                first = ref[row : row + HALF, :HALF]
                last = ref[row : row + HALF, HALF:]
                tail = ref[row + HALF : row + HALF + HALF // 2, :]
                cross = jnp.concatenate([tail[:, :HALF], tail[:, HALF:]], axis=0)
                row += EDGE * 3 // 4
                store(
                    i,
                    i,
                    jnp.concatenate(
                        [
                            jnp.concatenate([first, cross.T], axis=1),
                            jnp.concatenate([cross, last], axis=1),
                        ],
                        axis=0,
                    ),
                )


def inverse_factor(x_ref, w_ref, beside=None):
    n = x_ref.shape[0]
    groups = PIVOTS // 8
    tiles = n // 128
    lane = lax.broadcasted_iota(jnp.int32, (8, 128), 1)
    sub = lax.broadcasted_iota(jnp.int32, (8, 128), 0)
    for k in range(n // PIVOTS):
        o = PIVOTS * k
        home, lo = o // 128, o % 128
        panel = [
            [x_ref[o + 8 * g : o + 8 * g + 8, 128 * t : 128 * t + 128] for t in range(tiles)]
            for g in range(groups)
        ]
        col = {
            (i, g): jnp.broadcast_to(panel[g][home][:, lo + i : lo + i + 1], (8, 128))
            for i in range(PIVOTS)
            for g in range(i // 8, groups)
        }
        in_block = (lane >= lo) & (lane < lo + PIVOTS)
        for g in range(groups):
            unit = jnp.where(lane - lo == sub + 8 * g, 1.0, 0.0)
            panel[g][home] = jnp.where(in_block, unit, panel[g][home])
        if beside is not None:
            beside(k)
        for j in range(PIVOTS):
            gj, s = j // 8, j % 8
            scale = lax.rsqrt(jnp.broadcast_to(col[j, gj][s : s + 1, :], (8, 128)))
            low = {g: col[j, g] * scale for g in range(gj, groups)}
            for i in range(j + 1, PIVOTS):
                other = jnp.broadcast_to(low[i // 8][i % 8 : i % 8 + 1, :], (8, 128))
                for g in range(i // 8, groups):
                    col[i, g] = col[i, g] - low[g] * other
            low[gj] = jnp.where(sub > s, low[gj], 0.0)
            for t in range(tiles):
                row = jnp.broadcast_to(panel[gj][t][s : s + 1, :], (8, 128)) * scale
                for g in range(gj, groups):
                    left = panel[g][t] - low[g] * row
                    panel[g][t] = jnp.where(sub == s, row, left) if g == gj else left
        for g in range(groups):
            for t in range(tiles):
                part = panel[g][t]
                if t > home:
                    part = jnp.zeros_like(part)
                elif t == home:
                    part = jnp.where(lane < lo + PIVOTS, part, 0.0)
                w_ref[o + 8 * g : o + 8 * g + 8, 128 * t : 128 * t + 128] = part
        nxt = o + PIVOTS
        if nxt < n:
            rows = jnp.concatenate([jnp.concatenate(p, axis=1) for p in panel], axis=0)
            first = nxt // 128 * 128
            a, b, c = three(rows)
            left = jnp.concatenate([a, a, a, b, b, c], axis=0)[:, first:]
            right = jnp.concatenate([a, b, c, a, b, a], axis=0)
            update = product(left, right, ((0,), (0,)))
            old = x_ref[nxt:, :]
            column = lax.broadcasted_iota(jnp.int32, old.shape, 1)
            old = jnp.where((column >= o) & (column < nxt), 0.0, old)
            x_ref[nxt:, :] = old - update[nxt - first :, :]


def finish_kernel(
    chains, rows_total, factor, me_ref, sketch_ref, a_hbm, *refs
):
    chain_refs, refs = refs[: len(chains)], refs[len(chains) :]
    range_ref, coef_ref, moment, a_ref, power, y_ref, back_ref, x_ref, w_ref, sem = refs
    time_steps, rank = sketch_ref.shape
    nb = time_steps // EDGE
    fetch = pltpu.make_async_copy(a_hbm, a_ref, sem)
    fetch.start()

    def store(i, j, block):
        for p, part in enumerate(three(block)):
            moment[p, i * EDGE : (i + 1) * EDGE, j * EDGE : (j + 1) * EDGE] = part

    unpack(chains, chain_refs, store)

    def apply_moment(right_ref):
        for i in range(nb):
            band = slice(i * EDGE, (i + 1) * EDGE)
            total = product(moment[0, band, :], right_ref[...])
            total = total + product(moment[1, band, :], right_ref[...])
            y_ref[band, :] = total + product(moment[2, band, :], right_ref[...])

    def gram(left_ref):
        wide = product(left_ref[...], jnp.concatenate(three(y_ref[...]), axis=1), ((0,), (0,)))
        x_ref[...] = (wide[:, :rank] + wide[:, rank : 2 * rank] + wide[:, 2 * rank :]) / rows_total

    high = lax.Precision.HIGHEST
    apply_moment(sketch_ref)
    gram(sketch_ref)
    inverse_factor(x_ref, w_ref)
    for i in range(nb):
        band = slice(i * EDGE, (i + 1) * EDGE)
        back_ref[band, :] = (
            product(y_ref[band, :], w_ref[...], ((1,), (1,)), high) * factor
        ).astype(BF16)
    apply_moment(back_ref)
    gram(back_ref)
    fetch.wait()
    panels = rank // PIVOTS
    share = a_ref.shape[0] // panels

    def some_power(k):
        band = slice(k * share, (k + 1) * share)
        power[band, :] = product(a_ref[band, :], back_ref[...])

    inverse_factor(x_ref, w_ref, some_power)
    for k in range(panels):
        band = slice(k * share, (k + 1) * share)
        range_ref[band, :] = product(power[band, :], w_ref[...], ((1,), (1,)), high).astype(BF16)
    steps = coef_ref.shape[0]
    mine = y_ref[pl.ds(pl.multiple_of(me_ref[0] * steps, steps), steps), :]
    coef_ref[...] = (product(mine, w_ref[...], ((1,), (1,)), high) * factor).astype(BF16)


def body(series_data, sketch_matrix):
    devices_here = lax.axis_size(AXIS)
    local_rows = series_data.shape[0]
    rows_total = local_rows * devices_here
    local_steps, rank = sketch_matrix.shape
    time_steps = local_steps * devices_here
    factor = math.sqrt(time_steps) / rows_total
    chains = layout(time_steps)
    vmem = pl.BlockSpec(memory_space=pltpu.VMEM)

    sketch_all = gather_rows(sketch_matrix)
    partial = pl.pallas_call(
        functools.partial(moment_kernel, chains),
        out_shape=[jax.ShapeDtypeStruct((chain_rows(c), EDGE), F32) for c in chains],
        in_specs=[vmem],
        out_specs=[vmem] * len(chains),
        compiler_params=pltpu.CompilerParams(vmem_limit_bytes=20 << 20),
    )(series_data)
    summed = [sum_everywhere(p) for p in partial]
    me = lax.axis_index(AXIS).astype(jnp.int32).reshape(1)
    return tuple(
        pl.pallas_call(
            functools.partial(finish_kernel, chains, rows_total, factor),
            out_shape=[
                jax.ShapeDtypeStruct((local_rows, rank), BF16),
                jax.ShapeDtypeStruct((local_steps, rank), BF16),
            ],
            in_specs=[
                pl.BlockSpec(memory_space=pltpu.SMEM),
                vmem,
                pl.BlockSpec(memory_space=pl.ANY),
            ]
            + [vmem] * len(chains),
            out_specs=[vmem, vmem],
            scratch_shapes=[
                pltpu.VMEM((3, time_steps, time_steps), BF16),
                pltpu.VMEM(series_data.shape, BF16),
                pltpu.VMEM((local_rows, rank), F32),
                pltpu.VMEM((time_steps, rank), F32),
                pltpu.VMEM((time_steps, rank), BF16),
                pltpu.VMEM((rank, rank), F32),
                pltpu.VMEM((rank, rank), F32),
                pltpu.SemaphoreType.DMA,
            ],
            compiler_params=pltpu.CompilerParams(vmem_limit_bytes=40 << 20),
        )(me, sketch_all, series_data, *summed)
    )


def solution(mesh):
    in_specs = (P(("groups", "series"), None), P(("groups", "series"), None))
    out_specs = (P(("groups", "series"), None), P(("groups", "series"), None))
    return jax.shard_map(body, mesh=mesh, in_specs=in_specs, out_specs=out_specs, check_vma=False)
```

time: 259 us -> 96.9 us (0.37); the launches traced: 254 us -> 96.5 us
  other arithmetic: 125 us -> 3.6 us
  local copies, waits for them, and re-layouts: 39.5 us -> 4.52 us
  matrix products: 33.1 us -> 0 us
  Pallas kernels: 0 us -> 25.7 us
  waiting for transfers between devices: 23.8 us -> 28.5 us
  starting transfers between devices: 29 us -> 33.2 us
  between operations: 4.33 us -> 1.09 us
    another operation x18 -> x0, other arithmetic: 111 us -> none  [the longest x13 69.6 us: inverse_factor(): lower_factor = jnp.linalg.cholesky(gram)]
    dot_general x12 -> x0, matrix products: 27.2 us -> none  [the longest x7 14.8 us: exact(): lax.dot_general(a.astype(jnp.float32), b.astype(jnp.float32), ((contract[...]
    pallas_call x0 -> x2, Pallas kernels: none -> 25.7 us  [the longest x1 22.7 us: body(): pl.pallas_call(functools.partial(finish_kernel, chains, rows_total, facto...]
    another operation x21 -> x2, local copies, waits for them, and re-layouts: 10.6 us -> 0.04 us  [the longest x15 9.76 us: inverse_factor(): jax.scipy.linalg.solve_triangular(lower_factor, identity_k, lower=True)]
    dynamic_update_slice x11 -> x9, local copies, waits for them, and re-layouts: 10.4 us -> 0.1 us  [gather_stage(): out = lax.dynamic_update_slice_in_dim(out, got[k], (me ^ k) * rows, 0)]
    concatenate x3 -> x0, other arithmetic: 8.44 us -> none  [the longest x1 5.83 us: body(): jnp.concatenate([jnp.concatenate([at(i, j) for j in range(nb)], axis=1) f...]
    another operation x10 -> x0, matrix products: 5.85 us -> none  [the longest x4 3.26 us: inverse_factor(): lower_factor = jnp.linalg.cholesky(gram)]
    ppermute x25, waiting for transfers between devices: 23.8 us -> 28.5 us  [exchange(): return lax.ppermute(value, AXIS, [(i, i ^ distance) for i in range(n)])]
  transfers between devices with their start and end apart: 25 -> 25, of which waited for: 9 -> 11; matrix products, arithmetic and copies ran while one was open for 9% -> 4% of each run, Pallas kernels for 0% -> 0%
where the time goes in v2:
time: 96.9 us; the launch traced here: 96.5 us
  starting transfers between devices  33.2 us (34%)
  waiting for transfers between devices  28.5 us (29%)
  Pallas kernels  25.7 us (27%)
  local copies, waits for them, and re-layouts  4.52 us (5%)
  other arithmetic  3.6 us (4%)
  between operations  1.09 us (1%)
    ppermute x25, starting transfers between devices, exchange(): return lax.ppermute(value, AXIS, [(i, i ^ distance) for i in range(n)])  33.2 us
    ppermute x25, waiting for transfers between devices, exchange(): return lax.ppermute(value, AXIS, [(i, i ^ distance) for i in range(n)])  28.5 us
    pallas_call x1, Pallas kernels, body(): pl.pallas_call(functools.partial(finish_kernel, chains, rows_total, facto...  22.7 us
    unnamed x4, local copies, waits for them, and re-layouts  4.15 us
    pallas_call x1, Pallas kernels, body(): pl.pallas_call(functools.partial(moment_kernel, chains), out_shape=[jax.S...  2.94 us
    add x4, other arithmetic, scatter_stage(): total = total + item  2.36 us
  transfers between devices with their start and end apart: 25, of which 11 were waited for; matrix products, arithmetic and copies ran while one was open for 4% of the time, Pallas kernels for 0%

profile of v2, /device:TPU:0, one launch (start us, length us, event | category | flops | bytes accessed | tf_op | source)
XLA Modules:
  0.0 96.5 jit_solution(17659148993893170166)
XLA Ops:
  0.6 0.0 copy-start
  0.7 2.2 %copy-done = bf16[2048,1024]{1,0:T(8,128)(2,1)S(1)} copy-done((bf16[2048,1024]{1,0:T(8,128)(2,1)S(1)}, bf16[2048,1024]{1,0:T(8,128)(2,1)}, u32[]{:S(2)}) %copy-start) | copy-done | bytes 4194328
  2.8 2.9 %shard_map.41 = (f32[1152,256]{1,0:T(8,128)S(1)}, f32[1152,256]{1,0:T(8,128)S(1)}) custom-call(bf16[2048,1024]{1,0:T(8,128)(2,1)S(1)} %copy-done), custom_call_target="tpu_custom_call" | custom-call | tf_op jit(solution)/shard_map/pallas_call | solution.py:270
  5.8 0.5 collective-permute-start.15
  6.4 0.1 collective-permute-start.5
  6.5 0.4 collective-permute-start
  7.0 1.1 %collective-permute-done.15 = f32[576,256]{1,0:T(8,128)} collective-permute-done((f32[576,256]{1,0:T(8,128)S(1)}, f32[576,256]{1,0:T(8,128)}, u32[]{:S(2)}, u32[]{:S(2)}) %collective-permute-start.15) | collective-permute-done | bytes 589856 | tf_op jit(solution)/shard_map/ppermute | solution.py:22
  8.1 1.1 %dynamic-slice_add_fusion = f32[576,256]{1,0:T(8,128)S(1)} fusion(f32[576,256]{1,0:T(8,128)} %collective-permute-done.15, f32[1152,256]{1,0:T(8,128)S(1)} %get-tuple-element.5, s32[]{:T(128)S(6)} %select_n.102), kind=kLoop, calls=%fused_computation.4 | loop fusion | flops 147456 | bytes 1769476 | tf_op jit(solution)/shard_map/add | solution.py:35
  9.3 3.0 %collective-permute-start.16 = (f32[288,256]{1,0:T(8,128)S(1)}, f32[288,256]{1,0:T(8,128)S(1)}, u32[]{:S(2)}, u32[]{:S(2)}) collective-permute-start(f32[288,256]{1,0:T(8,128)S(1)} %constant_dynamic-slice_fusion.3), channel_id=1, source_target_pairs={{0,2},{1,3},{2,0},{3,1},{4,6},{5,7},{6,4},{7,5},{8,10},{9,11},{10,... | collective-permute-start | bytes 884744 | tf_op jit(solution)/shard_map/ppermute | solution.py:22
  12.2 0.0 collective-permute-done.5
  12.3 1.1 %dynamic-slice_add_fusion.1 = f32[576,256]{1,0:T(8,128)S(1)} fusion(f32[576,256]{1,0:T(8,128)} %collective-permute-done.5, f32[1152,256]{1,0:T(8,128)S(1)} %get-tuple-element.4, s32[]{:T(128)S(6)} %select_n.102), kind=kLoop, calls=%fused_computation.5 | loop fusion | flops 147456 | bytes 1769476 | tf_op jit(solution)/shard_map/add | solution.py:35
  13.4 0.1 collective-permute-start.6
  13.5 6.5 %collective-permute-done.16 = f32[288,256]{1,0:T(8,128)S(1)} collective-permute-done((f32[288,256]{1,0:T(8,128)S(1)}, f32[288,256]{1,0:T(8,128)S(1)}, u32[]{:S(2)}, u32[]{:S(2)}) %collective-permute-start.16) | collective-permute-done | bytes 294944 | tf_op jit(solution)/shard_map/ppermute | solution.py:22
  20.1 2.2 %collective-permute-start.17 = (f32[72,256]{1,0:T(8,128)S(1)}, f32[72,256]{1,0:T(8,128)S(1)}, u32[]{:S(2)}, u32[]{:S(2)}) collective-permute-start(f32[72,256]{1,0:T(8,128)S(1)} %get-tuple-element.12), channel_id=1, source_target_pairs={{0,4},{1,5},{2,6},{3,7},{4,0},{5,1},{6,2},{7,3},{8,12},{9,13},{10,... | collective-permute-start | bytes 221192 | tf_op jit(solution)/shard_map/ppermute | solution.py:22
  22.3 2.6 %collective-permute-start.18 = (f32[72,256]{1,0:T(8,128)S(1)}, f32[72,256]{1,0:T(8,128)S(1)}, u32[]{:S(2)}, u32[]{:S(2)}) collective-permute-start(f32[72,256]{1,0:T(8,128)S(1)} %get-tuple-element.14), channel_id=1, source_target_pairs={{0,8},{1,9},{2,10},{3,11},{4,12},{5,13},{6,14},{7,15},{8,0},{9,1},... | collective-permute-start | bytes 221192 | tf_op jit(solution)/shard_map/ppermute | solution.py:22
  24.9 0.0 collective-permute-start.19
  24.9 1.0 %collective-permute-done.6 = f32[288,256]{1,0:T(8,128)S(1)} collective-permute-done((f32[288,256]{1,0:T(8,128)S(1)}, f32[288,256]{1,0:T(8,128)S(1)}, u32[]{:S(2)}, u32[]{:S(2)}) %collective-permute-start.6) | collective-permute-done | bytes 294944 | tf_op jit(solution)/shard_map/ppermute | solution.py:22
  26.0 1.9 %collective-permute-start.7 = (f32[72,256]{1,0:T(8,128)S(1)}, f32[72,256]{1,0:T(8,128)S(1)}, u32[]{:S(2)}, u32[]{:S(2)}) collective-permute-start(f32[72,256]{1,0:T(8,128)S(1)} %get-tuple-element.15), channel_id=1, source_target_pairs={{0,4},{1,5},{2,6},{3,7},{4,0},{5,1},{6,2},{7,3},{8,12},{9,13},{10,... | collective-permute-start | bytes 221192 | tf_op jit(solution)/shard_map/ppermute | solution.py:22
  27.8 2.6 %collective-permute-start.8 = (f32[72,256]{1,0:T(8,128)S(1)}, f32[72,256]{1,0:T(8,128)S(1)}, u32[]{:S(2)}, u32[]{:S(2)}) collective-permute-start(f32[72,256]{1,0:T(8,128)S(1)} %get-tuple-element.17), channel_id=1, source_target_pairs={{0,8},{1,9},{2,10},{3,11},{4,12},{5,13},{6,14},{7,15},{8,0},{9,1},... | collective-permute-start | bytes 221192 | tf_op jit(solution)/shard_map/ppermute | solution.py:22
  30.4 1.9 %collective-permute-start.9 = (f32[72,256]{1,0:T(8,128)S(1)}, f32[72,256]{1,0:T(8,128)S(1)}, u32[]{:S(2)}, u32[]{:S(2)}) collective-permute-start(f32[72,256]{1,0:T(8,128)S(1)} %get-tuple-element.16), channel_id=1, source_target_pairs={{0,12},{1,13},{2,14},{3,15},{4,8},{5,9},{6,10},{7,11},{8,4},{9,5},... | collective-permute-start | bytes 221192 | tf_op jit(solution)/shard_map/ppermute | solution.py:22
  32.4 0.1 collective-permute-start.20
  32.4 2.5 %collective-permute-start.21 = (f32[72,256]{1,0:T(8,128)S(1)}, f32[72,256]{1,0:T(8,128)S(1)}, u32[]{:S(2)}, u32[]{:S(2)}) collective-permute-start(f32[72,256]{1,0:T(8,128)S(1)} %get-tuple-element.7), channel_id=1, source_target_pairs={{0,8},{1,9},{2,10},{3,11},{4,12},{5,13},{6,14},{7,15},{8,0},{9,1},... | collective-permute-start | bytes 221192 | tf_op jit(solution)/shard_map/ppermute | solution.py:22
  34.9 2.9 %collective-permute-done.8 = f32[72,256]{1,0:T(8,128)S(1)} collective-permute-done((f32[72,256]{1,0:T(8,128)S(1)}, f32[72,256]{1,0:T(8,128)S(1)}, u32[]{:S(2)}, u32[]{:S(2)}) %collective-permute-start.8) | collective-permute-done | bytes 73760 | tf_op jit(solution)/shard_map/ppermute | solution.py:22
  37.8 2.5 %collective-permute-start.22 = (f32[72,256]{1,0:T(8,128)S(1)}, f32[72,256]{1,0:T(8,128)S(1)}, u32[]{:S(2)}, u32[]{:S(2)}) collective-permute-start(f32[72,256]{1,0:T(8,128)S(1)} %get-tuple-element.7), channel_id=1, source_target_pairs={{0,12},{1,13},{2,14},{3,15},{4,8},{5,9},{6,10},{7,11},{8,4},{9,5},... | collective-permute-start | bytes 221192 | tf_op jit(solution)/shard_map/ppermute | solution.py:22
  40.4 1.8 %collective-permute-start.10 = (f32[72,256]{1,0:T(8,128)S(1)}, f32[72,256]{1,0:T(8,128)S(1)}, u32[]{:S(2)}, u32[]{:S(2)}) collective-permute-start(f32[72,256]{1,0:T(8,128)S(1)} %get-tuple-element.9), channel_id=1, source_target_pairs={{0,4},{1,5},{2,6},{3,7},{4,0},{5,1},{6,2},{7,3},{8,12},{9,13},{10,... | collective-permute-start | bytes 221192 | tf_op jit(solution)/shard_map/ppermute | solution.py:22
  42.2 0.7 collective-permute-start.11
  42.9 0.2 collective-permute-done.21
  43.1 2.1 %collective-permute-start.12 = (f32[72,256]{1,0:T(8,128)S(1)}, f32[72,256]{1,0:T(8,128)S(1)}, u32[]{:S(2)}, u32[]{:S(2)}) collective-permute-start(f32[72,256]{1,0:T(8,128)S(1)} %get-tuple-element.9), channel_id=1, source_target_pairs={{0,12},{1,13},{2,14},{3,15},{4,8},{5,9},{6,10},{7,11},{8,4},{9,5},... | collective-permute-start | bytes 221192 | tf_op jit(solution)/shard_map/ppermute | solution.py:22
  45.2 1.6 %collective-permute-start.23 = (f32[288,256]{1,0:T(8,128)S(1)}, f32[288,256]{1,0:T(8,128)S(1)}, u32[]{:S(2)}, u32[]{:S(2)}) collective-permute-start(f32[288,256]{1,0:T(8,128)S(1)} %constant_dynamic-update-slice_fusion), channel_id=1, source_target_pairs={{0,2},{1,3},{2,0},{3,1},{4,6},{5,7},{6,4},{7,5},{8,10},{9,11},{10,... | collective-permute-start | bytes 884744 | tf_op jit(solution)/shard_map/ppermute | solution.py:22
  46.8 1.7 %collective-permute-done.11 = f32[72,256]{1,0:T(8,128)S(1)} collective-permute-done((f32[72,256]{1,0:T(8,128)S(1)}, f32[72,256]{1,0:T(8,128)S(1)}, u32[]{:S(2)}, u32[]{:S(2)}) %collective-permute-start.11) | collective-permute-done | bytes 73760 | tf_op jit(solution)/shard_map/ppermute | solution.py:22
  48.5 0.8 collective-permute-done.12
  49.3 1.6 %collective-permute-start.13 = (f32[288,256]{1,0:T(8,128)S(1)}, f32[288,256]{1,0:T(8,128)S(1)}, u32[]{:S(2)}, u32[]{:S(2)}) collective-permute-start(f32[288,256]{1,0:T(8,128)S(1)} %constant_dynamic-update-slice_fusion.4), channel_id=1, source_target_pairs={{0,2},{1,3},{2,0},{3,1},{4,6},{5,7},{6,4},{7,5},{8,10},{9,11},{10,... | collective-permute-start | bytes 884744 | tf_op jit(solution)/shard_map/ppermute | solution.py:22
  50.9 0.9 maximum_select_fusion.5
  51.8 0.6 collective-permute-start.1
  52.4 2.3 %collective-permute-done.23 = f32[288,256]{1,0:T(8,128)S(1)} collective-permute-done((f32[288,256]{1,0:T(8,128)S(1)}, f32[288,256]{1,0:T(8,128)S(1)}, u32[]{:S(2)}, u32[]{:S(2)}) %collective-permute-start.23) | collective-permute-done | bytes 294944 | tf_op jit(solution)/shard_map/ppermute | solution.py:22
  54.8 0.1 collective-permute-start.24
  54.8 4.9 %collective-permute-done.1 = bf16[128,256]{1,0:T(8,128)(2,1)S(1)} collective-permute-done((bf16[128,256]{1,0:T(8,128)(2,1)S(1)}, bf16[128,256]{1,0:T(8,128)(2,1)S(1)}, u32[]{:S(2)}, u32[]{:S(2)}) %collective-permute-start.1) | collective-permute-done | bytes 65568 | tf_op jit(solution)/shard_map/ppermute | solution.py:22
  59.8 0.9 collective-permute-start.2
  60.7 1.5 %collective-permute-start.3 = (bf16[256,256]{1,0:T(8,128)(2,1)S(1)}, bf16[256,256]{1,0:T(8,128)(2,1)S(1)}, u32[]{:S(2)}, u32[]{:S(2)}) collective-permute-start(bf16[256,256]{1,0:T(8,128)(2,1)S(1)} %get-tuple-element.11), channel_id=1, source_target_pairs={{0,8},{1,9},{2,10},{3,11},{4,12},{5,13},{6,14},{7,15},{8,0},{9,1},... | collective-permute-start | bytes 393224 | tf_op jit(solution)/shard_map/ppermute | solution.py:22
  62.2 2.0 %collective-permute-start.4 = (bf16[256,256]{1,0:T(8,128)(2,1)S(1)}, bf16[256,256]{1,0:T(8,128)(2,1)S(1)}, u32[]{:S(2)}, u32[]{:S(2)}) collective-permute-start(bf16[256,256]{1,0:T(8,128)(2,1)S(1)} %get-tuple-element.11), channel_id=1, source_target_pairs={{0,12},{1,13},{2,14},{3,15},{4,8},{5,9},{6,10},{7,11},{8,4},{9,5},... | collective-permute-start | bytes 393224 | tf_op jit(solution)/shard_map/ppermute | solution.py:22
  64.3 0.1 collective-permute-start.14
  64.4 2.2 %collective-permute-done.2 = bf16[256,256]{1,0:T(8,128)(2,1)S(1)} collective-permute-done((bf16[256,256]{1,0:T(8,128)(2,1)S(1)}, bf16[256,256]{1,0:T(8,128)(2,1)S(1)}, u32[]{:S(2)}, u32[]{:S(2)}) %collective-permute-start.2) | collective-permute-done | bytes 131104 | tf_op jit(solution)/shard_map/ppermute | solution.py:22
  66.6 4.7 %collective-permute-done.3 = bf16[256,256]{1,0:T(8,128)(2,1)S(1)} collective-permute-done((bf16[256,256]{1,0:T(8,128)(2,1)S(1)}, bf16[256,256]{1,0:T(8,128)(2,1)S(1)}, u32[]{:S(2)}, u32[]{:S(2)}) %collective-permute-start.3) | collective-permute-done | bytes 131104 | tf_op jit(solution)/shard_map/ppermute | solution.py:22
  71.4 0.0 copy-start.1
  71.4 0.1 maximum_select_fusion.1.refs_1_
  71.5 0.1 maximum_select_fusion.refs_0_
  71.7 2.0 %copy-done.1 = bf16[2048,1024]{1,0:T(8,128)(2,1)S(1)} copy-done((bf16[2048,1024]{1,0:T(8,128)(2,1)S(1)}, bf16[2048,1024]{1,0:T(8,128)(2,1)}, u32[]{:S(2)}) %copy-start.1) | copy-done | bytes 4194328
  73.6 22.7 %shard_map.42 = (bf16[2048,256]{1,0:T(8,128)(2,1)}, bf16[64,256]{1,0:T(8,128)(2,1)}) custom-call(s32[1]{0:T(128)} %bitcast.me_ref, bf16[1024,256]{1,0:T(8,128)(2,1)S(1)} %constant_dynamic-update-slice_fusion.8.sketch_ref, bf16[2048,1024]{1,0:T(8,128)(2,1)S(1)} %copy-done.1, f32[1152,256]{1,0:T(8,128)S(1)} %maximum_select_fusion.refs_0_, ...), custom_call_target="tpu_custom_call" | custom-call | tf_op jit(solution)/shard_map/pallas_call | solution.py:280
  (38 shorter events, 0.7 us)
Async XLA Ops:
  0.6 2.2 %copy-start = (bf16[2048,1024]{1,0:T(8,128)(2,1)S(1)}, bf16[2048,1024]{1,0:T(8,128)(2,1)}, u32[]{:S(2)}) copy-start(bf16[2048,1024]{1,0:T(8,128)(2,1)} %a_hbm.1) | copy-start | bytes 12582916
  5.8 2.3 %collective-permute-start.15 = (f32[576,256]{1,0:T(8,128)S(1)}, f32[576,256]{1,0:T(8,128)}, u32[]{:S(2)}, u32[]{:S(2)}) collective-permute-start(f32[576,256]{1,0:T(8,128)S(1)} %constant_dynamic-slice_fusion.4), channel_id=1, source_target_pairs={{0,1},{1,0},{2,3},{3,2},{4,5},{5,4},{6,7},{7,6},{8,9},{9,8},{10,11... | collective-permute-start | bytes 1769480 | tf_op jit(solution)/shard_map/ppermute | solution.py:22
  6.4 5.9 %collective-permute-start.5 = (f32[576,256]{1,0:T(8,128)S(1)}, f32[576,256]{1,0:T(8,128)}, u32[]{:S(2)}, u32[]{:S(2)}) collective-permute-start(f32[576,256]{1,0:T(8,128)S(1)} %constant_dynamic-slice_fusion.9), channel_id=1, source_target_pairs={{0,1},{1,0},{2,3},{3,2},{4,5},{5,4},{6,7},{7,6},{8,9},{9,8},{10,11... | collective-permute-start | bytes 1769480 | tf_op jit(solution)/shard_map/ppermute | solution.py:22
  6.5 44.4 %collective-permute-start = (bf16[64,256]{1,0:T(8,128)(2,1)}, bf16[64,256]{1,0:T(8,128)(2,1)}, u32[]{:S(2)}, u32[]{:S(2)}) collective-permute-start(bf16[64,256]{1,0:T(8,128)(2,1)} %param.3), channel_id=1, source_target_pairs={{0,1},{1,0},{2,3},{3,2},{4,5},{5,4},{6,7},{7,6},{8,9},{9,8},{10,11... | collective-permute-start | bytes 98312 | tf_op jit(solution)/shard_map/ppermute | solution.py:22
  9.3 10.7 %collective-permute-start.16 = (f32[288,256]{1,0:T(8,128)S(1)}, f32[288,256]{1,0:T(8,128)S(1)}, u32[]{:S(2)}, u32[]{:S(2)}) collective-permute-start(f32[288,256]{1,0:T(8,128)S(1)} %constant_dynamic-slice_fusion.3), channel_id=1, source_target_pairs={{0,2},{1,3},{2,0},{3,1},{4,6},{5,7},{6,4},{7,5},{8,10},{9,11},{10,... | collective-permute-start | bytes 884744 | tf_op jit(solution)/shard_map/ppermute | solution.py:22
  13.4 12.4 %collective-permute-start.6 = (f32[288,256]{1,0:T(8,128)S(1)}, f32[288,256]{1,0:T(8,128)S(1)}, u32[]{:S(2)}, u32[]{:S(2)}) collective-permute-start(f32[288,256]{1,0:T(8,128)S(1)} %constant_dynamic-slice_fusion.8), channel_id=1, source_target_pairs={{0,2},{1,3},{2,0},{3,1},{4,6},{5,7},{6,4},{7,5},{8,10},{9,11},{10,... | collective-permute-start | bytes 884744 | tf_op jit(solution)/shard_map/ppermute | solution.py:22
  20.1 7.7 %collective-permute-start.17 = (f32[72,256]{1,0:T(8,128)S(1)}, f32[72,256]{1,0:T(8,128)S(1)}, u32[]{:S(2)}, u32[]{:S(2)}) collective-permute-start(f32[72,256]{1,0:T(8,128)S(1)} %get-tuple-element.12), channel_id=1, source_target_pairs={{0,4},{1,5},{2,6},{3,7},{4,0},{5,1},{6,2},{7,3},{8,12},{9,13},{10,... | collective-permute-start | bytes 221192 | tf_op jit(solution)/shard_map/ppermute | solution.py:22
  22.3 8.1 %collective-permute-start.18 = (f32[72,256]{1,0:T(8,128)S(1)}, f32[72,256]{1,0:T(8,128)S(1)}, u32[]{:S(2)}, u32[]{:S(2)}) collective-permute-start(f32[72,256]{1,0:T(8,128)S(1)} %get-tuple-element.14), channel_id=1, source_target_pairs={{0,8},{1,9},{2,10},{3,11},{4,12},{5,13},{6,14},{7,15},{8,0},{9,1},... | collective-permute-start | bytes 221192 | tf_op jit(solution)/shard_map/ppermute | solution.py:22
  24.9 7.4 %collective-permute-start.19 = (f32[72,256]{1,0:T(8,128)S(1)}, f32[72,256]{1,0:T(8,128)S(1)}, u32[]{:S(2)}, u32[]{:S(2)}) collective-permute-start(f32[72,256]{1,0:T(8,128)S(1)} %get-tuple-element.13), channel_id=1, source_target_pairs={{0,12},{1,13},{2,14},{3,15},{4,8},{5,9},{6,10},{7,11},{8,4},{9,5},... | collective-permute-start | bytes 221192 | tf_op jit(solution)/shard_map/ppermute | solution.py:22
  26.0 6.5 %collective-permute-start.7 = (f32[72,256]{1,0:T(8,128)S(1)}, f32[72,256]{1,0:T(8,128)S(1)}, u32[]{:S(2)}, u32[]{:S(2)}) collective-permute-start(f32[72,256]{1,0:T(8,128)S(1)} %get-tuple-element.15), channel_id=1, source_target_pairs={{0,4},{1,5},{2,6},{3,7},{4,0},{5,1},{6,2},{7,3},{8,12},{9,13},{10,... | collective-permute-start | bytes 221192 | tf_op jit(solution)/shard_map/ppermute | solution.py:22
  27.8 10.0 %collective-permute-start.8 = (f32[72,256]{1,0:T(8,128)S(1)}, f32[72,256]{1,0:T(8,128)S(1)}, u32[]{:S(2)}, u32[]{:S(2)}) collective-permute-start(f32[72,256]{1,0:T(8,128)S(1)} %get-tuple-element.17), channel_id=1, source_target_pairs={{0,8},{1,9},{2,10},{3,11},{4,12},{5,13},{6,14},{7,15},{8,0},{9,1},... | collective-permute-start | bytes 221192 | tf_op jit(solution)/shard_map/ppermute | solution.py:22
  30.4 9.9 %collective-permute-start.9 = (f32[72,256]{1,0:T(8,128)S(1)}, f32[72,256]{1,0:T(8,128)S(1)}, u32[]{:S(2)}, u32[]{:S(2)}) collective-permute-start(f32[72,256]{1,0:T(8,128)S(1)} %get-tuple-element.16), channel_id=1, source_target_pairs={{0,12},{1,13},{2,14},{3,15},{4,8},{5,9},{6,10},{7,11},{8,4},{9,5},... | collective-permute-start | bytes 221192 | tf_op jit(solution)/shard_map/ppermute | solution.py:22
  32.4 9.8 %collective-permute-start.20 = (f32[72,256]{1,0:T(8,128)S(1)}, f32[72,256]{1,0:T(8,128)S(1)}, u32[]{:S(2)}, u32[]{:S(2)}) collective-permute-start(f32[72,256]{1,0:T(8,128)S(1)} %get-tuple-element.7), channel_id=1, source_target_pairs={{0,4},{1,5},{2,6},{3,7},{4,0},{5,1},{6,2},{7,3},{8,12},{9,13},{10,... | collective-permute-start | bytes 221192 | tf_op jit(solution)/shard_map/ppermute | solution.py:22
  32.4 10.6 %collective-permute-start.21 = (f32[72,256]{1,0:T(8,128)S(1)}, f32[72,256]{1,0:T(8,128)S(1)}, u32[]{:S(2)}, u32[]{:S(2)}) collective-permute-start(f32[72,256]{1,0:T(8,128)S(1)} %get-tuple-element.7), channel_id=1, source_target_pairs={{0,8},{1,9},{2,10},{3,11},{4,12},{5,13},{6,14},{7,15},{8,0},{9,1},... | collective-permute-start | bytes 221192 | tf_op jit(solution)/shard_map/ppermute | solution.py:22
  37.8 7.3 %collective-permute-start.22 = (f32[72,256]{1,0:T(8,128)S(1)}, f32[72,256]{1,0:T(8,128)S(1)}, u32[]{:S(2)}, u32[]{:S(2)}) collective-permute-start(f32[72,256]{1,0:T(8,128)S(1)} %get-tuple-element.7), channel_id=1, source_target_pairs={{0,12},{1,13},{2,14},{3,15},{4,8},{5,9},{6,10},{7,11},{8,4},{9,5},... | collective-permute-start | bytes 221192 | tf_op jit(solution)/shard_map/ppermute | solution.py:22
  40.4 6.4 %collective-permute-start.10 = (f32[72,256]{1,0:T(8,128)S(1)}, f32[72,256]{1,0:T(8,128)S(1)}, u32[]{:S(2)}, u32[]{:S(2)}) collective-permute-start(f32[72,256]{1,0:T(8,128)S(1)} %get-tuple-element.9), channel_id=1, source_target_pairs={{0,4},{1,5},{2,6},{3,7},{4,0},{5,1},{6,2},{7,3},{8,12},{9,13},{10,... | collective-permute-start | bytes 221192 | tf_op jit(solution)/shard_map/ppermute | solution.py:22
  42.2 6.3 %collective-permute-start.11 = (f32[72,256]{1,0:T(8,128)S(1)}, f32[72,256]{1,0:T(8,128)S(1)}, u32[]{:S(2)}, u32[]{:S(2)}) collective-permute-start(f32[72,256]{1,0:T(8,128)S(1)} %get-tuple-element.9), channel_id=1, source_target_pairs={{0,8},{1,9},{2,10},{3,11},{4,12},{5,13},{6,14},{7,15},{8,0},{9,1},... | collective-permute-start | bytes 221192 | tf_op jit(solution)/shard_map/ppermute | solution.py:22
  43.1 6.3 %collective-permute-start.12 = (f32[72,256]{1,0:T(8,128)S(1)}, f32[72,256]{1,0:T(8,128)S(1)}, u32[]{:S(2)}, u32[]{:S(2)}) collective-permute-start(f32[72,256]{1,0:T(8,128)S(1)} %get-tuple-element.9), channel_id=1, source_target_pairs={{0,12},{1,13},{2,14},{3,15},{4,8},{5,9},{6,10},{7,11},{8,4},{9,5},... | collective-permute-start | bytes 221192 | tf_op jit(solution)/shard_map/ppermute | solution.py:22
  45.2 9.5 %collective-permute-start.23 = (f32[288,256]{1,0:T(8,128)S(1)}, f32[288,256]{1,0:T(8,128)S(1)}, u32[]{:S(2)}, u32[]{:S(2)}) collective-permute-start(f32[288,256]{1,0:T(8,128)S(1)} %constant_dynamic-update-slice_fusion), channel_id=1, source_target_pairs={{0,2},{1,3},{2,0},{3,1},{4,6},{5,7},{6,4},{7,5},{8,10},{9,11},{10,... | collective-permute-start | bytes 884744 | tf_op jit(solution)/shard_map/ppermute | solution.py:22
  49.3 14.9 %collective-permute-start.13 = (f32[288,256]{1,0:T(8,128)S(1)}, f32[288,256]{1,0:T(8,128)S(1)}, u32[]{:S(2)}, u32[]{:S(2)}) collective-permute-start(f32[288,256]{1,0:T(8,128)S(1)} %constant_dynamic-update-slice_fusion.4), channel_id=1, source_target_pairs={{0,2},{1,3},{2,0},{3,1},{4,6},{5,7},{6,4},{7,5},{8,10},{9,11},{10,... | collective-permute-start | bytes 884744 | tf_op jit(solution)/shard_map/ppermute | solution.py:22
  51.8 7.9 %collective-permute-start.1 = (bf16[128,256]{1,0:T(8,128)(2,1)S(1)}, bf16[128,256]{1,0:T(8,128)(2,1)S(1)}, u32[]{:S(2)}, u32[]{:S(2)}) collective-permute-start(bf16[128,256]{1,0:T(8,128)(2,1)S(1)} %maximum_select_fusion.5), channel_id=1, source_target_pairs={{0,2},{1,3},{2,0},{3,1},{4,6},{5,7},{6,4},{7,5},{8,10},{9,11},{10,... | collective-permute-start | bytes 196616 | tf_op jit(solution)/shard_map/ppermute | solution.py:22
  54.8 16.7 %collective-permute-start.24 = (f32[576,256]{1,0:T(8,128)S(1)}, f32[576,256]{1,0:T(8,128)S(1)}, u32[]{:S(2)}, u32[]{:S(2)}) collective-permute-start(f32[576,256]{1,0:T(8,128)S(1)} %maximum_select_fusion.3), channel_id=1, source_target_pairs={{0,1},{1,0},{2,3},{3,2},{4,5},{5,4},{6,7},{7,6},{8,9},{9,8},{10,11... | collective-permute-start | bytes 1769480 | tf_op jit(solution)/shard_map/ppermute | solution.py:22
  59.8 6.8 %collective-permute-start.2 = (bf16[256,256]{1,0:T(8,128)(2,1)S(1)}, bf16[256,256]{1,0:T(8,128)(2,1)S(1)}, u32[]{:S(2)}, u32[]{:S(2)}) collective-permute-start(bf16[256,256]{1,0:T(8,128)(2,1)S(1)} %get-tuple-element.11), channel_id=1, source_target_pairs={{0,4},{1,5},{2,6},{3,7},{4,0},{5,1},{6,2},{7,3},{8,12},{9,13},{10,... | collective-permute-start | bytes 393224 | tf_op jit(solution)/shard_map/ppermute | solution.py:22
  60.7 10.7 %collective-permute-start.3 = (bf16[256,256]{1,0:T(8,128)(2,1)S(1)}, bf16[256,256]{1,0:T(8,128)(2,1)S(1)}, u32[]{:S(2)}, u32[]{:S(2)}) collective-permute-start(bf16[256,256]{1,0:T(8,128)(2,1)S(1)} %get-tuple-element.11), channel_id=1, source_target_pairs={{0,8},{1,9},{2,10},{3,11},{4,12},{5,13},{6,14},{7,15},{8,0},{9,1},... | collective-permute-start | bytes 393224 | tf_op jit(solution)/shard_map/ppermute | solution.py:22
  62.2 9.2 %collective-permute-start.4 = (bf16[256,256]{1,0:T(8,128)(2,1)S(1)}, bf16[256,256]{1,0:T(8,128)(2,1)S(1)}, u32[]{:S(2)}, u32[]{:S(2)}) collective-permute-start(bf16[256,256]{1,0:T(8,128)(2,1)S(1)} %get-tuple-element.11), channel_id=1, source_target_pairs={{0,12},{1,13},{2,14},{3,15},{4,8},{5,9},{6,10},{7,11},{8,4},{9,5},... | collective-permute-start | bytes 393224 | tf_op jit(solution)/shard_map/ppermute | solution.py:22
  64.3 7.2 %collective-permute-start.14 = (f32[576,256]{1,0:T(8,128)S(1)}, f32[576,256]{1,0:T(8,128)S(1)}, u32[]{:S(2)}, u32[]{:S(2)}) collective-permute-start(f32[576,256]{1,0:T(8,128)S(1)} %maximum_select_fusion.2), channel_id=1, source_target_pairs={{0,1},{1,0},{2,3},{3,2},{4,5},{5,4},{6,7},{7,6},{8,9},{9,8},{10,11... | collective-permute-start | bytes 1769480 | tf_op jit(solution)/shard_map/ppermute | solution.py:22
  71.4 2.2 %copy-start.1 = (bf16[2048,1024]{1,0:T(8,128)(2,1)S(1)}, bf16[2048,1024]{1,0:T(8,128)(2,1)}, u32[]{:S(2)}) copy-start(bf16[2048,1024]{1,0:T(8,128)(2,1)} %a_hbm.1) | copy-start | bytes 12582916

commit v3 on v2

--- a/solution.py
+++ b/solution.py
@@ -53,18 +53,27 @@
     return [(0, 2), (1, 2), (2, n // 4)]
 
 
-def sum_everywhere(value):
-    for low, count in stages():
-        value = scatter_stage(value, low, count)
-    for low, count in reversed(stages()):
-        value = gather_stage(value, low, count)
-    return value
-
-
-def gather_rows(value):
-    for low, count in stages():
-        value = gather_stage(value, low, count)
-    return value
+def tie(value, other):
+    return lax.optimization_barrier((value, other))
+
+
+def sum_everywhere(parts, rows):
+    (c, _), (y, _), (z, others) = stages()
+    own = rows.shape[0]
+    parts = [scatter_stage(p, c, 2) for p in parts]
+    rows = gather_stage(rows, z, others)
+    parts = [scatter_stage(p, y, 2) for p in parts]
+    parts[0], rows = tie(parts[0], rows)
+    rows = gather_stage(rows, y, 2)
+    parts = [scatter_stage(p, z, others) for p in parts]
+    parts[0], rows = tie(parts[0], rows)
+    rows = gather_stage(rows, c, 2)
+    parts = [gather_stage(p, z, others) for p in parts]
+    parts[0], rows = tie(parts[0], rows)
+    parts = [gather_stage(p, y, 2) for p in parts]
+    parts = [gather_stage(p, c, 2) for p in parts]
+    rows = rows.reshape(2, 2, others, own, -1).transpose(2, 1, 0, 3, 4)
+    return parts, rows.reshape(4 * others * own, -1)
 
 
 def layout(time_steps):
@@ -96,21 +105,35 @@
     )
 
 
-def moment_kernel(chains, a_ref, *out_refs):
+def moment_kernel(chains, a_hbm, *refs):
+    out_refs, (a_ref, sems) = refs[: len(chains)], refs[len(chains) :]
+    nb = a_ref.shape[0]
+    fetches = [
+        pltpu.make_async_copy(a_hbm.at[:, pl.ds(i * EDGE, EDGE)], a_ref.at[i], sems.at[i])
+        for i in range(nb)
+    ]
+    for fetch in fetches:
+        fetch.start()
+    where = {}
     for chain, out in zip(chains, out_refs):
         row = 0
         for i, j in chain:
-            left = a_ref[:, i * EDGE : (i + 1) * EDGE]
-            block = product(left, a_ref[:, j * EDGE : (j + 1) * EDGE], ((0,), (0,)))
+            where[i, j] = out, row
+            row += EDGE if i != j else EDGE * 3 // 4
+    for i in range(nb):
+        fetches[i].wait()
+        left = a_ref[i]
+        for j in range(i + 1):
+            block = product(left, a_ref[j], ((0,), (0,)))
+            out, row = where[i, j]
             if i != j:
                 out[row : row + EDGE, :] = block
-                row += EDGE
             else:
+                cut = HALF + HALF // 2
                 out[row : row + HALF, :HALF] = block[:HALF, :HALF]
                 out[row : row + HALF, HALF:] = block[HALF:, HALF:]
-                out[row + HALF : row + HALF + HALF // 2, :HALF] = block[HALF : HALF + HALF // 2, :HALF]
-                out[row + HALF : row + HALF + HALF // 2, HALF:] = block[HALF + HALF // 2 :, :HALF]
-                row += EDGE * 3 // 4
+                out[row + HALF : row + cut, :HALF] = block[HALF:cut, :HALF]
+                out[row + HALF : row + cut, HALF:] = block[cut:, :HALF]
 
 
 def unpack(chains, refs, store):
@@ -266,15 +289,18 @@
     chains = layout(time_steps)
     vmem = pl.BlockSpec(memory_space=pltpu.VMEM)
 
-    sketch_all = gather_rows(sketch_matrix)
     partial = pl.pallas_call(
         functools.partial(moment_kernel, chains),
         out_shape=[jax.ShapeDtypeStruct((chain_rows(c), EDGE), F32) for c in chains],
-        in_specs=[vmem],
+        in_specs=[pl.BlockSpec(memory_space=pltpu.HBM)],
         out_specs=[vmem] * len(chains),
+        scratch_shapes=[
+            pltpu.VMEM((time_steps // EDGE, local_rows, EDGE), BF16),
+            pltpu.SemaphoreType.DMA((time_steps // EDGE,)),
+        ],
         compiler_params=pltpu.CompilerParams(vmem_limit_bytes=20 << 20),
     )(series_data)
-    summed = [sum_everywhere(p) for p in partial]
+    summed, sketch_all = sum_everywhere(list(partial), sketch_matrix)
     me = lax.axis_index(AXIS).astype(jnp.int32).reshape(1)
     return tuple(
         pl.pallas_call(
@@ -286,7 +312,7 @@
             in_specs=[
                 pl.BlockSpec(memory_space=pltpu.SMEM),
                 vmem,
-                pl.BlockSpec(memory_space=pl.ANY),
+                pl.BlockSpec(memory_space=pltpu.HBM),
             ]
             + [vmem] * len(chains),
             out_specs=[vmem, vmem],

time: 96.9 us -> 101 us (1.042)
  local copies, waits for them, and re-layouts: 4.52 us -> 8.83 us
  waiting for transfers between devices: 28.5 us -> 24.3 us
  Pallas kernels: 25.7 us -> 27.4 us
  starting transfers between devices: 33.2 us -> 34.8 us
    dynamic_update_slice x9 -> x11, local copies, waits for them, and re-layouts: 0.1 us -> 5.57 us  [gather_stage(): out = lax.dynamic_update_slice_in_dim(out, got[k], (me ^ k) * rows, 0)]
    ppermute x25, waiting for transfers between devices: 28.5 us -> 24.3 us  [exchange(): return lax.ppermute(value, AXIS, [(i, i ^ distance) for i in range(n)])]
    unnamed x4, local copies, waits for them, and re-layouts: 4.15 us -> 2.33 us
    pallas_call x1, Pallas kernels: 2.94 us -> 4.57 us  [body(): pl.pallas_call(functools.partial(moment_kernel, chains), out_shape=[jax.S...]
    ppermute x25, starting transfers between devices: 33.2 us -> 34.8 us  [exchange(): return lax.ppermute(value, AXIS, [(i, i ^ distance) for i in range(n)])]
    add x4 -> x5, other arithmetic: 2.36 us -> 2.38 us  [scatter_stage(): total = total + item]
  transfers between devices with their start and end apart: 25 -> 25, of which waited for: 11 -> 9; matrix products, arithmetic and copies ran while one was open for 4% -> 10% of each run, Pallas kernels for 0% -> 0%
where the time goes in v3:
time: 101 us; the launch traced here: 100 us
  starting transfers between devices  34.8 us (34%)
  Pallas kernels  27.4 us (27%)
  waiting for transfers between devices  24.3 us (24%)
  local copies, waits for them, and re-layouts  8.83 us (9%)
  other arithmetic  3.97 us (4%)
  between operations  1.12 us (1%)
    ppermute x25, starting transfers between devices, exchange(): return lax.ppermute(value, AXIS, [(i, i ^ distance) for i in range(n)])  34.8 us
    ppermute x25, waiting for transfers between devices, exchange(): return lax.ppermute(value, AXIS, [(i, i ^ distance) for i in range(n)])  24.3 us
    pallas_call x1, Pallas kernels, body(): pl.pallas_call(functools.partial(finish_kernel, chains, rows_total, facto...  22.8 us
    dynamic_update_slice x11, local copies, waits for them, and re-layouts, gather_stage(): out = lax.dynamic_update_slice_in_dim(out, got[k], (me ^ k) * rows, 0)  5.57 us
    pallas_call x1, Pallas kernels, body(): pl.pallas_call(functools.partial(moment_kernel, chains), out_shape=[jax.S...  4.57 us
    add x5, other arithmetic, scatter_stage(): total = total + item  2.38 us
    unnamed x4, local copies, waits for them, and re-layouts  2.33 us
  transfers between devices with their start and end apart: 25, of which 9 were waited for; matrix products, arithmetic and copies ran while one was open for 10% of the time, Pallas kernels for 0%

profile of v3, /device:TPU:0, one launch (start us, length us, event | category | flops | bytes accessed | tf_op | source)
XLA Modules:
  0.0 100.4 jit_solution(12437797968368185657)
XLA Ops:
  0.7 2.2 %copy-done = bf16[2048,1024]{1,0:T(8,128)(2,1)S(1)} copy-done((bf16[2048,1024]{1,0:T(8,128)(2,1)S(1)}, bf16[2048,1024]{1,0:T(8,128)(2,1)}, u32[]{:S(2)}) %copy-start) | copy-done | bytes 4194328
  2.8 4.6 %shard_map.41 = (f32[1152,256]{1,0:T(8,128)S(1)}, f32[1152,256]{1,0:T(8,128)S(1)}) custom-call(bf16[2048,1024]{1,0:T(8,128)(2,1)S(1)} %copy-done), custom_call_target="tpu_custom_call" | custom-call | tf_op jit(solution)/shard_map/pallas_call | solution.py:292
  7.5 0.5 collective-permute-start.15
  8.0 2.6 %collective-permute-start.2 = (bf16[64,256]{1,0:T(8,128)(2,1)}, bf16[64,256]{1,0:T(8,128)(2,1)}, u32[]{:S(2)}, u32[]{:S(2)}) collective-permute-start(bf16[64,256]{1,0:T(8,128)(2,1)} %param.3), channel_id=1, source_target_pairs={{0,4},{1,5},{2,6},{3,7},{4,0},{5,1},{6,2},{7,3},{8,12},{9,13},{10,... | collective-permute-start | bytes 98312 | tf_op jit(solution)/shard_map/ppermute | solution.py:22
  10.6 2.6 %collective-permute-start.3 = (bf16[64,256]{1,0:T(8,128)(2,1)}, bf16[64,256]{1,0:T(8,128)(2,1)}, u32[]{:S(2)}, u32[]{:S(2)}) collective-permute-start(bf16[64,256]{1,0:T(8,128)(2,1)} %param.3), channel_id=1, source_target_pairs={{0,8},{1,9},{2,10},{3,11},{4,12},{5,13},{6,14},{7,15},{8,0},{9,1},... | collective-permute-start | bytes 98312 | tf_op jit(solution)/shard_map/ppermute | solution.py:22
  13.3 0.1 collective-permute-start
  13.4 0.7 broadcast_in_dim.3
  14.0 1.4 %constant_dynamic-update-slice_fusion.11 = bf16[256,256]{1,0:T(8,128)(2,1)} fusion(bf16[256,256]{1,0:T(8,128)(2,1)} %broadcast_in_dim.3, bf16[64,256]{1,0:T(8,128)(2,1)} %param.3, s32[]{:T(128)S(6)} %select_n.96), kind=kLoop, calls=%fused_computation.31 | loop fusion | bytes 65540 | tf_op jit(solution)/shard_map/dynamic_update_slice | solution.py:47
  15.4 1.4 %constant_dynamic-update-slice_fusion.10 = bf16[256,256]{1,0:T(8,128)(2,1)} fusion(bf16[256,256]{1,0:T(8,128)(2,1)} %constant_dynamic-update-slice_fusion.11, bf16[64,256]{1,0:T(8,128)(2,1)} %collective-permute-done.2, s32[]{:T(128)S(6)} %select_n.97), kind=kLoop, calls=%fused_computation.30 | loop fusion | bytes 65540 | tf_op jit(solution)/shard_map/dynamic_update_slice | solution.py:47
  16.8 1.4 %constant_dynamic-update-slice_fusion.9 = bf16[256,256]{1,0:T(8,128)(2,1)} fusion(bf16[256,256]{1,0:T(8,128)(2,1)} %constant_dynamic-update-slice_fusion.10, bf16[64,256]{1,0:T(8,128)(2,1)} %collective-permute-done.3, s32[]{:T(128)S(6)} %select_n.98), kind=kLoop, calls=%fused_computation.29 | loop fusion | bytes 65540 | tf_op jit(solution)/shard_map/dynamic_update_slice | solution.py:47
  18.2 1.1 %collective-permute-done.4 = bf16[64,256]{1,0:T(8,128)(2,1)} collective-permute-done((bf16[64,256]{1,0:T(8,128)(2,1)}, bf16[64,256]{1,0:T(8,128)(2,1)}, u32[]{:S(2)}, u32[]{:S(2)}) %collective-permute-start.4) | collective-permute-done | bytes 32800 | tf_op jit(solution)/shard_map/ppermute | solution.py:22
  19.3 1.4 %constant_dynamic-update-slice_fusion.8 = bf16[256,256]{1,0:T(8,128)(2,1)} fusion(bf16[256,256]{1,0:T(8,128)(2,1)} %constant_dynamic-update-slice_fusion.9, bf16[64,256]{1,0:T(8,128)(2,1)} %collective-permute-done.4, s32[]{:T(128)S(6)} %select_n.99), kind=kLoop, calls=%fused_computation.28 | loop fusion | bytes 65540 | tf_op jit(solution)/shard_map/dynamic_update_slice | solution.py:47
  20.6 1.1 %dynamic-slice_add_fusion = f32[576,256]{1,0:T(8,128)S(1)} fusion(f32[576,256]{1,0:T(8,128)} %collective-permute-done.15, f32[1152,256]{1,0:T(8,128)S(1)} %get-tuple-element.17, s32[]{:T(128)S(6)} %select_n.92), kind=kLoop, calls=%fused_computation.4 | loop fusion | flops 147456 | bytes 1769476 | tf_op jit(solution)/shard_map/add | solution.py:35
  21.8 1.6 %collective-permute-start.16 = (f32[288,256]{1,0:T(8,128)S(1)}, f32[288,256]{1,0:T(8,128)S(1)}, u32[]{:S(2)}, u32[]{:S(2)}) collective-permute-start(f32[288,256]{1,0:T(8,128)S(1)} %constant_dynamic-slice_fusion.3), channel_id=1, source_target_pairs={{0,2},{1,3},{2,0},{3,1},{4,6},{5,7},{6,4},{7,5},{8,10},{9,11},{10,... | collective-permute-start | bytes 884744 | tf_op jit(solution)/shard_map/ppermute | solution.py:22
  23.4 1.1 %dynamic-slice_add_fusion.1 = f32[576,256]{1,0:T(8,128)S(1)} fusion(f32[576,256]{1,0:T(8,128)} %collective-permute-done, f32[1152,256]{1,0:T(8,128)S(1)} %get-tuple-element.10, s32[]{:T(128)S(6)} %select_n.92), kind=kLoop, calls=%fused_computation.5 | loop fusion | flops 147456 | bytes 1769476 | tf_op jit(solution)/shard_map/add | solution.py:35
  24.6 0.6 collective-permute-start.1
  25.2 6.7 %collective-permute-done.16 = f32[288,256]{1,0:T(8,128)S(1)} collective-permute-done((f32[288,256]{1,0:T(8,128)S(1)}, f32[288,256]{1,0:T(8,128)S(1)}, u32[]{:S(2)}, u32[]{:S(2)}) %collective-permute-start.16) | collective-permute-done | bytes 294944 | tf_op jit(solution)/shard_map/ppermute | solution.py:22
  31.9 0.1 collective-permute-start.17
  32.0 3.1 %collective-permute-start.18 = (f32[72,256]{1,0:T(8,128)S(1)}, f32[72,256]{1,0:T(8,128)S(1)}, u32[]{:S(2)}, u32[]{:S(2)}) collective-permute-start(f32[72,256]{1,0:T(8,128)S(1)} %get-tuple-element.22), channel_id=1, source_target_pairs={{0,8},{1,9},{2,10},{3,11},{4,12},{5,13},{6,14},{7,15},{8,0},{9,1},... | collective-permute-start | bytes 221192 | tf_op jit(solution)/shard_map/ppermute | solution.py:22
  35.1 1.2 %collective-permute-start.19 = (f32[72,256]{1,0:T(8,128)S(1)}, f32[72,256]{1,0:T(8,128)S(1)}, u32[]{:S(2)}, u32[]{:S(2)}) collective-permute-start(f32[72,256]{1,0:T(8,128)S(1)} %get-tuple-element.21), channel_id=1, source_target_pairs={{0,12},{1,13},{2,14},{3,15},{4,8},{5,9},{6,10},{7,11},{8,4},{9,5},... | collective-permute-start | bytes 221192 | tf_op jit(solution)/shard_map/ppermute | solution.py:22
  36.4 0.2 collective-permute-done.1
  36.5 1.8 %collective-permute-start.8 = (bf16[256,256]{1,0:T(8,128)(2,1)}, bf16[256,256]{1,0:T(8,128)(2,1)S(1)}, u32[]{:S(2)}, u32[]{:S(2)}) collective-permute-start(bf16[256,256]{1,0:T(8,128)(2,1)} %constant_dynamic-update-slice_fusion.8), channel_id=1, source_target_pairs={{0,2},{1,3},{2,0},{3,1},{4,6},{5,7},{6,4},{7,5},{8,10},{9,11},{10,... | collective-permute-start | bytes 393224 | tf_op jit(solution)/shard_map/ppermute | solution.py:22
  38.4 0.7 collective-permute-start.5
  39.1 3.5 %collective-permute-start.6 = (f32[72,256]{1,0:T(8,128)S(1)}, f32[72,256]{1,0:T(8,128)S(1)}, u32[]{:S(2)}, u32[]{:S(2)}) collective-permute-start(f32[72,256]{1,0:T(8,128)S(1)} %get-tuple-element.25), channel_id=1, source_target_pairs={{0,8},{1,9},{2,10},{3,11},{4,12},{5,13},{6,14},{7,15},{8,0},{9,1},... | collective-permute-start | bytes 221192 | tf_op jit(solution)/shard_map/ppermute | solution.py:22
  42.6 0.3 collective-permute-start.7
  43.0 0.4 collective-permute-start.20
  43.4 3.7 %collective-permute-start.21 = (f32[72,256]{1,0:T(8,128)S(1)}, f32[72,256]{1,0:T(8,128)S(1)}, u32[]{:S(2)}, u32[]{:S(2)}) collective-permute-start(f32[72,256]{1,0:T(8,128)S(1)} %get-tuple-element.19), channel_id=1, source_target_pairs={{0,8},{1,9},{2,10},{3,11},{4,12},{5,13},{6,14},{7,15},{8,0},{9,1},... | collective-permute-start | bytes 221192 | tf_op jit(solution)/shard_map/ppermute | solution.py:22
  47.1 0.3 collective-permute-done.6
  47.4 6.1 %collective-permute-start.22 = (f32[72,256]{1,0:T(8,128)S(1)}, f32[72,256]{1,0:T(8,128)S(1)}, u32[]{:S(2)}, u32[]{:S(2)}) collective-permute-start(f32[72,256]{1,0:T(8,128)S(1)} %get-tuple-element.19), channel_id=1, source_target_pairs={{0,12},{1,13},{2,14},{3,15},{4,8},{5,9},{6,10},{7,11},{8,4},{9,5},... | collective-permute-start | bytes 221192 | tf_op jit(solution)/shard_map/ppermute | solution.py:22
  53.5 1.0 %maximum_select_fusion.5 = bf16[512,256]{1,0:T(8,128)(2,1)S(1)} fusion(bf16[256,256]{1,0:T(8,128)(2,1)S(1)} %collective-permute-done.8, bf16[256,256]{1,0:T(8,128)(2,1)} %constant_dynamic-update-slice_fusion.8, pred[]{:T(512)S(6)} %eq.4), kind=kLoop, calls=%fused_computation.9 | loop fusion | flops 1179648 | bytes 524289 | tf_op jit(solution)/shard_map/jit(_where)/select_n | solution.py:43
  54.5 0.1 collective-permute-start.9
  54.6 1.5 %collective-permute-start.10 = (f32[72,256]{1,0:T(8,128)S(1)}, f32[72,256]{1,0:T(8,128)S(1)}, u32[]{:S(2)}, u32[]{:S(2)}) collective-permute-start(f32[72,256]{1,0:T(8,128)S(1)} %add_add_fusion.1), channel_id=1, source_target_pairs={{0,8},{1,9},{2,10},{3,11},{4,12},{5,13},{6,14},{7,15},{8,0},{9,1},... | collective-permute-start | bytes 221192 | tf_op jit(solution)/shard_map/ppermute | solution.py:22
  56.2 2.9 %collective-permute-start.11 = (f32[72,256]{1,0:T(8,128)S(1)}, f32[72,256]{1,0:T(8,128)S(1)}, u32[]{:S(2)}, u32[]{:S(2)}) collective-permute-start(f32[72,256]{1,0:T(8,128)S(1)} %add_add_fusion.1), channel_id=1, source_target_pairs={{0,12},{1,13},{2,14},{3,15},{4,8},{5,9},{6,10},{7,11},{8,4},{9,5},... | collective-permute-start | bytes 221192 | tf_op jit(solution)/shard_map/ppermute | solution.py:22
  59.1 0.1 collective-permute-start.12
  59.3 0.6 collective-permute-start.23
  59.9 0.1 collective-permute-done.10
  59.9 2.5 %collective-permute-done.11 = f32[72,256]{1,0:T(8,128)S(1)} collective-permute-done((f32[72,256]{1,0:T(8,128)S(1)}, f32[72,256]{1,0:T(8,128)S(1)}, u32[]{:S(2)}, u32[]{:S(2)}) %collective-permute-start.11) | collective-permute-done | bytes 73760 | tf_op jit(solution)/shard_map/ppermute | solution.py:22
  62.5 0.2 maximum_select_fusion.4
  62.7 0.6 collective-permute-start.13
  63.3 5.9 %collective-permute-done.23 = f32[288,256]{1,0:T(8,128)S(1)} collective-permute-done((f32[288,256]{1,0:T(8,128)S(1)}, f32[288,256]{1,0:T(8,128)S(1)}, u32[]{:S(2)}, u32[]{:S(2)}) %collective-permute-start.23) | collective-permute-done | bytes 294944 | tf_op jit(solution)/shard_map/ppermute | solution.py:22
  69.2 0.1 collective-permute-start.24
  69.3 5.8 %collective-permute-done.13 = f32[288,256]{1,0:T(8,128)S(1)} collective-permute-done((f32[288,256]{1,0:T(8,128)S(1)}, f32[288,256]{1,0:T(8,128)S(1)}, u32[]{:S(2)}, u32[]{:S(2)}) %collective-permute-start.13) | collective-permute-done | bytes 294944 | tf_op jit(solution)/shard_map/ppermute | solution.py:22
  75.1 0.1 collective-permute-start.14
  75.2 0.1 maximum_select_fusion.1.refs_1_
  75.4 1.8 %collective-permute-done.14 = f32[576,256]{1,0:T(8,128)S(1)} collective-permute-done((f32[576,256]{1,0:T(8,128)S(1)}, f32[576,256]{1,0:T(8,128)S(1)}, u32[]{:S(2)}, u32[]{:S(2)}) %collective-permute-start.14) | collective-permute-done | bytes 589856 | tf_op jit(solution)/shard_map/ppermute | solution.py:22
  77.2 0.1 maximum_select_fusion.refs_0_
  77.3 0.1 copy-done.1
  77.4 22.8 %shard_map.42 = (bf16[2048,256]{1,0:T(8,128)(2,1)}, bf16[64,256]{1,0:T(8,128)(2,1)}) custom-call(s32[1]{0:T(128)} %bitcast.me_ref, bf16[1024,256]{1,0:T(8,128)(2,1)S(1)} %bitcast.5, bf16[2048,1024]{1,0:T(8,128)(2,1)S(1)} %copy-done.1, f32[1152,256]{1,0:T(8,128)S(1)} %maximum_select_fusion.refs_0_, f32[1152,256]{1,0:T(8,128)S(1)} %maximum_select_fusion.1.refs_1_), custom_call_target="tpu_custom_call" | custom-call | tf_op jit(solution)/shard_map/pallas_call | solution.py:306
  (41 shorter events, 0.6 us)
Async XLA Ops:
  0.6 2.2 %copy-start = (bf16[2048,1024]{1,0:T(8,128)(2,1)S(1)}, bf16[2048,1024]{1,0:T(8,128)(2,1)}, u32[]{:S(2)}) copy-start(bf16[2048,1024]{1,0:T(8,128)(2,1)} %a_hbm.3) | copy-start | bytes 12582916
  7.5 13.2 %collective-permute-start.15 = (f32[576,256]{1,0:T(8,128)S(1)}, f32[576,256]{1,0:T(8,128)}, u32[]{:S(2)}, u32[]{:S(2)}) collective-permute-start(f32[576,256]{1,0:T(8,128)S(1)} %constant_dynamic-slice_fusion.4), channel_id=1, source_target_pairs={{0,1},{1,0},{2,3},{3,2},{4,5},{5,4},{6,7},{7,6},{8,9},{9,8},{10,11... | collective-permute-start | bytes 1769480 | tf_op jit(solution)/shard_map/ppermute | solution.py:22
  8.0 7.4 %collective-permute-start.2 = (bf16[64,256]{1,0:T(8,128)(2,1)}, bf16[64,256]{1,0:T(8,128)(2,1)}, u32[]{:S(2)}, u32[]{:S(2)}) collective-permute-start(bf16[64,256]{1,0:T(8,128)(2,1)} %param.3), channel_id=1, source_target_pairs={{0,4},{1,5},{2,6},{3,7},{4,0},{5,1},{6,2},{7,3},{8,12},{9,13},{10,... | collective-permute-start | bytes 98312 | tf_op jit(solution)/shard_map/ppermute | solution.py:22
  10.6 6.1 %collective-permute-start.3 = (bf16[64,256]{1,0:T(8,128)(2,1)}, bf16[64,256]{1,0:T(8,128)(2,1)}, u32[]{:S(2)}, u32[]{:S(2)}) collective-permute-start(bf16[64,256]{1,0:T(8,128)(2,1)} %param.3), channel_id=1, source_target_pairs={{0,8},{1,9},{2,10},{3,11},{4,12},{5,13},{6,14},{7,15},{8,0},{9,1},... | collective-permute-start | bytes 98312 | tf_op jit(solution)/shard_map/ppermute | solution.py:22
  13.2 6.0 %collective-permute-start.4 = (bf16[64,256]{1,0:T(8,128)(2,1)}, bf16[64,256]{1,0:T(8,128)(2,1)}, u32[]{:S(2)}, u32[]{:S(2)}) collective-permute-start(bf16[64,256]{1,0:T(8,128)(2,1)} %param.3), channel_id=1, source_target_pairs={{0,12},{1,13},{2,14},{3,15},{4,8},{5,9},{6,10},{7,11},{8,4},{9,5},... | collective-permute-start | bytes 98312 | tf_op jit(solution)/shard_map/ppermute | solution.py:22
  13.3 10.1 %collective-permute-start = (f32[576,256]{1,0:T(8,128)S(1)}, f32[576,256]{1,0:T(8,128)}, u32[]{:S(2)}, u32[]{:S(2)}) collective-permute-start(f32[576,256]{1,0:T(8,128)S(1)} %constant_dynamic-slice_fusion.9), channel_id=1, source_target_pairs={{0,1},{1,0},{2,3},{3,2},{4,5},{5,4},{6,7},{7,6},{8,9},{9,8},{10,11... | collective-permute-start | bytes 1769480 | tf_op jit(solution)/shard_map/ppermute | solution.py:22
  21.8 10.0 %collective-permute-start.16 = (f32[288,256]{1,0:T(8,128)S(1)}, f32[288,256]{1,0:T(8,128)S(1)}, u32[]{:S(2)}, u32[]{:S(2)}) collective-permute-start(f32[288,256]{1,0:T(8,128)S(1)} %constant_dynamic-slice_fusion.3), channel_id=1, source_target_pairs={{0,2},{1,3},{2,0},{3,1},{4,6},{5,7},{6,4},{7,5},{8,10},{9,11},{10,... | collective-permute-start | bytes 884744 | tf_op jit(solution)/shard_map/ppermute | solution.py:22
  24.6 11.9 %collective-permute-start.1 = (f32[288,256]{1,0:T(8,128)S(1)}, f32[288,256]{1,0:T(8,128)S(1)}, u32[]{:S(2)}, u32[]{:S(2)}) collective-permute-start(f32[288,256]{1,0:T(8,128)S(1)} %constant_dynamic-slice_fusion.8), channel_id=1, source_target_pairs={{0,2},{1,3},{2,0},{3,1},{4,6},{5,7},{6,4},{7,5},{8,10},{9,11},{10,... | collective-permute-start | bytes 884744 | tf_op jit(solution)/shard_map/ppermute | solution.py:22
  31.9 7.2 %collective-permute-start.17 = (f32[72,256]{1,0:T(8,128)S(1)}, f32[72,256]{1,0:T(8,128)S(1)}, u32[]{:S(2)}, u32[]{:S(2)}) collective-permute-start(f32[72,256]{1,0:T(8,128)S(1)} %get-tuple-element.20), channel_id=1, source_target_pairs={{0,4},{1,5},{2,6},{3,7},{4,0},{5,1},{6,2},{7,3},{8,12},{9,13},{10,... | collective-permute-start | bytes 221192 | tf_op jit(solution)/shard_map/ppermute | solution.py:22
  32.0 10.6 %collective-permute-start.18 = (f32[72,256]{1,0:T(8,128)S(1)}, f32[72,256]{1,0:T(8,128)S(1)}, u32[]{:S(2)}, u32[]{:S(2)}) collective-permute-start(f32[72,256]{1,0:T(8,128)S(1)} %get-tuple-element.22), channel_id=1, source_target_pairs={{0,8},{1,9},{2,10},{3,11},{4,12},{5,13},{6,14},{7,15},{8,0},{9,1},... | collective-permute-start | bytes 221192 | tf_op jit(solution)/shard_map/ppermute | solution.py:22
  35.1 7.8 %collective-permute-start.19 = (f32[72,256]{1,0:T(8,128)S(1)}, f32[72,256]{1,0:T(8,128)S(1)}, u32[]{:S(2)}, u32[]{:S(2)}) collective-permute-start(f32[72,256]{1,0:T(8,128)S(1)} %get-tuple-element.21), channel_id=1, source_target_pairs={{0,12},{1,13},{2,14},{3,15},{4,8},{5,9},{6,10},{7,11},{8,4},{9,5},... | collective-permute-start | bytes 221192 | tf_op jit(solution)/shard_map/ppermute | solution.py:22
  36.5 16.9 %collective-permute-start.8 = (bf16[256,256]{1,0:T(8,128)(2,1)}, bf16[256,256]{1,0:T(8,128)(2,1)S(1)}, u32[]{:S(2)}, u32[]{:S(2)}) collective-permute-start(bf16[256,256]{1,0:T(8,128)(2,1)} %constant_dynamic-update-slice_fusion.8), channel_id=1, source_target_pairs={{0,2},{1,3},{2,0},{3,1},{4,6},{5,7},{6,4},{7,5},{8,10},{9,11},{10,... | collective-permute-start | bytes 393224 | tf_op jit(solution)/shard_map/ppermute | solution.py:22
  38.4 5.0 %collective-permute-start.5 = (f32[72,256]{1,0:T(8,128)S(1)}, f32[72,256]{1,0:T(8,128)S(1)}, u32[]{:S(2)}, u32[]{:S(2)}) collective-permute-start(f32[72,256]{1,0:T(8,128)S(1)} %get-tuple-element.23), channel_id=1, source_target_pairs={{0,4},{1,5},{2,6},{3,7},{4,0},{5,1},{6,2},{7,3},{8,12},{9,13},{10,... | collective-permute-start | bytes 221192 | tf_op jit(solution)/shard_map/ppermute | solution.py:22
  39.1 8.3 %collective-permute-start.6 = (f32[72,256]{1,0:T(8,128)S(1)}, f32[72,256]{1,0:T(8,128)S(1)}, u32[]{:S(2)}, u32[]{:S(2)}) collective-permute-start(f32[72,256]{1,0:T(8,128)S(1)} %get-tuple-element.25), channel_id=1, source_target_pairs={{0,8},{1,9},{2,10},{3,11},{4,12},{5,13},{6,14},{7,15},{8,0},{9,1},... | collective-permute-start | bytes 221192 | tf_op jit(solution)/shard_map/ppermute | solution.py:22
  42.6 10.8 %collective-permute-start.7 = (f32[72,256]{1,0:T(8,128)S(1)}, f32[72,256]{1,0:T(8,128)S(1)}, u32[]{:S(2)}, u32[]{:S(2)}) collective-permute-start(f32[72,256]{1,0:T(8,128)S(1)} %get-tuple-element.24), channel_id=1, source_target_pairs={{0,12},{1,13},{2,14},{3,15},{4,8},{5,9},{6,10},{7,11},{8,4},{9,5},... | collective-permute-start | bytes 221192 | tf_op jit(solution)/shard_map/ppermute | solution.py:22
  43.0 13.2 %collective-permute-start.20 = (f32[72,256]{1,0:T(8,128)S(1)}, f32[72,256]{1,0:T(8,128)S(1)}, u32[]{:S(2)}, u32[]{:S(2)}) collective-permute-start(f32[72,256]{1,0:T(8,128)S(1)} %get-tuple-element.19), channel_id=1, source_target_pairs={{0,4},{1,5},{2,6},{3,7},{4,0},{5,1},{6,2},{7,3},{8,12},{9,13},{10,... | collective-permute-start | bytes 221192 | tf_op jit(solution)/shard_map/ppermute | solution.py:22
  43.4 15.7 %collective-permute-start.21 = (f32[72,256]{1,0:T(8,128)S(1)}, f32[72,256]{1,0:T(8,128)S(1)}, u32[]{:S(2)}, u32[]{:S(2)}) collective-permute-start(f32[72,256]{1,0:T(8,128)S(1)} %get-tuple-element.19), channel_id=1, source_target_pairs={{0,8},{1,9},{2,10},{3,11},{4,12},{5,13},{6,14},{7,15},{8,0},{9,1},... | collective-permute-start | bytes 221192 | tf_op jit(solution)/shard_map/ppermute | solution.py:22
  47.4 11.8 %collective-permute-start.22 = (f32[72,256]{1,0:T(8,128)S(1)}, f32[72,256]{1,0:T(8,128)S(1)}, u32[]{:S(2)}, u32[]{:S(2)}) collective-permute-start(f32[72,256]{1,0:T(8,128)S(1)} %get-tuple-element.19), channel_id=1, source_target_pairs={{0,12},{1,13},{2,14},{3,15},{4,8},{5,9},{6,10},{7,11},{8,4},{9,5},... | collective-permute-start | bytes 221192 | tf_op jit(solution)/shard_map/ppermute | solution.py:22
  54.5 5.3 %collective-permute-start.9 = (f32[72,256]{1,0:T(8,128)S(1)}, f32[72,256]{1,0:T(8,128)S(1)}, u32[]{:S(2)}, u32[]{:S(2)}) collective-permute-start(f32[72,256]{1,0:T(8,128)S(1)} %add_add_fusion.1), channel_id=1, source_target_pairs={{0,4},{1,5},{2,6},{3,7},{4,0},{5,1},{6,2},{7,3},{8,12},{9,13},{10,... | collective-permute-start | bytes 221192 | tf_op jit(solution)/shard_map/ppermute | solution.py:22
  54.6 5.3 %collective-permute-start.10 = (f32[72,256]{1,0:T(8,128)S(1)}, f32[72,256]{1,0:T(8,128)S(1)}, u32[]{:S(2)}, u32[]{:S(2)}) collective-permute-start(f32[72,256]{1,0:T(8,128)S(1)} %add_add_fusion.1), channel_id=1, source_target_pairs={{0,8},{1,9},{2,10},{3,11},{4,12},{5,13},{6,14},{7,15},{8,0},{9,1},... | collective-permute-start | bytes 221192 | tf_op jit(solution)/shard_map/ppermute | solution.py:22
  56.2 6.3 %collective-permute-start.11 = (f32[72,256]{1,0:T(8,128)S(1)}, f32[72,256]{1,0:T(8,128)S(1)}, u32[]{:S(2)}, u32[]{:S(2)}) collective-permute-start(f32[72,256]{1,0:T(8,128)S(1)} %add_add_fusion.1), channel_id=1, source_target_pairs={{0,12},{1,13},{2,14},{3,15},{4,8},{5,9},{6,10},{7,11},{8,4},{9,5},... | collective-permute-start | bytes 221192 | tf_op jit(solution)/shard_map/ppermute | solution.py:22
  59.1 3.3 %collective-permute-start.12 = (bf16[512,256]{1,0:T(8,128)(2,1)S(1)}, bf16[512,256]{1,0:T(8,128)(2,1)S(1)}, u32[]{:S(2)}, u32[]{:S(2)}) collective-permute-start(bf16[512,256]{1,0:T(8,128)(2,1)S(1)} %maximum_select_fusion.5), channel_id=1, source_target_pairs={{0,1},{1,0},{2,3},{3,2},{4,5},{5,4},{6,7},{7,6},{8,9},{9,8},{10,11... | collective-permute-start | bytes 786440 | tf_op jit(solution)/shard_map/ppermute | solution.py:22
  59.3 9.9 %collective-permute-start.23 = (f32[288,256]{1,0:T(8,128)S(1)}, f32[288,256]{1,0:T(8,128)S(1)}, u32[]{:S(2)}, u32[]{:S(2)}) collective-permute-start(f32[288,256]{1,0:T(8,128)S(1)} %constant_dynamic-update-slice_fusion), channel_id=1, source_target_pairs={{0,2},{1,3},{2,0},{3,1},{4,6},{5,7},{6,4},{7,5},{8,10},{9,11},{10,... | collective-permute-start | bytes 884744 | tf_op jit(solution)/shard_map/ppermute | solution.py:22
  62.7 12.3 %collective-permute-start.13 = (f32[288,256]{1,0:T(8,128)S(1)}, f32[288,256]{1,0:T(8,128)S(1)}, u32[]{:S(2)}, u32[]{:S(2)}) collective-permute-start(f32[288,256]{1,0:T(8,128)S(1)} %constant_dynamic-update-slice_fusion.4), channel_id=1, source_target_pairs={{0,2},{1,3},{2,0},{3,1},{4,6},{5,7},{6,4},{7,5},{8,10},{9,11},{10,... | collective-permute-start | bytes 884744 | tf_op jit(solution)/shard_map/ppermute | solution.py:22
  69.2 6.0 %collective-permute-start.24 = (f32[576,256]{1,0:T(8,128)S(1)}, f32[576,256]{1,0:T(8,128)S(1)}, u32[]{:S(2)}, u32[]{:S(2)}) collective-permute-start(f32[576,256]{1,0:T(8,128)S(1)} %maximum_select_fusion.3), channel_id=1, source_target_pairs={{0,1},{1,0},{2,3},{3,2},{4,5},{5,4},{6,7},{7,6},{8,9},{9,8},{10,11... | collective-permute-start | bytes 1769480 | tf_op jit(solution)/shard_map/ppermute | solution.py:22
  75.1 2.1 %collective-permute-start.14 = (f32[576,256]{1,0:T(8,128)S(1)}, f32[576,256]{1,0:T(8,128)S(1)}, u32[]{:S(2)}, u32[]{:S(2)}) collective-permute-start(f32[576,256]{1,0:T(8,128)S(1)} %maximum_select_fusion.2), channel_id=1, source_target_pairs={{0,1},{1,0},{2,3},{3,2},{4,5},{5,4},{6,7},{7,6},{8,9},{9,8},{10,11... | collective-permute-start | bytes 1769480 | tf_op jit(solution)/shard_map/ppermute | solution.py:22
  75.2 2.2 %copy-start.1 = (bf16[2048,1024]{1,0:T(8,128)(2,1)S(1)}, bf16[2048,1024]{1,0:T(8,128)(2,1)}, u32[]{:S(2)}) copy-start(bf16[2048,1024]{1,0:T(8,128)(2,1)} %a_hbm.3) | copy-start | bytes 12582916

commit v4 on v2

--- a/solution.py
+++ b/solution.py
@@ -50,21 +50,31 @@
 
 def stages():
     n = lax.axis_size(AXIS)
-    return [(0, 2), (1, 2), (2, n // 4)]
-
-
-def sum_everywhere(value):
-    for low, count in stages():
-        value = scatter_stage(value, low, count)
-    for low, count in reversed(stages()):
-        value = gather_stage(value, low, count)
-    return value
-
-
-def gather_rows(value):
-    for low, count in stages():
-        value = gather_stage(value, low, count)
-    return value
+    return [(0, 2), (1, 4), (3, n // 8)]
+
+
+def tie(value, other):
+    return lax.optimization_barrier((value, other))
+
+
+def widen(rows, low, count):
+    return jnp.concatenate([rows] + [exchange(rows, k << low) for k in range(1, count)])
+
+
+def sum_everywhere(parts, rows):
+    core, square, far = stages()
+    parts = [scatter_stage(p, *core) for p in parts]
+    rows = widen(rows, *far)
+    parts = [scatter_stage(p, *square) for p in parts]
+    parts[0], rows = tie(parts[0], rows)
+    parts = [scatter_stage(p, *far) for p in parts]
+    rows = widen(rows, *square)
+    parts = [gather_stage(p, *far) for p in parts]
+    parts[0], rows = tie(parts[0], rows)
+    rows = widen(rows, *core)
+    parts = [gather_stage(p, *square) for p in parts]
+    parts = [gather_stage(p, *core) for p in parts]
+    return parts, rows
 
 
 def layout(time_steps):
@@ -106,10 +116,11 @@
                 out[row : row + EDGE, :] = block
                 row += EDGE
             else:
+                cut = HALF + HALF // 2
                 out[row : row + HALF, :HALF] = block[:HALF, :HALF]
                 out[row : row + HALF, HALF:] = block[HALF:, HALF:]
-                out[row + HALF : row + HALF + HALF // 2, :HALF] = block[HALF : HALF + HALF // 2, :HALF]
-                out[row + HALF : row + HALF + HALF // 2, HALF:] = block[HALF + HALF // 2 :, :HALF]
+                out[row + HALF : row + cut, :HALF] = block[HALF:cut, :HALF]
+                out[row + HALF : row + cut, HALF:] = block[cut:, :HALF]
                 row += EDGE * 3 // 4
 
 
@@ -207,9 +218,20 @@
     chain_refs, refs = refs[: len(chains)], refs[len(chains) :]
     range_ref, coef_ref, moment, a_ref, power, y_ref, back_ref, x_ref, w_ref, sem = refs
     time_steps, rank = sketch_ref.shape
+    steps = coef_ref.shape[0]
     nb = time_steps // EDGE
     fetch = pltpu.make_async_copy(a_hbm, a_ref, sem)
     fetch.start()
+
+    devices = time_steps // steps
+    for k in range(devices):
+        others = devices // 8
+        away = k % others * 8 + k // others % 4 * 2 + k // others // 4
+        block = sketch_ref[k * steps : (k + 1) * steps, :].astype(F32)
+        spot = lax.bitwise_xor(me_ref[0], jnp.int32(away)) * steps
+        y_ref[pl.ds(pl.multiple_of(spot, steps), steps), :] = block
+    sketch_ref = back_ref
+    sketch_ref[...] = y_ref[...].astype(BF16)
 
     def store(i, j, block):
         for p, part in enumerate(three(block)):
@@ -251,7 +273,6 @@
     for k in range(panels):
         band = slice(k * share, (k + 1) * share)
         range_ref[band, :] = product(power[band, :], w_ref[...], ((1,), (1,)), high).astype(BF16)
-    steps = coef_ref.shape[0]
     mine = y_ref[pl.ds(pl.multiple_of(me_ref[0] * steps, steps), steps), :]
     coef_ref[...] = (product(mine, w_ref[...], ((1,), (1,)), high) * factor).astype(BF16)
 
@@ -266,7 +287,6 @@
     chains = layout(time_steps)
     vmem = pl.BlockSpec(memory_space=pltpu.VMEM)
 
-    sketch_all = gather_rows(sketch_matrix)
     partial = pl.pallas_call(
         functools.partial(moment_kernel, chains),
         out_shape=[jax.ShapeDtypeStruct((chain_rows(c), EDGE), F32) for c in chains],
@@ -274,7 +294,7 @@
         out_specs=[vmem] * len(chains),
         compiler_params=pltpu.CompilerParams(vmem_limit_bytes=20 << 20),
     )(series_data)
-    summed = [sum_everywhere(p) for p in partial]
+    summed, sketch_all = sum_everywhere(list(partial), sketch_matrix)
     me = lax.axis_index(AXIS).astype(jnp.int32).reshape(1)
     return tuple(
         pl.pallas_call(
@@ -286,7 +306,7 @@
             in_specs=[
                 pl.BlockSpec(memory_space=pltpu.SMEM),
                 vmem,
-                pl.BlockSpec(memory_space=pl.ANY),
+                pl.BlockSpec(memory_space=pltpu.HBM),
             ]
             + [vmem] * len(chains),
             out_specs=[vmem, vmem],

time: 96.9 us -> 85.7 us (0.88)
  waiting for transfers between devices: 28.5 us -> 18.7 us
  local copies, waits for them, and re-layouts: 4.52 us -> 2.73 us
    ppermute x25, waiting for transfers between devices: 28.5 us -> 18.7 us  [exchange(): return lax.ppermute(value, AXIS, [(i, i ^ distance) for i in range(n)])]
    unnamed x4, local copies, waits for them, and re-layouts: 4.15 us -> 2.36 us
    add x4 -> x6, other arithmetic: 2.36 us -> 2.38 us  [scatter_stage(): total = total + item]
  transfers between devices with their start and end apart: 25 -> 25, of which waited for: 11 -> 10; matrix products, arithmetic and copies ran while one was open for 4% -> 4% of each run, Pallas kernels for 0% -> 0%
where the time goes in v4:
time: 85.7 us; the launch traced here: 85.3 us
  starting transfers between devices  33.7 us (39%)
  Pallas kernels  25.7 us (30%)
  waiting for transfers between devices  18.7 us (22%)
  other arithmetic  3.44 us (4%)
  local copies, waits for them, and re-layouts  2.73 us (3%)
  between operations  1.09 us (1%)
    ppermute x25, starting transfers between devices, exchange(): return lax.ppermute(value, AXIS, [(i, i ^ distance) for i in range(n)])  33.7 us
    pallas_call x1, Pallas kernels, body(): pl.pallas_call(functools.partial(finish_kernel, chains, rows_total, facto...  22.8 us
    ppermute x25, waiting for transfers between devices, exchange(): return lax.ppermute(value, AXIS, [(i, i ^ distance) for i in range(n)])  18.7 us
    pallas_call x1, Pallas kernels, body(): pl.pallas_call(functools.partial(moment_kernel, chains), out_shape=[jax.S...  2.94 us
    add x6, other arithmetic, scatter_stage(): total = total + item  2.38 us
    unnamed x4, local copies, waits for them, and re-layouts  2.36 us
  transfers between devices with their start and end apart: 25, of which 10 were waited for; matrix products, arithmetic and copies ran while one was open for 4% of the time, Pallas kernels for 0%

profile of v4, /device:TPU:0, one launch (start us, length us, event | category | flops | bytes accessed | tf_op | source)
XLA Modules:
  0.0 85.3 jit_solution(4501678867608052501)
XLA Ops:
  0.6 0.0 copy-start
  0.7 2.2 %copy-done = bf16[2048,1024]{1,0:T(8,128)(2,1)S(1)} copy-done((bf16[2048,1024]{1,0:T(8,128)(2,1)S(1)}, bf16[2048,1024]{1,0:T(8,128)(2,1)}, u32[]{:S(2)}) %copy-start) | copy-done | bytes 4194328
  2.8 2.9 %shard_map.41 = (f32[1152,256]{1,0:T(8,128)S(1)}, f32[1152,256]{1,0:T(8,128)S(1)}) custom-call(bf16[2048,1024]{1,0:T(8,128)(2,1)S(1)} %copy-done), custom_call_target="tpu_custom_call" | custom-call | tf_op jit(solution)/shard_map/pallas_call | solution.py:290
  5.8 0.5 collective-permute-start
  6.4 0.1 collective-permute-start.15
  6.5 4.0 %collective-permute-start.4 = (bf16[64,256]{1,0:T(8,128)(2,1)}, bf16[64,256]{1,0:T(8,128)(2,1)}, u32[]{:S(2)}, u32[]{:S(2)}) collective-permute-start(bf16[64,256]{1,0:T(8,128)(2,1)} %param.3), channel_id=1, source_target_pairs={{0,8},{1,9},{2,10},{3,11},{4,12},{5,13},{6,14},{7,15},{8,0},{9,1},... | collective-permute-start | bytes 98312 | tf_op jit(solution)/shard_map/ppermute | solution.py:22
  10.6 2.2 %collective-permute-done.4 = bf16[64,256]{1,0:T(8,128)(2,1)} collective-permute-done((bf16[64,256]{1,0:T(8,128)(2,1)}, bf16[64,256]{1,0:T(8,128)(2,1)}, u32[]{:S(2)}, u32[]{:S(2)}) %collective-permute-start.4) | collective-permute-done | bytes 32800 | tf_op jit(solution)/shard_map/ppermute | solution.py:22
  12.8 0.8 pad_maximum_fusion.2
  13.5 0.0 collective-permute-done
  13.5 1.1 %dynamic-slice_add_fusion.1 = f32[576,256]{1,0:T(8,128)S(1)} fusion(f32[576,256]{1,0:T(8,128)} %collective-permute-done, f32[1152,256]{1,0:T(8,128)S(1)} %get-tuple-element.8, s32[]{:T(128)S(6)} %select_n.65), kind=kLoop, calls=%fused_computation.3 | loop fusion | flops 147456 | bytes 1769476 | tf_op jit(solution)/shard_map/add | solution.py:35
  14.7 2.3 %collective-permute-start.1 = (f32[144,256]{1,0:T(8,128)S(1)}, f32[144,256]{1,0:T(8,128)S(1)}, u32[]{:S(2)}, u32[]{:S(2)}) collective-permute-start(f32[144,256]{1,0:T(8,128)S(1)} %get-tuple-element.19), channel_id=1, source_target_pairs={{0,2},{1,3},{2,0},{3,1},{4,6},{5,7},{6,4},{7,5},{8,10},{9,11},{10,... | collective-permute-start | bytes 442376 | tf_op jit(solution)/shard_map/ppermute | solution.py:22
  17.0 1.2 %collective-permute-start.2 = (f32[144,256]{1,0:T(8,128)S(1)}, f32[144,256]{1,0:T(8,128)S(1)}, u32[]{:S(2)}, u32[]{:S(2)}) collective-permute-start(f32[144,256]{1,0:T(8,128)S(1)} %get-tuple-element.21), channel_id=1, source_target_pairs={{0,4},{1,5},{2,6},{3,7},{4,0},{5,1},{6,2},{7,3},{8,12},{9,13},{10,... | collective-permute-start | bytes 442376 | tf_op jit(solution)/shard_map/ppermute | solution.py:22
  18.2 0.3 collective-permute-start.3
  18.6 1.1 %dynamic-slice_add_fusion = f32[576,256]{1,0:T(8,128)S(1)} fusion(f32[576,256]{1,0:T(8,128)} %collective-permute-done.15, f32[1152,256]{1,0:T(8,128)S(1)} %get-tuple-element.13, s32[]{:T(128)S(6)} %select_n.65), kind=kLoop, calls=%fused_computation.2 | loop fusion | flops 147456 | bytes 1769476 | tf_op jit(solution)/shard_map/add | solution.py:35
  19.7 2.0 %collective-permute-start.16 = (f32[144,256]{1,0:T(8,128)S(1)}, f32[144,256]{1,0:T(8,128)S(1)}, u32[]{:S(2)}, u32[]{:S(2)}) collective-permute-start(f32[144,256]{1,0:T(8,128)S(1)} %get-tuple-element.16), channel_id=1, source_target_pairs={{0,2},{1,3},{2,0},{3,1},{4,6},{5,7},{6,4},{7,5},{8,10},{9,11},{10,... | collective-permute-start | bytes 442376 | tf_op jit(solution)/shard_map/ppermute | solution.py:22
  21.8 1.2 %collective-permute-start.17 = (f32[144,256]{1,0:T(8,128)S(1)}, f32[144,256]{1,0:T(8,128)S(1)}, u32[]{:S(2)}, u32[]{:S(2)}) collective-permute-start(f32[144,256]{1,0:T(8,128)S(1)} %get-tuple-element.18), channel_id=1, source_target_pairs={{0,4},{1,5},{2,6},{3,7},{4,0},{5,1},{6,2},{7,3},{8,12},{9,13},{10,... | collective-permute-start | bytes 442376 | tf_op jit(solution)/shard_map/ppermute | solution.py:22
  23.0 0.0 collective-permute-done.1
  23.0 1.9 %collective-permute-start.18 = (f32[144,256]{1,0:T(8,128)S(1)}, f32[144,256]{1,0:T(8,128)S(1)}, u32[]{:S(2)}, u32[]{:S(2)}) collective-permute-start(f32[144,256]{1,0:T(8,128)S(1)} %get-tuple-element.17), channel_id=1, source_target_pairs={{0,6},{1,7},{2,4},{3,5},{4,2},{5,3},{6,0},{7,1},{8,14},{9,15},{10,... | collective-permute-start | bytes 442376 | tf_op jit(solution)/shard_map/ppermute | solution.py:22
  24.9 0.0 collective-permute-done.2
  24.9 1.4 %collective-permute-done.3 = f32[144,256]{1,0:T(8,128)S(1)} collective-permute-done((f32[144,256]{1,0:T(8,128)S(1)}, f32[144,256]{1,0:T(8,128)S(1)}, u32[]{:S(2)}, u32[]{:S(2)}) %collective-permute-start.3) | collective-permute-done | bytes 147488 | tf_op jit(solution)/shard_map/ppermute | solution.py:22
  26.3 2.0 %collective-permute-start.7 = (bf16[128,256]{1,0:T(8,128)(2,1)S(1)}, bf16[128,256]{1,0:T(8,128)(2,1)S(1)}, u32[]{:S(2)}, u32[]{:S(2)}) collective-permute-start(bf16[128,256]{1,0:T(8,128)(2,1)S(1)} %pad_maximum_fusion.2), channel_id=1, source_target_pairs={{0,2},{1,3},{2,0},{3,1},{4,6},{5,7},{6,4},{7,5},{8,10},{9,11},{10,... | collective-permute-start | bytes 196616 | tf_op jit(solution)/shard_map/ppermute | solution.py:22
  28.4 1.5 %collective-permute-start.8 = (bf16[128,256]{1,0:T(8,128)(2,1)S(1)}, bf16[128,256]{1,0:T(8,128)(2,1)S(1)}, u32[]{:S(2)}, u32[]{:S(2)}) collective-permute-start(bf16[128,256]{1,0:T(8,128)(2,1)S(1)} %pad_maximum_fusion.2), channel_id=1, source_target_pairs={{0,4},{1,5},{2,6},{3,7},{4,0},{5,1},{6,2},{7,3},{8,12},{9,13},{10,... | collective-permute-start | bytes 196616 | tf_op jit(solution)/shard_map/ppermute | solution.py:22
  29.9 1.6 %collective-permute-start.9 = (bf16[128,256]{1,0:T(8,128)(2,1)S(1)}, bf16[128,256]{1,0:T(8,128)(2,1)S(1)}, u32[]{:S(2)}, u32[]{:S(2)}) collective-permute-start(bf16[128,256]{1,0:T(8,128)(2,1)S(1)} %pad_maximum_fusion.2), channel_id=1, source_target_pairs={{0,6},{1,7},{2,4},{3,5},{4,2},{5,3},{6,0},{7,1},{8,14},{9,15},{10,... | collective-permute-start | bytes 196616 | tf_op jit(solution)/shard_map/ppermute | solution.py:22
  31.4 1.2 %collective-permute-done.18 = f32[144,256]{1,0:T(8,128)S(1)} collective-permute-done((f32[144,256]{1,0:T(8,128)S(1)}, f32[144,256]{1,0:T(8,128)S(1)}, u32[]{:S(2)}, u32[]{:S(2)}) %collective-permute-start.18) | collective-permute-done | bytes 147488 | tf_op jit(solution)/shard_map/ppermute | solution.py:22
  32.7 3.0 %collective-permute-start.19 = (f32[72,256]{1,0:T(8,128)S(1)}, f32[72,256]{1,0:T(8,128)S(1)}, u32[]{:S(2)}, u32[]{:S(2)}) collective-permute-start(f32[72,256]{1,0:T(8,128)S(1)} %constant_dynamic-slice_fusion), channel_id=1, source_target_pairs={{0,8},{1,9},{2,10},{3,11},{4,12},{5,13},{6,14},{7,15},{8,0},{9,1},... | collective-permute-start | bytes 221192 | tf_op jit(solution)/shard_map/ppermute | solution.py:22
  35.7 0.1 collective-permute-start.5
  35.8 4.0 %collective-permute-done.19 = f32[72,256]{1,0:T(8,128)S(1)} collective-permute-done((f32[72,256]{1,0:T(8,128)S(1)}, f32[72,256]{1,0:T(8,128)S(1)}, u32[]{:S(2)}, u32[]{:S(2)}) %collective-permute-start.19) | collective-permute-done | bytes 73760 | tf_op jit(solution)/shard_map/ppermute | solution.py:22
  39.8 1.3 %collective-permute-start.20 = (f32[72,256]{1,0:T(8,128)S(1)}, f32[72,256]{1,0:T(8,128)S(1)}, u32[]{:S(2)}, u32[]{:S(2)}) collective-permute-start(f32[72,256]{1,0:T(8,128)S(1)} %dynamic-slice_add_fusion.2), channel_id=1, source_target_pairs={{0,8},{1,9},{2,10},{3,11},{4,12},{5,13},{6,14},{7,15},{8,0},{9,1},... | collective-permute-start | bytes 221192 | tf_op jit(solution)/shard_map/ppermute | solution.py:22
  41.1 2.3 %collective-permute-done.5 = f32[72,256]{1,0:T(8,128)S(1)} collective-permute-done((f32[72,256]{1,0:T(8,128)S(1)}, f32[72,256]{1,0:T(8,128)S(1)}, u32[]{:S(2)}, u32[]{:S(2)}) %collective-permute-start.5) | collective-permute-done | bytes 73760 | tf_op jit(solution)/shard_map/ppermute | solution.py:22
  43.4 0.1 collective-permute-start.6
  43.4 1.7 %collective-permute-done.20 = f32[72,256]{1,0:T(8,128)S(1)} collective-permute-done((f32[72,256]{1,0:T(8,128)S(1)}, f32[72,256]{1,0:T(8,128)S(1)}, u32[]{:S(2)}, u32[]{:S(2)}) %collective-permute-start.20) | collective-permute-done | bytes 73760 | tf_op jit(solution)/shard_map/ppermute | solution.py:22
  45.2 0.9 %collective-permute-start.21 = (f32[144,256]{1,0:T(8,128)S(1)}, f32[144,256]{1,0:T(8,128)S(1)}, u32[]{:S(2)}, u32[]{:S(2)}) collective-permute-start(f32[144,256]{1,0:T(8,128)S(1)} %get-tuple-element.15), channel_id=1, source_target_pairs={{0,2},{1,3},{2,0},{3,1},{4,6},{5,7},{6,4},{7,5},{8,10},{9,11},{10,... | collective-permute-start | bytes 442376 | tf_op jit(solution)/shard_map/ppermute | solution.py:22
  46.1 4.2 %collective-permute-start.22 = (f32[144,256]{1,0:T(8,128)S(1)}, f32[144,256]{1,0:T(8,128)S(1)}, u32[]{:S(2)}, u32[]{:S(2)}) collective-permute-start(f32[144,256]{1,0:T(8,128)S(1)} %get-tuple-element.15), channel_id=1, source_target_pairs={{0,4},{1,5},{2,6},{3,7},{4,0},{5,1},{6,2},{7,3},{8,12},{9,13},{10,... | collective-permute-start | bytes 442376 | tf_op jit(solution)/shard_map/ppermute | solution.py:22
  50.3 1.5 %collective-permute-start.11 = (f32[144,256]{1,0:T(8,128)S(1)}, f32[144,256]{1,0:T(8,128)S(1)}, u32[]{:S(2)}, u32[]{:S(2)}) collective-permute-start(f32[144,256]{1,0:T(8,128)S(1)} %maximum_select_fusion.2), channel_id=1, source_target_pairs={{0,2},{1,3},{2,0},{3,1},{4,6},{5,7},{6,4},{7,5},{8,10},{9,11},{10,... | collective-permute-start | bytes 442376 | tf_op jit(solution)/shard_map/ppermute | solution.py:22
  51.8 2.0 %collective-permute-start.12 = (f32[144,256]{1,0:T(8,128)S(1)}, f32[144,256]{1,0:T(8,128)S(1)}, u32[]{:S(2)}, u32[]{:S(2)}) collective-permute-start(f32[144,256]{1,0:T(8,128)S(1)} %maximum_select_fusion.2), channel_id=1, source_target_pairs={{0,4},{1,5},{2,6},{3,7},{4,0},{5,1},{6,2},{7,3},{8,12},{9,13},{10,... | collective-permute-start | bytes 442376 | tf_op jit(solution)/shard_map/ppermute | solution.py:22
  53.9 1.7 %collective-permute-start.13 = (f32[144,256]{1,0:T(8,128)S(1)}, f32[144,256]{1,0:T(8,128)S(1)}, u32[]{:S(2)}, u32[]{:S(2)}) collective-permute-start(f32[144,256]{1,0:T(8,128)S(1)} %maximum_select_fusion.2), channel_id=1, source_target_pairs={{0,6},{1,7},{2,4},{3,5},{4,2},{5,3},{6,0},{7,1},{8,14},{9,15},{10,... | collective-permute-start | bytes 442376 | tf_op jit(solution)/shard_map/ppermute | solution.py:22
  55.7 0.1 collective-permute-start.10
  55.8 0.8 collective-permute-done.23
  56.6 0.1 collective-permute-start.24
  56.7 1.1 %collective-permute-done.11 = f32[144,256]{1,0:T(8,128)S(1)} collective-permute-done((f32[144,256]{1,0:T(8,128)S(1)}, f32[144,256]{1,0:T(8,128)S(1)}, u32[]{:S(2)}, u32[]{:S(2)}) %collective-permute-start.11) | collective-permute-done | bytes 147488 | tf_op jit(solution)/shard_map/ppermute | solution.py:22
  57.8 2.2 %collective-permute-done.13 = f32[144,256]{1,0:T(8,128)S(1)} collective-permute-done((f32[144,256]{1,0:T(8,128)S(1)}, f32[144,256]{1,0:T(8,128)S(1)}, u32[]{:S(2)}, u32[]{:S(2)}) %collective-permute-start.13) | collective-permute-done | bytes 147488 | tf_op jit(solution)/shard_map/ppermute | solution.py:22
  60.1 0.1 collective-permute-start.14
  60.2 0.0 copy-start.1
  60.2 0.1 maximum_select_fusion.1.refs_1_
  60.3 1.8 %collective-permute-done.14 = f32[576,256]{1,0:T(8,128)S(1)} collective-permute-done((f32[576,256]{1,0:T(8,128)S(1)}, f32[576,256]{1,0:T(8,128)S(1)}, u32[]{:S(2)}, u32[]{:S(2)}) %collective-permute-start.14) | collective-permute-done | bytes 589856 | tf_op jit(solution)/shard_map/ppermute | solution.py:22
  62.1 0.1 maximum_select_fusion.refs_0_
  62.2 0.2 copy-done.1
  62.4 22.8 %shard_map.42 = (bf16[2048,256]{1,0:T(8,128)(2,1)}, bf16[64,256]{1,0:T(8,128)(2,1)}) custom-call(s32[1]{0:T(128)} %bitcast.me_ref, bf16[1024,256]{1,0:T(8,128)(2,1)S(1)} %pad_maximum_fusion.sketch_ref, bf16[2048,1024]{1,0:T(8,128)(2,1)S(1)} %copy-done.1, f32[1152,256]{1,0:T(8,128)S(1)} %maximum_select_fusion.refs_0_, ...), custom_call_target="tpu_custom_call" | custom-call | tf_op jit(solution)/shard_map/pallas_call | solution.py:300
  (36 shorter events, 0.6 us)
Async XLA Ops:
  0.6 2.2 %copy-start = (bf16[2048,1024]{1,0:T(8,128)(2,1)S(1)}, bf16[2048,1024]{1,0:T(8,128)(2,1)}, u32[]{:S(2)}) copy-start(bf16[2048,1024]{1,0:T(8,128)(2,1)} %a_hbm.1) | copy-start | bytes 12582916
  5.8 7.7 %collective-permute-start = (f32[576,256]{1,0:T(8,128)S(1)}, f32[576,256]{1,0:T(8,128)}, u32[]{:S(2)}, u32[]{:S(2)}) collective-permute-start(f32[576,256]{1,0:T(8,128)S(1)} %constant_dynamic-slice_fusion.9), channel_id=1, source_target_pairs={{0,1},{1,0},{2,3},{3,2},{4,5},{5,4},{6,7},{7,6},{8,9},{9,8},{10,11... | collective-permute-start | bytes 1769480 | tf_op jit(solution)/shard_map/ppermute | solution.py:22
  6.4 12.2 %collective-permute-start.15 = (f32[576,256]{1,0:T(8,128)S(1)}, f32[576,256]{1,0:T(8,128)}, u32[]{:S(2)}, u32[]{:S(2)}) collective-permute-start(f32[576,256]{1,0:T(8,128)S(1)} %constant_dynamic-slice_fusion.4), channel_id=1, source_target_pairs={{0,1},{1,0},{2,3},{3,2},{4,5},{5,4},{6,7},{7,6},{8,9},{9,8},{10,11... | collective-permute-start | bytes 1769480 | tf_op jit(solution)/shard_map/ppermute | solution.py:22
  6.5 6.2 %collective-permute-start.4 = (bf16[64,256]{1,0:T(8,128)(2,1)}, bf16[64,256]{1,0:T(8,128)(2,1)}, u32[]{:S(2)}, u32[]{:S(2)}) collective-permute-start(bf16[64,256]{1,0:T(8,128)(2,1)} %param.3), channel_id=1, source_target_pairs={{0,8},{1,9},{2,10},{3,11},{4,12},{5,13},{6,14},{7,15},{8,0},{9,1},... | collective-permute-start | bytes 98312 | tf_op jit(solution)/shard_map/ppermute | solution.py:22
  14.7 8.2 %collective-permute-start.1 = (f32[144,256]{1,0:T(8,128)S(1)}, f32[144,256]{1,0:T(8,128)S(1)}, u32[]{:S(2)}, u32[]{:S(2)}) collective-permute-start(f32[144,256]{1,0:T(8,128)S(1)} %get-tuple-element.19), channel_id=1, source_target_pairs={{0,2},{1,3},{2,0},{3,1},{4,6},{5,7},{6,4},{7,5},{8,10},{9,11},{10,... | collective-permute-start | bytes 442376 | tf_op jit(solution)/shard_map/ppermute | solution.py:22
  17.0 7.8 %collective-permute-start.2 = (f32[144,256]{1,0:T(8,128)S(1)}, f32[144,256]{1,0:T(8,128)S(1)}, u32[]{:S(2)}, u32[]{:S(2)}) collective-permute-start(f32[144,256]{1,0:T(8,128)S(1)} %get-tuple-element.21), channel_id=1, source_target_pairs={{0,4},{1,5},{2,6},{3,7},{4,0},{5,1},{6,2},{7,3},{8,12},{9,13},{10,... | collective-permute-start | bytes 442376 | tf_op jit(solution)/shard_map/ppermute | solution.py:22
  18.2 8.1 %collective-permute-start.3 = (f32[144,256]{1,0:T(8,128)S(1)}, f32[144,256]{1,0:T(8,128)S(1)}, u32[]{:S(2)}, u32[]{:S(2)}) collective-permute-start(f32[144,256]{1,0:T(8,128)S(1)} %get-tuple-element.20), channel_id=1, source_target_pairs={{0,6},{1,7},{2,4},{3,5},{4,2},{5,3},{6,0},{7,1},{8,14},{9,15},{10,... | collective-permute-start | bytes 442376 | tf_op jit(solution)/shard_map/ppermute | solution.py:22
  19.7 10.1 %collective-permute-start.16 = (f32[144,256]{1,0:T(8,128)S(1)}, f32[144,256]{1,0:T(8,128)S(1)}, u32[]{:S(2)}, u32[]{:S(2)}) collective-permute-start(f32[144,256]{1,0:T(8,128)S(1)} %get-tuple-element.16), channel_id=1, source_target_pairs={{0,2},{1,3},{2,0},{3,1},{4,6},{5,7},{6,4},{7,5},{8,10},{9,11},{10,... | collective-permute-start | bytes 442376 | tf_op jit(solution)/shard_map/ppermute | solution.py:22
  21.8 9.7 %collective-permute-start.17 = (f32[144,256]{1,0:T(8,128)S(1)}, f32[144,256]{1,0:T(8,128)S(1)}, u32[]{:S(2)}, u32[]{:S(2)}) collective-permute-start(f32[144,256]{1,0:T(8,128)S(1)} %get-tuple-element.18), channel_id=1, source_target_pairs={{0,4},{1,5},{2,6},{3,7},{4,0},{5,1},{6,2},{7,3},{8,12},{9,13},{10,... | collective-permute-start | bytes 442376 | tf_op jit(solution)/shard_map/ppermute | solution.py:22
  23.0 9.6 %collective-permute-start.18 = (f32[144,256]{1,0:T(8,128)S(1)}, f32[144,256]{1,0:T(8,128)S(1)}, u32[]{:S(2)}, u32[]{:S(2)}) collective-permute-start(f32[144,256]{1,0:T(8,128)S(1)} %get-tuple-element.17), channel_id=1, source_target_pairs={{0,6},{1,7},{2,4},{3,5},{4,2},{5,3},{6,0},{7,1},{8,14},{9,15},{10,... | collective-permute-start | bytes 442376 | tf_op jit(solution)/shard_map/ppermute | solution.py:22
  26.3 9.4 %collective-permute-start.7 = (bf16[128,256]{1,0:T(8,128)(2,1)S(1)}, bf16[128,256]{1,0:T(8,128)(2,1)S(1)}, u32[]{:S(2)}, u32[]{:S(2)}) collective-permute-start(bf16[128,256]{1,0:T(8,128)(2,1)S(1)} %pad_maximum_fusion.2), channel_id=1, source_target_pairs={{0,2},{1,3},{2,0},{3,1},{4,6},{5,7},{6,4},{7,5},{8,10},{9,11},{10,... | collective-permute-start | bytes 196616 | tf_op jit(solution)/shard_map/ppermute | solution.py:22
  28.4 7.4 %collective-permute-start.8 = (bf16[128,256]{1,0:T(8,128)(2,1)S(1)}, bf16[128,256]{1,0:T(8,128)(2,1)S(1)}, u32[]{:S(2)}, u32[]{:S(2)}) collective-permute-start(bf16[128,256]{1,0:T(8,128)(2,1)S(1)} %pad_maximum_fusion.2), channel_id=1, source_target_pairs={{0,4},{1,5},{2,6},{3,7},{4,0},{5,1},{6,2},{7,3},{8,12},{9,13},{10,... | collective-permute-start | bytes 196616 | tf_op jit(solution)/shard_map/ppermute | solution.py:22
  29.9 5.9 %collective-permute-start.9 = (bf16[128,256]{1,0:T(8,128)(2,1)S(1)}, bf16[128,256]{1,0:T(8,128)(2,1)S(1)}, u32[]{:S(2)}, u32[]{:S(2)}) collective-permute-start(bf16[128,256]{1,0:T(8,128)(2,1)S(1)} %pad_maximum_fusion.2), channel_id=1, source_target_pairs={{0,6},{1,7},{2,4},{3,5},{4,2},{5,3},{6,0},{7,1},{8,14},{9,15},{10,... | collective-permute-start | bytes 196616 | tf_op jit(solution)/shard_map/ppermute | solution.py:22
  32.7 7.1 %collective-permute-start.19 = (f32[72,256]{1,0:T(8,128)S(1)}, f32[72,256]{1,0:T(8,128)S(1)}, u32[]{:S(2)}, u32[]{:S(2)}) collective-permute-start(f32[72,256]{1,0:T(8,128)S(1)} %constant_dynamic-slice_fusion), channel_id=1, source_target_pairs={{0,8},{1,9},{2,10},{3,11},{4,12},{5,13},{6,14},{7,15},{8,0},{9,1},... | collective-permute-start | bytes 221192 | tf_op jit(solution)/shard_map/ppermute | solution.py:22
  35.7 7.7 %collective-permute-start.5 = (f32[72,256]{1,0:T(8,128)S(1)}, f32[72,256]{1,0:T(8,128)S(1)}, u32[]{:S(2)}, u32[]{:S(2)}) collective-permute-start(f32[72,256]{1,0:T(8,128)S(1)} %constant_dynamic-slice_fusion.5), channel_id=1, source_target_pairs={{0,8},{1,9},{2,10},{3,11},{4,12},{5,13},{6,14},{7,15},{8,0},{9,1},... | collective-permute-start | bytes 221192 | tf_op jit(solution)/shard_map/ppermute | solution.py:22
  39.8 5.3 %collective-permute-start.20 = (f32[72,256]{1,0:T(8,128)S(1)}, f32[72,256]{1,0:T(8,128)S(1)}, u32[]{:S(2)}, u32[]{:S(2)}) collective-permute-start(f32[72,256]{1,0:T(8,128)S(1)} %dynamic-slice_add_fusion.2), channel_id=1, source_target_pairs={{0,8},{1,9},{2,10},{3,11},{4,12},{5,13},{6,14},{7,15},{8,0},{9,1},... | collective-permute-start | bytes 221192 | tf_op jit(solution)/shard_map/ppermute | solution.py:22
  43.4 6.9 %collective-permute-start.6 = (f32[72,256]{1,0:T(8,128)S(1)}, f32[72,256]{1,0:T(8,128)S(1)}, u32[]{:S(2)}, u32[]{:S(2)}) collective-permute-start(f32[72,256]{1,0:T(8,128)S(1)} %dynamic-slice_add_fusion.3), channel_id=1, source_target_pairs={{0,8},{1,9},{2,10},{3,11},{4,12},{5,13},{6,14},{7,15},{8,0},{9,1},... | collective-permute-start | bytes 221192 | tf_op jit(solution)/shard_map/ppermute | solution.py:22
  45.2 8.7 %collective-permute-start.21 = (f32[144,256]{1,0:T(8,128)S(1)}, f32[144,256]{1,0:T(8,128)S(1)}, u32[]{:S(2)}, u32[]{:S(2)}) collective-permute-start(f32[144,256]{1,0:T(8,128)S(1)} %get-tuple-element.15), channel_id=1, source_target_pairs={{0,2},{1,3},{2,0},{3,1},{4,6},{5,7},{6,4},{7,5},{8,10},{9,11},{10,... | collective-permute-start | bytes 442376 | tf_op jit(solution)/shard_map/ppermute | solution.py:22
  46.1 9.6 %collective-permute-start.22 = (f32[144,256]{1,0:T(8,128)S(1)}, f32[144,256]{1,0:T(8,128)S(1)}, u32[]{:S(2)}, u32[]{:S(2)}) collective-permute-start(f32[144,256]{1,0:T(8,128)S(1)} %get-tuple-element.15), channel_id=1, source_target_pairs={{0,4},{1,5},{2,6},{3,7},{4,0},{5,1},{6,2},{7,3},{8,12},{9,13},{10,... | collective-permute-start | bytes 442376 | tf_op jit(solution)/shard_map/ppermute | solution.py:22
  50.3 6.3 %collective-permute-start.23 = (f32[144,256]{1,0:T(8,128)S(1)}, f32[144,256]{1,0:T(8,128)S(1)}, u32[]{:S(2)}, u32[]{:S(2)}) collective-permute-start(f32[144,256]{1,0:T(8,128)S(1)} %get-tuple-element.15), channel_id=1, source_target_pairs={{0,6},{1,7},{2,4},{3,5},{4,2},{5,3},{6,0},{7,1},{8,14},{9,15},{10,... | collective-permute-start | bytes 442376 | tf_op jit(solution)/shard_map/ppermute | solution.py:22
  50.3 7.4 %collective-permute-start.11 = (f32[144,256]{1,0:T(8,128)S(1)}, f32[144,256]{1,0:T(8,128)S(1)}, u32[]{:S(2)}, u32[]{:S(2)}) collective-permute-start(f32[144,256]{1,0:T(8,128)S(1)} %maximum_select_fusion.2), channel_id=1, source_target_pairs={{0,2},{1,3},{2,0},{3,1},{4,6},{5,7},{6,4},{7,5},{8,10},{9,11},{10,... | collective-permute-start | bytes 442376 | tf_op jit(solution)/shard_map/ppermute | solution.py:22
  51.8 5.9 %collective-permute-start.12 = (f32[144,256]{1,0:T(8,128)S(1)}, f32[144,256]{1,0:T(8,128)S(1)}, u32[]{:S(2)}, u32[]{:S(2)}) collective-permute-start(f32[144,256]{1,0:T(8,128)S(1)} %maximum_select_fusion.2), channel_id=1, source_target_pairs={{0,4},{1,5},{2,6},{3,7},{4,0},{5,1},{6,2},{7,3},{8,12},{9,13},{10,... | collective-permute-start | bytes 442376 | tf_op jit(solution)/shard_map/ppermute | solution.py:22
  53.9 6.1 %collective-permute-start.13 = (f32[144,256]{1,0:T(8,128)S(1)}, f32[144,256]{1,0:T(8,128)S(1)}, u32[]{:S(2)}, u32[]{:S(2)}) collective-permute-start(f32[144,256]{1,0:T(8,128)S(1)} %maximum_select_fusion.2), channel_id=1, source_target_pairs={{0,6},{1,7},{2,4},{3,5},{4,2},{5,3},{6,0},{7,1},{8,14},{9,15},{10,... | collective-permute-start | bytes 442376 | tf_op jit(solution)/shard_map/ppermute | solution.py:22
  55.7 4.5 %collective-permute-start.10 = (bf16[512,256]{1,0:T(8,128)(2,1)S(1)}, bf16[512,256]{1,0:T(8,128)(2,1)S(1)}, u32[]{:S(2)}, u32[]{:S(2)}) collective-permute-start(bf16[512,256]{1,0:T(8,128)(2,1)S(1)} %pad_maximum_fusion.1), channel_id=1, source_target_pairs={{0,1},{1,0},{2,3},{3,2},{4,5},{5,4},{6,7},{7,6},{8,9},{9,8},{10,11... | collective-permute-start | bytes 786440 | tf_op jit(solution)/shard_map/ppermute | solution.py:22
  56.6 3.6 %collective-permute-start.24 = (f32[576,256]{1,0:T(8,128)S(1)}, f32[576,256]{1,0:T(8,128)S(1)}, u32[]{:S(2)}, u32[]{:S(2)}) collective-permute-start(f32[576,256]{1,0:T(8,128)S(1)} %constant_dynamic-update-slice_fusion), channel_id=1, source_target_pairs={{0,1},{1,0},{2,3},{3,2},{4,5},{5,4},{6,7},{7,6},{8,9},{9,8},{10,11... | collective-permute-start | bytes 1769480 | tf_op jit(solution)/shard_map/ppermute | solution.py:22
  60.1 2.1 %collective-permute-start.14 = (f32[576,256]{1,0:T(8,128)S(1)}, f32[576,256]{1,0:T(8,128)S(1)}, u32[]{:S(2)}, u32[]{:S(2)}) collective-permute-start(f32[576,256]{1,0:T(8,128)S(1)} %constant_dynamic-update-slice_fusion.4), channel_id=1, source_target_pairs={{0,1},{1,0},{2,3},{3,2},{4,5},{5,4},{6,7},{7,6},{8,9},{9,8},{10,11... | collective-permute-start | bytes 1769480 | tf_op jit(solution)/shard_map/ppermute | solution.py:22
  60.2 2.2 %copy-start.1 = (bf16[2048,1024]{1,0:T(8,128)(2,1)S(1)}, bf16[2048,1024]{1,0:T(8,128)(2,1)}, u32[]{:S(2)}) copy-start(bf16[2048,1024]{1,0:T(8,128)(2,1)} %a_hbm.1) | copy-start | bytes 12582916

commit v5 on v4

--- a/solution.py
+++ b/solution.py
@@ -64,13 +64,14 @@
 def sum_everywhere(parts, rows):
     core, square, far = stages()
     parts = [scatter_stage(p, *core) for p in parts]
+    parts[0], rows = tie(parts[0], rows)
     rows = widen(rows, *far)
     parts = [scatter_stage(p, *square) for p in parts]
-    parts[0], rows = tie(parts[0], rows)
+    parts[1], rows = tie(parts[1], rows)
     parts = [scatter_stage(p, *far) for p in parts]
     rows = widen(rows, *square)
     parts = [gather_stage(p, *far) for p in parts]
-    parts[0], rows = tie(parts[0], rows)
+    parts[1], rows = tie(parts[1], rows)
     rows = widen(rows, *core)
     parts = [gather_stage(p, *square) for p in parts]
     parts = [gather_stage(p, *core) for p in parts]

time: 85.7 us -> 81.9 us (0.956)
  starting transfers between devices: 33.7 us -> 29.9 us
    ppermute x25, starting transfers between devices: 33.7 us -> 29.9 us  [exchange(): return lax.ppermute(value, AXIS, [(i, i ^ distance) for i in range(n)])]
    unnamed x4 -> x6, local copies, waits for them, and re-layouts: 2.36 us -> 2.37 us
  transfers between devices with their start and end apart: 25 -> 25, of which waited for: 10 -> 15; matrix products, arithmetic and copies ran while one was open for 4% -> 4% of each run, Pallas kernels for 0% -> 0%
where the time goes in v5:
time: 81.9 us; the launch traced here: 81.6 us
  starting transfers between devices  29.9 us (37%)
  Pallas kernels  25.7 us (31%)
  waiting for transfers between devices  19.5 us (24%)
  local copies, waits for them, and re-layouts  2.72 us (3%)
  other arithmetic  2.66 us (3%)
  between operations  1.11 us (1%)
    ppermute x25, starting transfers between devices, exchange(): return lax.ppermute(value, AXIS, [(i, i ^ distance) for i in range(n)])  29.9 us
    pallas_call x1, Pallas kernels, body(): pl.pallas_call(functools.partial(finish_kernel, chains, rows_total, facto...  22.8 us
    ppermute x25, waiting for transfers between devices, exchange(): return lax.ppermute(value, AXIS, [(i, i ^ distance) for i in range(n)])  19.5 us
    pallas_call x1, Pallas kernels, body(): pl.pallas_call(functools.partial(moment_kernel, chains), out_shape=[jax.S...  2.94 us
    add x6, other arithmetic, scatter_stage(): total = total + item  2.38 us
    unnamed x6, local copies, waits for them, and re-layouts  2.37 us
  transfers between devices with their start and end apart: 25, of which 15 were waited for; matrix products, arithmetic and copies ran while one was open for 4% of the time, Pallas kernels for 0%

profile of v5, /device:TPU:0, one launch (start us, length us, event | category | flops | bytes accessed | tf_op | source)
XLA Modules:
  0.0 81.6 jit_solution(11413696180001617724)
XLA Ops:
  0.6 0.0 copy-start
  0.7 2.2 %copy-done = bf16[2048,1024]{1,0:T(8,128)(2,1)S(1)} copy-done((bf16[2048,1024]{1,0:T(8,128)(2,1)S(1)}, bf16[2048,1024]{1,0:T(8,128)(2,1)}, u32[]{:S(2)}) %copy-start) | copy-done | bytes 4194328
  2.8 2.9 %shard_map.41 = (f32[1152,256]{1,0:T(8,128)S(1)}, f32[1152,256]{1,0:T(8,128)S(1)}) custom-call(bf16[2048,1024]{1,0:T(8,128)(2,1)S(1)} %copy-done), custom_call_target="tpu_custom_call" | custom-call | tf_op jit(solution)/shard_map/pallas_call | solution.py:291
  5.8 0.5 collective-permute-start
  6.4 0.1 collective-permute-start.4
  6.5 1.6 %collective-permute-done = f32[576,256]{1,0:T(8,128)} collective-permute-done((f32[576,256]{1,0:T(8,128)S(1)}, f32[576,256]{1,0:T(8,128)}, u32[]{:S(2)}, u32[]{:S(2)}) %collective-permute-start) | collective-permute-done | bytes 589856 | tf_op jit(solution)/shard_map/ppermute | solution.py:22
  8.1 1.1 %dynamic-slice_add_fusion.1 = f32[576,256]{1,0:T(8,128)S(1)} fusion(f32[576,256]{1,0:T(8,128)} %collective-permute-done, f32[1152,256]{1,0:T(8,128)S(1)} %get-tuple-element.10, s32[]{:T(128)S(6)} %select_n.65), kind=kLoop, calls=%fused_computation.3 | loop fusion | flops 147456 | bytes 1769476 | tf_op jit(solution)/shard_map/add | solution.py:35
  9.3 3.0 %collective-permute-start.1 = (f32[144,256]{1,0:T(8,128)S(1)}, f32[144,256]{1,0:T(8,128)S(1)}, u32[]{:S(2)}, u32[]{:S(2)}) collective-permute-start(f32[144,256]{1,0:T(8,128)S(1)} %get-tuple-element.23), channel_id=1, source_target_pairs={{0,2},{1,3},{2,0},{3,1},{4,6},{5,7},{6,4},{7,5},{8,10},{9,11},{10,... | collective-permute-start | bytes 442376 | tf_op jit(solution)/shard_map/ppermute | solution.py:22
  12.3 1.6 %collective-permute-start.2 = (f32[144,256]{1,0:T(8,128)S(1)}, f32[144,256]{1,0:T(8,128)S(1)}, u32[]{:S(2)}, u32[]{:S(2)}) collective-permute-start(f32[144,256]{1,0:T(8,128)S(1)} %get-tuple-element.25), channel_id=1, source_target_pairs={{0,4},{1,5},{2,6},{3,7},{4,0},{5,1},{6,2},{7,3},{8,12},{9,13},{10,... | collective-permute-start | bytes 442376 | tf_op jit(solution)/shard_map/ppermute | solution.py:22
  13.9 1.1 %dynamic-slice_add_fusion = f32[576,256]{1,0:T(8,128)S(1)} fusion(f32[576,256]{1,0:T(8,128)} %collective-permute-done.4, f32[1152,256]{1,0:T(8,128)S(1)} %get-tuple-element.11, s32[]{:T(128)S(6)} %select_n.65), kind=kLoop, calls=%fused_computation.2 | loop fusion | flops 147456 | bytes 1769476 | tf_op jit(solution)/shard_map/add | solution.py:35
  15.0 3.0 %collective-permute-start.5 = (bf16[64,256]{1,0:T(8,128)(2,1)S(1)}, bf16[64,256]{1,0:T(8,128)(2,1)S(1)}, u32[]{:S(2)}, u32[]{:S(2)}) collective-permute-start(bf16[64,256]{1,0:T(8,128)(2,1)S(1)} %copy-done.2), channel_id=1, source_target_pairs={{0,8},{1,9},{2,10},{3,11},{4,12},{5,13},{6,14},{7,15},{8,0},{9,1},... | collective-permute-start | bytes 98312 | tf_op jit(solution)/shard_map/ppermute | solution.py:22
  18.1 1.6 %collective-permute-start.12 = (f32[144,256]{1,0:T(8,128)S(1)}, f32[144,256]{1,0:T(8,128)S(1)}, u32[]{:S(2)}, u32[]{:S(2)}) collective-permute-start(f32[144,256]{1,0:T(8,128)S(1)} %get-tuple-element.20), channel_id=1, source_target_pairs={{0,2},{1,3},{2,0},{3,1},{4,6},{5,7},{6,4},{7,5},{8,10},{9,11},{10,... | collective-permute-start | bytes 442376 | tf_op jit(solution)/shard_map/ppermute | solution.py:22
  19.7 1.2 %collective-permute-done.5 = bf16[64,256]{1,0:T(8,128)(2,1)S(1)} collective-permute-done((bf16[64,256]{1,0:T(8,128)(2,1)S(1)}, bf16[64,256]{1,0:T(8,128)(2,1)S(1)}, u32[]{:S(2)}, u32[]{:S(2)}) %collective-permute-start.5) | collective-permute-done | bytes 32800 | tf_op jit(solution)/shard_map/ppermute | solution.py:22
  20.8 3.5 %collective-permute-start.13 = (f32[144,256]{1,0:T(8,128)S(1)}, f32[144,256]{1,0:T(8,128)S(1)}, u32[]{:S(2)}, u32[]{:S(2)}) collective-permute-start(f32[144,256]{1,0:T(8,128)S(1)} %get-tuple-element.22), channel_id=1, source_target_pairs={{0,4},{1,5},{2,6},{3,7},{4,0},{5,1},{6,2},{7,3},{8,12},{9,13},{10,... | collective-permute-start | bytes 442376 | tf_op jit(solution)/shard_map/ppermute | solution.py:22
  24.3 0.1 collective-permute-start.14
  24.5 3.0 %collective-permute-start.10 = (bf16[128,256]{1,0:T(8,128)(2,1)S(1)}, bf16[128,256]{1,0:T(8,128)(2,1)S(1)}, u32[]{:S(2)}, u32[]{:S(2)}) collective-permute-start(bf16[128,256]{1,0:T(8,128)(2,1)S(1)} %pad_maximum_fusion.2), channel_id=1, source_target_pairs={{0,6},{1,7},{2,4},{3,5},{4,2},{5,3},{6,0},{7,1},{8,14},{9,15},{10,... | collective-permute-start | bytes 196616 | tf_op jit(solution)/shard_map/ppermute | solution.py:22
  27.4 0.6 collective-permute-start.8
  28.0 0.2 collective-permute-start.9
  28.2 0.8 collective-permute-done.13
  29.0 2.0 %collective-permute-start.6 = (f32[72,256]{1,0:T(8,128)S(1)}, f32[72,256]{1,0:T(8,128)S(1)}, u32[]{:S(2)}, u32[]{:S(2)}) collective-permute-start(f32[72,256]{1,0:T(8,128)S(1)} %constant_dynamic-slice_fusion.4), channel_id=1, source_target_pairs={{0,8},{1,9},{2,10},{3,11},{4,12},{5,13},{6,14},{7,15},{8,0},{9,1},... | collective-permute-start | bytes 221192 | tf_op jit(solution)/shard_map/ppermute | solution.py:22
  31.0 1.9 %collective-permute-done.14 = f32[144,256]{1,0:T(8,128)S(1)} collective-permute-done((f32[144,256]{1,0:T(8,128)S(1)}, f32[144,256]{1,0:T(8,128)S(1)}, u32[]{:S(2)}, u32[]{:S(2)}) %collective-permute-start.14) | collective-permute-done | bytes 147488 | tf_op jit(solution)/shard_map/ppermute | solution.py:22
  33.0 1.3 %collective-permute-start.15 = (f32[72,256]{1,0:T(8,128)S(1)}, f32[72,256]{1,0:T(8,128)S(1)}, u32[]{:S(2)}, u32[]{:S(2)}) collective-permute-start(f32[72,256]{1,0:T(8,128)S(1)} %constant_dynamic-slice_fusion), channel_id=1, source_target_pairs={{0,8},{1,9},{2,10},{3,11},{4,12},{5,13},{6,14},{7,15},{8,0},{9,1},... | collective-permute-start | bytes 221192 | tf_op jit(solution)/shard_map/ppermute | solution.py:22
  34.3 1.0 %collective-permute-done.9 = bf16[128,256]{1,0:T(8,128)(2,1)S(1)} collective-permute-done((bf16[128,256]{1,0:T(8,128)(2,1)S(1)}, bf16[128,256]{1,0:T(8,128)(2,1)S(1)}, u32[]{:S(2)}, u32[]{:S(2)}) %collective-permute-start.9) | collective-permute-done | bytes 65568 | tf_op jit(solution)/shard_map/ppermute | solution.py:22
  35.4 0.5 collective-permute-done.6
  35.9 2.3 %collective-permute-start.7 = (f32[72,256]{1,0:T(8,128)S(1)}, f32[72,256]{1,0:T(8,128)S(1)}, u32[]{:S(2)}, u32[]{:S(2)}) collective-permute-start(f32[72,256]{1,0:T(8,128)S(1)} %dynamic-slice_add_fusion.3), channel_id=1, source_target_pairs={{0,8},{1,9},{2,10},{3,11},{4,12},{5,13},{6,14},{7,15},{8,0},{9,1},... | collective-permute-start | bytes 221192 | tf_op jit(solution)/shard_map/ppermute | solution.py:22
  38.2 3.1 %collective-permute-done.15 = f32[72,256]{1,0:T(8,128)S(1)} collective-permute-done((f32[72,256]{1,0:T(8,128)S(1)}, f32[72,256]{1,0:T(8,128)S(1)}, u32[]{:S(2)}, u32[]{:S(2)}) %collective-permute-start.15) | collective-permute-done | bytes 73760 | tf_op jit(solution)/shard_map/ppermute | solution.py:22
  41.3 0.1 collective-permute-start.16
  41.4 1.7 %collective-permute-done.7 = f32[72,256]{1,0:T(8,128)S(1)} collective-permute-done((f32[72,256]{1,0:T(8,128)S(1)}, f32[72,256]{1,0:T(8,128)S(1)}, u32[]{:S(2)}, u32[]{:S(2)}) %collective-permute-start.7) | collective-permute-done | bytes 73760 | tf_op jit(solution)/shard_map/ppermute | solution.py:22
  43.2 0.9 %collective-permute-start.21 = (f32[144,256]{1,0:T(8,128)S(1)}, f32[144,256]{1,0:T(8,128)S(1)}, u32[]{:S(2)}, u32[]{:S(2)}) collective-permute-start(f32[144,256]{1,0:T(8,128)S(1)} %maximum_select_fusion.2), channel_id=1, source_target_pairs={{0,2},{1,3},{2,0},{3,1},{4,6},{5,7},{6,4},{7,5},{8,10},{9,11},{10,... | collective-permute-start | bytes 442376 | tf_op jit(solution)/shard_map/ppermute | solution.py:22
  44.1 1.3 %collective-permute-start.22 = (f32[144,256]{1,0:T(8,128)S(1)}, f32[144,256]{1,0:T(8,128)S(1)}, u32[]{:S(2)}, u32[]{:S(2)}) collective-permute-start(f32[144,256]{1,0:T(8,128)S(1)} %maximum_select_fusion.2), channel_id=1, source_target_pairs={{0,4},{1,5},{2,6},{3,7},{4,0},{5,1},{6,2},{7,3},{8,12},{9,13},{10,... | collective-permute-start | bytes 442376 | tf_op jit(solution)/shard_map/ppermute | solution.py:22
  45.4 1.3 %collective-permute-start.23 = (f32[144,256]{1,0:T(8,128)S(1)}, f32[144,256]{1,0:T(8,128)S(1)}, u32[]{:S(2)}, u32[]{:S(2)}) collective-permute-start(f32[144,256]{1,0:T(8,128)S(1)} %maximum_select_fusion.2), channel_id=1, source_target_pairs={{0,6},{1,7},{2,4},{3,5},{4,2},{5,3},{6,0},{7,1},{8,14},{9,15},{10,... | collective-permute-start | bytes 442376 | tf_op jit(solution)/shard_map/ppermute | solution.py:22
  46.7 0.4 collective-permute-done.16
  47.2 0.6 collective-permute-start.17
  47.8 1.2 %collective-permute-start.18 = (f32[144,256]{1,0:T(8,128)S(1)}, f32[144,256]{1,0:T(8,128)S(1)}, u32[]{:S(2)}, u32[]{:S(2)}) collective-permute-start(f32[144,256]{1,0:T(8,128)S(1)} %get-tuple-element.19), channel_id=1, source_target_pairs={{0,4},{1,5},{2,6},{3,7},{4,0},{5,1},{6,2},{7,3},{8,12},{9,13},{10,... | collective-permute-start | bytes 442376 | tf_op jit(solution)/shard_map/ppermute | solution.py:22
  49.1 0.6 collective-permute-done.21
  49.8 1.6 %collective-permute-start.19 = (f32[144,256]{1,0:T(8,128)S(1)}, f32[144,256]{1,0:T(8,128)S(1)}, u32[]{:S(2)}, u32[]{:S(2)}) collective-permute-start(f32[144,256]{1,0:T(8,128)S(1)} %get-tuple-element.19), channel_id=1, source_target_pairs={{0,6},{1,7},{2,4},{3,5},{4,2},{5,3},{6,0},{7,1},{8,14},{9,15},{10,... | collective-permute-start | bytes 442376 | tf_op jit(solution)/shard_map/ppermute | solution.py:22
  51.3 0.1 collective-permute-start.11
  51.4 1.8 %collective-permute-done.23 = f32[144,256]{1,0:T(8,128)S(1)} collective-permute-done((f32[144,256]{1,0:T(8,128)S(1)}, f32[144,256]{1,0:T(8,128)S(1)}, u32[]{:S(2)}, u32[]{:S(2)}) %collective-permute-start.23) | collective-permute-done | bytes 147488 | tf_op jit(solution)/shard_map/ppermute | solution.py:22
  53.2 0.1 collective-permute-start.24
  53.3 1.1 %collective-permute-done.17 = f32[144,256]{1,0:T(8,128)S(1)} collective-permute-done((f32[144,256]{1,0:T(8,128)S(1)}, f32[144,256]{1,0:T(8,128)S(1)}, u32[]{:S(2)}, u32[]{:S(2)}) %collective-permute-start.17) | collective-permute-done | bytes 147488 | tf_op jit(solution)/shard_map/ppermute | solution.py:22
  54.4 0.4 collective-permute-done.18
  54.8 1.5 %collective-permute-done.19 = f32[144,256]{1,0:T(8,128)S(1)} collective-permute-done((f32[144,256]{1,0:T(8,128)S(1)}, f32[144,256]{1,0:T(8,128)S(1)}, u32[]{:S(2)}, u32[]{:S(2)}) %collective-permute-start.19) | collective-permute-done | bytes 147488 | tf_op jit(solution)/shard_map/ppermute | solution.py:22
  56.3 0.1 collective-permute-start.20
  56.5 0.1 maximum_select_fusion.1.refs_1_
  56.6 1.8 %collective-permute-done.20 = f32[576,256]{1,0:T(8,128)S(1)} collective-permute-done((f32[576,256]{1,0:T(8,128)S(1)}, f32[576,256]{1,0:T(8,128)S(1)}, u32[]{:S(2)}, u32[]{:S(2)}) %collective-permute-start.20) | collective-permute-done | bytes 589856 | tf_op jit(solution)/shard_map/ppermute | solution.py:22
  58.4 0.1 maximum_select_fusion.refs_0_
  58.5 0.2 copy-done.1
  58.7 22.8 %shard_map.42 = (bf16[2048,256]{1,0:T(8,128)(2,1)}, bf16[64,256]{1,0:T(8,128)(2,1)}) custom-call(s32[1]{0:T(128)} %bitcast.me_ref, bf16[1024,256]{1,0:T(8,128)(2,1)S(1)} %pad_maximum_fusion.sketch_ref, bf16[2048,1024]{1,0:T(8,128)(2,1)S(1)} %copy-done.1, f32[1152,256]{1,0:T(8,128)S(1)} %maximum_select_fusion.refs_0_, ...), custom_call_target="tpu_custom_call" | custom-call | tf_op jit(solution)/shard_map/pallas_call | solution.py:301
  (38 shorter events, 0.6 us)
Async XLA Ops:
  0.6 2.2 %copy-start = (bf16[2048,1024]{1,0:T(8,128)(2,1)S(1)}, bf16[2048,1024]{1,0:T(8,128)(2,1)}, u32[]{:S(2)}) copy-start(bf16[2048,1024]{1,0:T(8,128)(2,1)} %a_hbm.1) | copy-start | bytes 12582916
  5.8 2.3 %collective-permute-start = (f32[576,256]{1,0:T(8,128)S(1)}, f32[576,256]{1,0:T(8,128)}, u32[]{:S(2)}, u32[]{:S(2)}) collective-permute-start(f32[576,256]{1,0:T(8,128)S(1)} %constant_dynamic-slice_fusion.9), channel_id=1, source_target_pairs={{0,1},{1,0},{2,3},{3,2},{4,5},{5,4},{6,7},{7,6},{8,9},{9,8},{10,11... | collective-permute-start | bytes 1769480 | tf_op jit(solution)/shard_map/ppermute | solution.py:22
  6.4 7.5 %collective-permute-start.4 = (f32[576,256]{1,0:T(8,128)S(1)}, f32[576,256]{1,0:T(8,128)}, u32[]{:S(2)}, u32[]{:S(2)}) collective-permute-start(f32[576,256]{1,0:T(8,128)S(1)} %constant_dynamic-slice_fusion.5), channel_id=1, source_target_pairs={{0,1},{1,0},{2,3},{3,2},{4,5},{5,4},{6,7},{7,6},{8,9},{9,8},{10,11... | collective-permute-start | bytes 1769480 | tf_op jit(solution)/shard_map/ppermute | solution.py:22
  9.3 5.7 %copy-start.2 = (bf16[64,256]{1,0:T(8,128)(2,1)S(1)}, bf16[64,256]{1,0:T(8,128)(2,1)}, u32[]{:S(2)}) copy-start(bf16[64,256]{1,0:T(8,128)(2,1)} %param.3) | copy-start | bytes 98308
  9.3 15.0 %collective-permute-start.1 = (f32[144,256]{1,0:T(8,128)S(1)}, f32[144,256]{1,0:T(8,128)S(1)}, u32[]{:S(2)}, u32[]{:S(2)}) collective-permute-start(f32[144,256]{1,0:T(8,128)S(1)} %get-tuple-element.23), channel_id=1, source_target_pairs={{0,2},{1,3},{2,0},{3,1},{4,6},{5,7},{6,4},{7,5},{8,10},{9,11},{10,... | collective-permute-start | bytes 442376 | tf_op jit(solution)/shard_map/ppermute | solution.py:22
  12.3 12.2 %collective-permute-start.2 = (f32[144,256]{1,0:T(8,128)S(1)}, f32[144,256]{1,0:T(8,128)S(1)}, u32[]{:S(2)}, u32[]{:S(2)}) collective-permute-start(f32[144,256]{1,0:T(8,128)S(1)} %get-tuple-element.25), channel_id=1, source_target_pairs={{0,4},{1,5},{2,6},{3,7},{4,0},{5,1},{6,2},{7,3},{8,12},{9,13},{10,... | collective-permute-start | bytes 442376 | tf_op jit(solution)/shard_map/ppermute | solution.py:22
  13.8 10.6 %collective-permute-start.3 = (f32[144,256]{1,0:T(8,128)S(1)}, f32[144,256]{1,0:T(8,128)S(1)}, u32[]{:S(2)}, u32[]{:S(2)}) collective-permute-start(f32[144,256]{1,0:T(8,128)S(1)} %get-tuple-element.24), channel_id=1, source_target_pairs={{0,6},{1,7},{2,4},{3,5},{4,2},{5,3},{6,0},{7,1},{8,14},{9,15},{10,... | collective-permute-start | bytes 442376 | tf_op jit(solution)/shard_map/ppermute | solution.py:22
  15.0 5.8 %collective-permute-start.5 = (bf16[64,256]{1,0:T(8,128)(2,1)S(1)}, bf16[64,256]{1,0:T(8,128)(2,1)S(1)}, u32[]{:S(2)}, u32[]{:S(2)}) collective-permute-start(bf16[64,256]{1,0:T(8,128)(2,1)S(1)} %copy-done.2), channel_id=1, source_target_pairs={{0,8},{1,9},{2,10},{3,11},{4,12},{5,13},{6,14},{7,15},{8,0},{9,1},... | collective-permute-start | bytes 98312 | tf_op jit(solution)/shard_map/ppermute | solution.py:22
  18.1 9.9 %collective-permute-start.12 = (f32[144,256]{1,0:T(8,128)S(1)}, f32[144,256]{1,0:T(8,128)S(1)}, u32[]{:S(2)}, u32[]{:S(2)}) collective-permute-start(f32[144,256]{1,0:T(8,128)S(1)} %get-tuple-element.20), channel_id=1, source_target_pairs={{0,2},{1,3},{2,0},{3,1},{4,6},{5,7},{6,4},{7,5},{8,10},{9,11},{10,... | collective-permute-start | bytes 442376 | tf_op jit(solution)/shard_map/ppermute | solution.py:22
  20.8 8.1 %collective-permute-start.13 = (f32[144,256]{1,0:T(8,128)S(1)}, f32[144,256]{1,0:T(8,128)S(1)}, u32[]{:S(2)}, u32[]{:S(2)}) collective-permute-start(f32[144,256]{1,0:T(8,128)S(1)} %get-tuple-element.22), channel_id=1, source_target_pairs={{0,4},{1,5},{2,6},{3,7},{4,0},{5,1},{6,2},{7,3},{8,12},{9,13},{10,... | collective-permute-start | bytes 442376 | tf_op jit(solution)/shard_map/ppermute | solution.py:22
  24.3 8.6 %collective-permute-start.14 = (f32[144,256]{1,0:T(8,128)S(1)}, f32[144,256]{1,0:T(8,128)S(1)}, u32[]{:S(2)}, u32[]{:S(2)}) collective-permute-start(f32[144,256]{1,0:T(8,128)S(1)} %get-tuple-element.21), channel_id=1, source_target_pairs={{0,6},{1,7},{2,4},{3,5},{4,2},{5,3},{6,0},{7,1},{8,14},{9,15},{10,... | collective-permute-start | bytes 442376 | tf_op jit(solution)/shard_map/ppermute | solution.py:22
  24.5 9.9 %collective-permute-start.10 = (bf16[128,256]{1,0:T(8,128)(2,1)S(1)}, bf16[128,256]{1,0:T(8,128)(2,1)S(1)}, u32[]{:S(2)}, u32[]{:S(2)}) collective-permute-start(bf16[128,256]{1,0:T(8,128)(2,1)S(1)} %pad_maximum_fusion.2), channel_id=1, source_target_pairs={{0,6},{1,7},{2,4},{3,5},{4,2},{5,3},{6,0},{7,1},{8,14},{9,15},{10,... | collective-permute-start | bytes 196616 | tf_op jit(solution)/shard_map/ppermute | solution.py:22
  27.4 6.9 %collective-permute-start.8 = (bf16[128,256]{1,0:T(8,128)(2,1)S(1)}, bf16[128,256]{1,0:T(8,128)(2,1)S(1)}, u32[]{:S(2)}, u32[]{:S(2)}) collective-permute-start(bf16[128,256]{1,0:T(8,128)(2,1)S(1)} %pad_maximum_fusion.2), channel_id=1, source_target_pairs={{0,2},{1,3},{2,0},{3,1},{4,6},{5,7},{6,4},{7,5},{8,10},{9,11},{10,... | collective-permute-start | bytes 196616 | tf_op jit(solution)/shard_map/ppermute | solution.py:22
  28.0 7.3 %collective-permute-start.9 = (bf16[128,256]{1,0:T(8,128)(2,1)S(1)}, bf16[128,256]{1,0:T(8,128)(2,1)S(1)}, u32[]{:S(2)}, u32[]{:S(2)}) collective-permute-start(bf16[128,256]{1,0:T(8,128)(2,1)S(1)} %pad_maximum_fusion.2), channel_id=1, source_target_pairs={{0,4},{1,5},{2,6},{3,7},{4,0},{5,1},{6,2},{7,3},{8,12},{9,13},{10,... | collective-permute-start | bytes 196616 | tf_op jit(solution)/shard_map/ppermute | solution.py:22
  29.0 6.9 %collective-permute-start.6 = (f32[72,256]{1,0:T(8,128)S(1)}, f32[72,256]{1,0:T(8,128)S(1)}, u32[]{:S(2)}, u32[]{:S(2)}) collective-permute-start(f32[72,256]{1,0:T(8,128)S(1)} %constant_dynamic-slice_fusion.4), channel_id=1, source_target_pairs={{0,8},{1,9},{2,10},{3,11},{4,12},{5,13},{6,14},{7,15},{8,0},{9,1},... | collective-permute-start | bytes 221192 | tf_op jit(solution)/shard_map/ppermute | solution.py:22
  33.0 8.3 %collective-permute-start.15 = (f32[72,256]{1,0:T(8,128)S(1)}, f32[72,256]{1,0:T(8,128)S(1)}, u32[]{:S(2)}, u32[]{:S(2)}) collective-permute-start(f32[72,256]{1,0:T(8,128)S(1)} %constant_dynamic-slice_fusion), channel_id=1, source_target_pairs={{0,8},{1,9},{2,10},{3,11},{4,12},{5,13},{6,14},{7,15},{8,0},{9,1},... | collective-permute-start | bytes 221192 | tf_op jit(solution)/shard_map/ppermute | solution.py:22
  35.9 7.3 %collective-permute-start.7 = (f32[72,256]{1,0:T(8,128)S(1)}, f32[72,256]{1,0:T(8,128)S(1)}, u32[]{:S(2)}, u32[]{:S(2)}) collective-permute-start(f32[72,256]{1,0:T(8,128)S(1)} %dynamic-slice_add_fusion.3), channel_id=1, source_target_pairs={{0,8},{1,9},{2,10},{3,11},{4,12},{5,13},{6,14},{7,15},{8,0},{9,1},... | collective-permute-start | bytes 221192 | tf_op jit(solution)/shard_map/ppermute | solution.py:22
  41.3 5.8 %collective-permute-start.16 = (f32[72,256]{1,0:T(8,128)S(1)}, f32[72,256]{1,0:T(8,128)S(1)}, u32[]{:S(2)}, u32[]{:S(2)}) collective-permute-start(f32[72,256]{1,0:T(8,128)S(1)} %dynamic-slice_add_fusion.2), channel_id=1, source_target_pairs={{0,8},{1,9},{2,10},{3,11},{4,12},{5,13},{6,14},{7,15},{8,0},{9,1},... | collective-permute-start | bytes 221192 | tf_op jit(solution)/shard_map/ppermute | solution.py:22
  43.2 6.6 %collective-permute-start.21 = (f32[144,256]{1,0:T(8,128)S(1)}, f32[144,256]{1,0:T(8,128)S(1)}, u32[]{:S(2)}, u32[]{:S(2)}) collective-permute-start(f32[144,256]{1,0:T(8,128)S(1)} %maximum_select_fusion.2), channel_id=1, source_target_pairs={{0,2},{1,3},{2,0},{3,1},{4,6},{5,7},{6,4},{7,5},{8,10},{9,11},{10,... | collective-permute-start | bytes 442376 | tf_op jit(solution)/shard_map/ppermute | solution.py:22
  44.1 7.3 %collective-permute-start.22 = (f32[144,256]{1,0:T(8,128)S(1)}, f32[144,256]{1,0:T(8,128)S(1)}, u32[]{:S(2)}, u32[]{:S(2)}) collective-permute-start(f32[144,256]{1,0:T(8,128)S(1)} %maximum_select_fusion.2), channel_id=1, source_target_pairs={{0,4},{1,5},{2,6},{3,7},{4,0},{5,1},{6,2},{7,3},{8,12},{9,13},{10,... | collective-permute-start | bytes 442376 | tf_op jit(solution)/shard_map/ppermute | solution.py:22
  45.4 7.8 %collective-permute-start.23 = (f32[144,256]{1,0:T(8,128)S(1)}, f32[144,256]{1,0:T(8,128)S(1)}, u32[]{:S(2)}, u32[]{:S(2)}) collective-permute-start(f32[144,256]{1,0:T(8,128)S(1)} %maximum_select_fusion.2), channel_id=1, source_target_pairs={{0,6},{1,7},{2,4},{3,5},{4,2},{5,3},{6,0},{7,1},{8,14},{9,15},{10,... | collective-permute-start | bytes 442376 | tf_op jit(solution)/shard_map/ppermute | solution.py:22
  47.2 7.1 %collective-permute-start.17 = (f32[144,256]{1,0:T(8,128)S(1)}, f32[144,256]{1,0:T(8,128)S(1)}, u32[]{:S(2)}, u32[]{:S(2)}) collective-permute-start(f32[144,256]{1,0:T(8,128)S(1)} %get-tuple-element.19), channel_id=1, source_target_pairs={{0,2},{1,3},{2,0},{3,1},{4,6},{5,7},{6,4},{7,5},{8,10},{9,11},{10,... | collective-permute-start | bytes 442376 | tf_op jit(solution)/shard_map/ppermute | solution.py:22
  47.8 7.0 %collective-permute-start.18 = (f32[144,256]{1,0:T(8,128)S(1)}, f32[144,256]{1,0:T(8,128)S(1)}, u32[]{:S(2)}, u32[]{:S(2)}) collective-permute-start(f32[144,256]{1,0:T(8,128)S(1)} %get-tuple-element.19), channel_id=1, source_target_pairs={{0,4},{1,5},{2,6},{3,7},{4,0},{5,1},{6,2},{7,3},{8,12},{9,13},{10,... | collective-permute-start | bytes 442376 | tf_op jit(solution)/shard_map/ppermute | solution.py:22
  49.8 6.6 %collective-permute-start.19 = (f32[144,256]{1,0:T(8,128)S(1)}, f32[144,256]{1,0:T(8,128)S(1)}, u32[]{:S(2)}, u32[]{:S(2)}) collective-permute-start(f32[144,256]{1,0:T(8,128)S(1)} %get-tuple-element.19), channel_id=1, source_target_pairs={{0,6},{1,7},{2,4},{3,5},{4,2},{5,3},{6,0},{7,1},{8,14},{9,15},{10,... | collective-permute-start | bytes 442376 | tf_op jit(solution)/shard_map/ppermute | solution.py:22
  51.3 5.1 %collective-permute-start.11 = (bf16[512,256]{1,0:T(8,128)(2,1)S(1)}, bf16[512,256]{1,0:T(8,128)(2,1)S(1)}, u32[]{:S(2)}, u32[]{:S(2)}) collective-permute-start(bf16[512,256]{1,0:T(8,128)(2,1)S(1)} %pad_maximum_fusion.1), channel_id=1, source_target_pairs={{0,1},{1,0},{2,3},{3,2},{4,5},{5,4},{6,7},{7,6},{8,9},{9,8},{10,11... | collective-permute-start | bytes 786440 | tf_op jit(solution)/shard_map/ppermute | solution.py:22
  53.2 3.2 %collective-permute-start.24 = (f32[576,256]{1,0:T(8,128)S(1)}, f32[576,256]{1,0:T(8,128)S(1)}, u32[]{:S(2)}, u32[]{:S(2)}) collective-permute-start(f32[576,256]{1,0:T(8,128)S(1)} %constant_dynamic-update-slice_fusion), channel_id=1, source_target_pairs={{0,1},{1,0},{2,3},{3,2},{4,5},{5,4},{6,7},{7,6},{8,9},{9,8},{10,11... | collective-permute-start | bytes 1769480 | tf_op jit(solution)/shard_map/ppermute | solution.py:22
  56.3 2.1 %collective-permute-start.20 = (f32[576,256]{1,0:T(8,128)S(1)}, f32[576,256]{1,0:T(8,128)S(1)}, u32[]{:S(2)}, u32[]{:S(2)}) collective-permute-start(f32[576,256]{1,0:T(8,128)S(1)} %constant_dynamic-update-slice_fusion.4), channel_id=1, source_target_pairs={{0,1},{1,0},{2,3},{3,2},{4,5},{5,4},{6,7},{7,6},{8,9},{9,8},{10,11... | collective-permute-start | bytes 1769480 | tf_op jit(solution)/shard_map/ppermute | solution.py:22
  56.5 2.2 %copy-start.1 = (bf16[2048,1024]{1,0:T(8,128)(2,1)S(1)}, bf16[2048,1024]{1,0:T(8,128)(2,1)}, u32[]{:S(2)}) copy-start(bf16[2048,1024]{1,0:T(8,128)(2,1)} %a_hbm.1) | copy-start | bytes 12582916

commit v6 on v5

--- a/solution.py
+++ b/solution.py
@@ -255,8 +255,9 @@
     apply_moment(sketch_ref)
     gram(sketch_ref)
     inverse_factor(x_ref, w_ref)
-    for i in range(nb):
-        band = slice(i * EDGE, (i + 1) * EDGE)
+    half = time_steps // 2
+    for i in range(2):
+        band = slice(i * half, (i + 1) * half)
         back_ref[band, :] = (
             product(y_ref[band, :], w_ref[...], ((1,), (1,)), high) * factor
         ).astype(BF16)
@@ -271,8 +272,9 @@
         power[band, :] = product(a_ref[band, :], back_ref[...])
 
     inverse_factor(x_ref, w_ref, some_power)
-    for k in range(panels):
-        band = slice(k * share, (k + 1) * share)
+    half = a_ref.shape[0] // 2
+    for k in range(2):
+        band = slice(k * half, (k + 1) * half)
         range_ref[band, :] = product(power[band, :], w_ref[...], ((1,), (1,)), high).astype(BF16)
     mine = y_ref[pl.ds(pl.multiple_of(me_ref[0] * steps, steps), steps), :]
     coef_ref[...] = (product(mine, w_ref[...], ((1,), (1,)), high) * factor).astype(BF16)

time: 81.9 us -> 81.7 us (level)
  no operation moved by 1% of the time
where the time goes in v6:
time: 81.7 us; the launch traced here: 81.4 us
  starting transfers between devices  29.9 us (37%)
  Pallas kernels  25.5 us (31%)
  waiting for transfers between devices  19.5 us (24%)
  local copies, waits for them, and re-layouts  2.72 us (3%)
  other arithmetic  2.66 us (3%)
  between operations  1.11 us (1%)
    ppermute x25, starting transfers between devices, exchange(): return lax.ppermute(value, AXIS, [(i, i ^ distance) for i in range(n)])  29.9 us
    pallas_call x1, Pallas kernels, body(): pl.pallas_call(functools.partial(finish_kernel, chains, rows_total, facto...  22.5 us
    ppermute x25, waiting for transfers between devices, exchange(): return lax.ppermute(value, AXIS, [(i, i ^ distance) for i in range(n)])  19.5 us
    pallas_call x1, Pallas kernels, body(): pl.pallas_call(functools.partial(moment_kernel, chains), out_shape=[jax.S...  2.94 us
    add x6, other arithmetic, scatter_stage(): total = total + item  2.38 us
    unnamed x6, local copies, waits for them, and re-layouts  2.37 us
  transfers between devices with their start and end apart: 25, of which 15 were waited for; matrix products, arithmetic and copies ran while one was open for 4% of the time, Pallas kernels for 0%

profile of v6, /device:TPU:0, one launch (start us, length us, event | category | flops | bytes accessed | tf_op | source)
XLA Modules:
  0.0 81.4 jit_solution(11922078331531150503)
XLA Ops:
  0.6 0.0 copy-start
  0.7 2.2 %copy-done = bf16[2048,1024]{1,0:T(8,128)(2,1)S(1)} copy-done((bf16[2048,1024]{1,0:T(8,128)(2,1)S(1)}, bf16[2048,1024]{1,0:T(8,128)(2,1)}, u32[]{:S(2)}) %copy-start) | copy-done | bytes 4194328
  2.8 2.9 %shard_map.41 = (f32[1152,256]{1,0:T(8,128)S(1)}, f32[1152,256]{1,0:T(8,128)S(1)}) custom-call(bf16[2048,1024]{1,0:T(8,128)(2,1)S(1)} %copy-done), custom_call_target="tpu_custom_call" | custom-call | tf_op jit(solution)/shard_map/pallas_call | solution.py:293
  5.8 0.5 collective-permute-start
  6.4 0.1 collective-permute-start.4
  6.5 1.6 %collective-permute-done = f32[576,256]{1,0:T(8,128)} collective-permute-done((f32[576,256]{1,0:T(8,128)S(1)}, f32[576,256]{1,0:T(8,128)}, u32[]{:S(2)}, u32[]{:S(2)}) %collective-permute-start) | collective-permute-done | bytes 589856 | tf_op jit(solution)/shard_map/ppermute | solution.py:22
  8.1 1.1 %dynamic-slice_add_fusion.1 = f32[576,256]{1,0:T(8,128)S(1)} fusion(f32[576,256]{1,0:T(8,128)} %collective-permute-done, f32[1152,256]{1,0:T(8,128)S(1)} %get-tuple-element.10, s32[]{:T(128)S(6)} %select_n.65), kind=kLoop, calls=%fused_computation.3 | loop fusion | flops 147456 | bytes 1769476 | tf_op jit(solution)/shard_map/add | solution.py:35
  9.3 3.0 %collective-permute-start.1 = (f32[144,256]{1,0:T(8,128)S(1)}, f32[144,256]{1,0:T(8,128)S(1)}, u32[]{:S(2)}, u32[]{:S(2)}) collective-permute-start(f32[144,256]{1,0:T(8,128)S(1)} %get-tuple-element.23), channel_id=1, source_target_pairs={{0,2},{1,3},{2,0},{3,1},{4,6},{5,7},{6,4},{7,5},{8,10},{9,11},{10,... | collective-permute-start | bytes 442376 | tf_op jit(solution)/shard_map/ppermute | solution.py:22
  12.3 1.6 %collective-permute-start.2 = (f32[144,256]{1,0:T(8,128)S(1)}, f32[144,256]{1,0:T(8,128)S(1)}, u32[]{:S(2)}, u32[]{:S(2)}) collective-permute-start(f32[144,256]{1,0:T(8,128)S(1)} %get-tuple-element.25), channel_id=1, source_target_pairs={{0,4},{1,5},{2,6},{3,7},{4,0},{5,1},{6,2},{7,3},{8,12},{9,13},{10,... | collective-permute-start | bytes 442376 | tf_op jit(solution)/shard_map/ppermute | solution.py:22
  13.9 1.1 %dynamic-slice_add_fusion = f32[576,256]{1,0:T(8,128)S(1)} fusion(f32[576,256]{1,0:T(8,128)} %collective-permute-done.4, f32[1152,256]{1,0:T(8,128)S(1)} %get-tuple-element.11, s32[]{:T(128)S(6)} %select_n.65), kind=kLoop, calls=%fused_computation.2 | loop fusion | flops 147456 | bytes 1769476 | tf_op jit(solution)/shard_map/add | solution.py:35
  15.0 3.0 %collective-permute-start.5 = (bf16[64,256]{1,0:T(8,128)(2,1)S(1)}, bf16[64,256]{1,0:T(8,128)(2,1)S(1)}, u32[]{:S(2)}, u32[]{:S(2)}) collective-permute-start(bf16[64,256]{1,0:T(8,128)(2,1)S(1)} %copy-done.2), channel_id=1, source_target_pairs={{0,8},{1,9},{2,10},{3,11},{4,12},{5,13},{6,14},{7,15},{8,0},{9,1},... | collective-permute-start | bytes 98312 | tf_op jit(solution)/shard_map/ppermute | solution.py:22
  18.1 1.6 %collective-permute-start.12 = (f32[144,256]{1,0:T(8,128)S(1)}, f32[144,256]{1,0:T(8,128)S(1)}, u32[]{:S(2)}, u32[]{:S(2)}) collective-permute-start(f32[144,256]{1,0:T(8,128)S(1)} %get-tuple-element.20), channel_id=1, source_target_pairs={{0,2},{1,3},{2,0},{3,1},{4,6},{5,7},{6,4},{7,5},{8,10},{9,11},{10,... | collective-permute-start | bytes 442376 | tf_op jit(solution)/shard_map/ppermute | solution.py:22
  19.7 1.2 %collective-permute-done.5 = bf16[64,256]{1,0:T(8,128)(2,1)S(1)} collective-permute-done((bf16[64,256]{1,0:T(8,128)(2,1)S(1)}, bf16[64,256]{1,0:T(8,128)(2,1)S(1)}, u32[]{:S(2)}, u32[]{:S(2)}) %collective-permute-start.5) | collective-permute-done | bytes 32800 | tf_op jit(solution)/shard_map/ppermute | solution.py:22
  20.8 3.5 %collective-permute-start.13 = (f32[144,256]{1,0:T(8,128)S(1)}, f32[144,256]{1,0:T(8,128)S(1)}, u32[]{:S(2)}, u32[]{:S(2)}) collective-permute-start(f32[144,256]{1,0:T(8,128)S(1)} %get-tuple-element.22), channel_id=1, source_target_pairs={{0,4},{1,5},{2,6},{3,7},{4,0},{5,1},{6,2},{7,3},{8,12},{9,13},{10,... | collective-permute-start | bytes 442376 | tf_op jit(solution)/shard_map/ppermute | solution.py:22
  24.3 0.1 collective-permute-start.14
  24.5 3.0 %collective-permute-start.10 = (bf16[128,256]{1,0:T(8,128)(2,1)S(1)}, bf16[128,256]{1,0:T(8,128)(2,1)S(1)}, u32[]{:S(2)}, u32[]{:S(2)}) collective-permute-start(bf16[128,256]{1,0:T(8,128)(2,1)S(1)} %pad_maximum_fusion.2), channel_id=1, source_target_pairs={{0,6},{1,7},{2,4},{3,5},{4,2},{5,3},{6,0},{7,1},{8,14},{9,15},{10,... | collective-permute-start | bytes 196616 | tf_op jit(solution)/shard_map/ppermute | solution.py:22
  27.4 0.6 collective-permute-start.8
  28.0 0.2 collective-permute-start.9
  28.2 0.8 collective-permute-done.13
  29.0 2.0 %collective-permute-start.6 = (f32[72,256]{1,0:T(8,128)S(1)}, f32[72,256]{1,0:T(8,128)S(1)}, u32[]{:S(2)}, u32[]{:S(2)}) collective-permute-start(f32[72,256]{1,0:T(8,128)S(1)} %constant_dynamic-slice_fusion.4), channel_id=1, source_target_pairs={{0,8},{1,9},{2,10},{3,11},{4,12},{5,13},{6,14},{7,15},{8,0},{9,1},... | collective-permute-start | bytes 221192 | tf_op jit(solution)/shard_map/ppermute | solution.py:22
  31.0 1.9 %collective-permute-done.14 = f32[144,256]{1,0:T(8,128)S(1)} collective-permute-done((f32[144,256]{1,0:T(8,128)S(1)}, f32[144,256]{1,0:T(8,128)S(1)}, u32[]{:S(2)}, u32[]{:S(2)}) %collective-permute-start.14) | collective-permute-done | bytes 147488 | tf_op jit(solution)/shard_map/ppermute | solution.py:22
  33.0 1.3 %collective-permute-start.15 = (f32[72,256]{1,0:T(8,128)S(1)}, f32[72,256]{1,0:T(8,128)S(1)}, u32[]{:S(2)}, u32[]{:S(2)}) collective-permute-start(f32[72,256]{1,0:T(8,128)S(1)} %constant_dynamic-slice_fusion), channel_id=1, source_target_pairs={{0,8},{1,9},{2,10},{3,11},{4,12},{5,13},{6,14},{7,15},{8,0},{9,1},... | collective-permute-start | bytes 221192 | tf_op jit(solution)/shard_map/ppermute | solution.py:22
  34.3 1.0 %collective-permute-done.9 = bf16[128,256]{1,0:T(8,128)(2,1)S(1)} collective-permute-done((bf16[128,256]{1,0:T(8,128)(2,1)S(1)}, bf16[128,256]{1,0:T(8,128)(2,1)S(1)}, u32[]{:S(2)}, u32[]{:S(2)}) %collective-permute-start.9) | collective-permute-done | bytes 65568 | tf_op jit(solution)/shard_map/ppermute | solution.py:22
  35.4 0.5 collective-permute-done.6
  35.9 2.3 %collective-permute-start.7 = (f32[72,256]{1,0:T(8,128)S(1)}, f32[72,256]{1,0:T(8,128)S(1)}, u32[]{:S(2)}, u32[]{:S(2)}) collective-permute-start(f32[72,256]{1,0:T(8,128)S(1)} %dynamic-slice_add_fusion.3), channel_id=1, source_target_pairs={{0,8},{1,9},{2,10},{3,11},{4,12},{5,13},{6,14},{7,15},{8,0},{9,1},... | collective-permute-start | bytes 221192 | tf_op jit(solution)/shard_map/ppermute | solution.py:22
  38.2 3.1 %collective-permute-done.15 = f32[72,256]{1,0:T(8,128)S(1)} collective-permute-done((f32[72,256]{1,0:T(8,128)S(1)}, f32[72,256]{1,0:T(8,128)S(1)}, u32[]{:S(2)}, u32[]{:S(2)}) %collective-permute-start.15) | collective-permute-done | bytes 73760 | tf_op jit(solution)/shard_map/ppermute | solution.py:22
  41.3 0.1 collective-permute-start.16
  41.4 1.7 %collective-permute-done.7 = f32[72,256]{1,0:T(8,128)S(1)} collective-permute-done((f32[72,256]{1,0:T(8,128)S(1)}, f32[72,256]{1,0:T(8,128)S(1)}, u32[]{:S(2)}, u32[]{:S(2)}) %collective-permute-start.7) | collective-permute-done | bytes 73760 | tf_op jit(solution)/shard_map/ppermute | solution.py:22
  43.2 0.9 %collective-permute-start.21 = (f32[144,256]{1,0:T(8,128)S(1)}, f32[144,256]{1,0:T(8,128)S(1)}, u32[]{:S(2)}, u32[]{:S(2)}) collective-permute-start(f32[144,256]{1,0:T(8,128)S(1)} %maximum_select_fusion.2), channel_id=1, source_target_pairs={{0,2},{1,3},{2,0},{3,1},{4,6},{5,7},{6,4},{7,5},{8,10},{9,11},{10,... | collective-permute-start | bytes 442376 | tf_op jit(solution)/shard_map/ppermute | solution.py:22
  44.1 1.3 %collective-permute-start.22 = (f32[144,256]{1,0:T(8,128)S(1)}, f32[144,256]{1,0:T(8,128)S(1)}, u32[]{:S(2)}, u32[]{:S(2)}) collective-permute-start(f32[144,256]{1,0:T(8,128)S(1)} %maximum_select_fusion.2), channel_id=1, source_target_pairs={{0,4},{1,5},{2,6},{3,7},{4,0},{5,1},{6,2},{7,3},{8,12},{9,13},{10,... | collective-permute-start | bytes 442376 | tf_op jit(solution)/shard_map/ppermute | solution.py:22
  45.4 1.3 %collective-permute-start.23 = (f32[144,256]{1,0:T(8,128)S(1)}, f32[144,256]{1,0:T(8,128)S(1)}, u32[]{:S(2)}, u32[]{:S(2)}) collective-permute-start(f32[144,256]{1,0:T(8,128)S(1)} %maximum_select_fusion.2), channel_id=1, source_target_pairs={{0,6},{1,7},{2,4},{3,5},{4,2},{5,3},{6,0},{7,1},{8,14},{9,15},{10,... | collective-permute-start | bytes 442376 | tf_op jit(solution)/shard_map/ppermute | solution.py:22
  46.7 0.4 collective-permute-done.16
  47.2 0.6 collective-permute-start.17
  47.8 1.2 %collective-permute-start.18 = (f32[144,256]{1,0:T(8,128)S(1)}, f32[144,256]{1,0:T(8,128)S(1)}, u32[]{:S(2)}, u32[]{:S(2)}) collective-permute-start(f32[144,256]{1,0:T(8,128)S(1)} %get-tuple-element.19), channel_id=1, source_target_pairs={{0,4},{1,5},{2,6},{3,7},{4,0},{5,1},{6,2},{7,3},{8,12},{9,13},{10,... | collective-permute-start | bytes 442376 | tf_op jit(solution)/shard_map/ppermute | solution.py:22
  49.1 0.6 collective-permute-done.21
  49.8 1.6 %collective-permute-start.19 = (f32[144,256]{1,0:T(8,128)S(1)}, f32[144,256]{1,0:T(8,128)S(1)}, u32[]{:S(2)}, u32[]{:S(2)}) collective-permute-start(f32[144,256]{1,0:T(8,128)S(1)} %get-tuple-element.19), channel_id=1, source_target_pairs={{0,6},{1,7},{2,4},{3,5},{4,2},{5,3},{6,0},{7,1},{8,14},{9,15},{10,... | collective-permute-start | bytes 442376 | tf_op jit(solution)/shard_map/ppermute | solution.py:22
  51.3 0.1 collective-permute-start.11
  51.4 1.8 %collective-permute-done.23 = f32[144,256]{1,0:T(8,128)S(1)} collective-permute-done((f32[144,256]{1,0:T(8,128)S(1)}, f32[144,256]{1,0:T(8,128)S(1)}, u32[]{:S(2)}, u32[]{:S(2)}) %collective-permute-start.23) | collective-permute-done | bytes 147488 | tf_op jit(solution)/shard_map/ppermute | solution.py:22
  53.2 0.1 collective-permute-start.24
  53.3 1.1 %collective-permute-done.17 = f32[144,256]{1,0:T(8,128)S(1)} collective-permute-done((f32[144,256]{1,0:T(8,128)S(1)}, f32[144,256]{1,0:T(8,128)S(1)}, u32[]{:S(2)}, u32[]{:S(2)}) %collective-permute-start.17) | collective-permute-done | bytes 147488 | tf_op jit(solution)/shard_map/ppermute | solution.py:22
  54.4 0.4 collective-permute-done.18
  54.8 1.5 %collective-permute-done.19 = f32[144,256]{1,0:T(8,128)S(1)} collective-permute-done((f32[144,256]{1,0:T(8,128)S(1)}, f32[144,256]{1,0:T(8,128)S(1)}, u32[]{:S(2)}, u32[]{:S(2)}) %collective-permute-start.19) | collective-permute-done | bytes 147488 | tf_op jit(solution)/shard_map/ppermute | solution.py:22
  56.3 0.1 collective-permute-start.20
  56.5 0.1 maximum_select_fusion.1.refs_1_
  56.6 1.8 %collective-permute-done.20 = f32[576,256]{1,0:T(8,128)S(1)} collective-permute-done((f32[576,256]{1,0:T(8,128)S(1)}, f32[576,256]{1,0:T(8,128)S(1)}, u32[]{:S(2)}, u32[]{:S(2)}) %collective-permute-start.20) | collective-permute-done | bytes 589856 | tf_op jit(solution)/shard_map/ppermute | solution.py:22
  58.4 0.1 maximum_select_fusion.refs_0_
  58.5 0.2 copy-done.1
  58.7 22.5 %shard_map.42 = (bf16[2048,256]{1,0:T(8,128)(2,1)}, bf16[64,256]{1,0:T(8,128)(2,1)}) custom-call(s32[1]{0:T(128)} %bitcast.me_ref, bf16[1024,256]{1,0:T(8,128)(2,1)S(1)} %pad_maximum_fusion.sketch_ref, bf16[2048,1024]{1,0:T(8,128)(2,1)S(1)} %copy-done.1, f32[1152,256]{1,0:T(8,128)S(1)} %maximum_select_fusion.refs_0_, ...), custom_call_target="tpu_custom_call" | custom-call | tf_op jit(solution)/shard_map/pallas_call | solution.py:303
  (38 shorter events, 0.6 us)
Async XLA Ops:
  0.6 2.2 %copy-start = (bf16[2048,1024]{1,0:T(8,128)(2,1)S(1)}, bf16[2048,1024]{1,0:T(8,128)(2,1)}, u32[]{:S(2)}) copy-start(bf16[2048,1024]{1,0:T(8,128)(2,1)} %a_hbm.1) | copy-start | bytes 12582916
  5.8 2.3 %collective-permute-start = (f32[576,256]{1,0:T(8,128)S(1)}, f32[576,256]{1,0:T(8,128)}, u32[]{:S(2)}, u32[]{:S(2)}) collective-permute-start(f32[576,256]{1,0:T(8,128)S(1)} %constant_dynamic-slice_fusion.9), channel_id=1, source_target_pairs={{0,1},{1,0},{2,3},{3,2},{4,5},{5,4},{6,7},{7,6},{8,9},{9,8},{10,11... | collective-permute-start | bytes 1769480 | tf_op jit(solution)/shard_map/ppermute | solution.py:22
  6.4 7.5 %collective-permute-start.4 = (f32[576,256]{1,0:T(8,128)S(1)}, f32[576,256]{1,0:T(8,128)}, u32[]{:S(2)}, u32[]{:S(2)}) collective-permute-start(f32[576,256]{1,0:T(8,128)S(1)} %constant_dynamic-slice_fusion.5), channel_id=1, source_target_pairs={{0,1},{1,0},{2,3},{3,2},{4,5},{5,4},{6,7},{7,6},{8,9},{9,8},{10,11... | collective-permute-start | bytes 1769480 | tf_op jit(solution)/shard_map/ppermute | solution.py:22
  9.3 5.7 %copy-start.2 = (bf16[64,256]{1,0:T(8,128)(2,1)S(1)}, bf16[64,256]{1,0:T(8,128)(2,1)}, u32[]{:S(2)}) copy-start(bf16[64,256]{1,0:T(8,128)(2,1)} %param.3) | copy-start | bytes 98308
  9.3 15.0 %collective-permute-start.1 = (f32[144,256]{1,0:T(8,128)S(1)}, f32[144,256]{1,0:T(8,128)S(1)}, u32[]{:S(2)}, u32[]{:S(2)}) collective-permute-start(f32[144,256]{1,0:T(8,128)S(1)} %get-tuple-element.23), channel_id=1, source_target_pairs={{0,2},{1,3},{2,0},{3,1},{4,6},{5,7},{6,4},{7,5},{8,10},{9,11},{10,... | collective-permute-start | bytes 442376 | tf_op jit(solution)/shard_map/ppermute | solution.py:22
  12.3 12.2 %collective-permute-start.2 = (f32[144,256]{1,0:T(8,128)S(1)}, f32[144,256]{1,0:T(8,128)S(1)}, u32[]{:S(2)}, u32[]{:S(2)}) collective-permute-start(f32[144,256]{1,0:T(8,128)S(1)} %get-tuple-element.25), channel_id=1, source_target_pairs={{0,4},{1,5},{2,6},{3,7},{4,0},{5,1},{6,2},{7,3},{8,12},{9,13},{10,... | collective-permute-start | bytes 442376 | tf_op jit(solution)/shard_map/ppermute | solution.py:22
  13.8 10.6 %collective-permute-start.3 = (f32[144,256]{1,0:T(8,128)S(1)}, f32[144,256]{1,0:T(8,128)S(1)}, u32[]{:S(2)}, u32[]{:S(2)}) collective-permute-start(f32[144,256]{1,0:T(8,128)S(1)} %get-tuple-element.24), channel_id=1, source_target_pairs={{0,6},{1,7},{2,4},{3,5},{4,2},{5,3},{6,0},{7,1},{8,14},{9,15},{10,... | collective-permute-start | bytes 442376 | tf_op jit(solution)/shard_map/ppermute | solution.py:22
  15.0 5.8 %collective-permute-start.5 = (bf16[64,256]{1,0:T(8,128)(2,1)S(1)}, bf16[64,256]{1,0:T(8,128)(2,1)S(1)}, u32[]{:S(2)}, u32[]{:S(2)}) collective-permute-start(bf16[64,256]{1,0:T(8,128)(2,1)S(1)} %copy-done.2), channel_id=1, source_target_pairs={{0,8},{1,9},{2,10},{3,11},{4,12},{5,13},{6,14},{7,15},{8,0},{9,1},... | collective-permute-start | bytes 98312 | tf_op jit(solution)/shard_map/ppermute | solution.py:22
  18.1 9.9 %collective-permute-start.12 = (f32[144,256]{1,0:T(8,128)S(1)}, f32[144,256]{1,0:T(8,128)S(1)}, u32[]{:S(2)}, u32[]{:S(2)}) collective-permute-start(f32[144,256]{1,0:T(8,128)S(1)} %get-tuple-element.20), channel_id=1, source_target_pairs={{0,2},{1,3},{2,0},{3,1},{4,6},{5,7},{6,4},{7,5},{8,10},{9,11},{10,... | collective-permute-start | bytes 442376 | tf_op jit(solution)/shard_map/ppermute | solution.py:22
  20.8 8.1 %collective-permute-start.13 = (f32[144,256]{1,0:T(8,128)S(1)}, f32[144,256]{1,0:T(8,128)S(1)}, u32[]{:S(2)}, u32[]{:S(2)}) collective-permute-start(f32[144,256]{1,0:T(8,128)S(1)} %get-tuple-element.22), channel_id=1, source_target_pairs={{0,4},{1,5},{2,6},{3,7},{4,0},{5,1},{6,2},{7,3},{8,12},{9,13},{10,... | collective-permute-start | bytes 442376 | tf_op jit(solution)/shard_map/ppermute | solution.py:22
  24.3 8.6 %collective-permute-start.14 = (f32[144,256]{1,0:T(8,128)S(1)}, f32[144,256]{1,0:T(8,128)S(1)}, u32[]{:S(2)}, u32[]{:S(2)}) collective-permute-start(f32[144,256]{1,0:T(8,128)S(1)} %get-tuple-element.21), channel_id=1, source_target_pairs={{0,6},{1,7},{2,4},{3,5},{4,2},{5,3},{6,0},{7,1},{8,14},{9,15},{10,... | collective-permute-start | bytes 442376 | tf_op jit(solution)/shard_map/ppermute | solution.py:22
  24.5 9.9 %collective-permute-start.10 = (bf16[128,256]{1,0:T(8,128)(2,1)S(1)}, bf16[128,256]{1,0:T(8,128)(2,1)S(1)}, u32[]{:S(2)}, u32[]{:S(2)}) collective-permute-start(bf16[128,256]{1,0:T(8,128)(2,1)S(1)} %pad_maximum_fusion.2), channel_id=1, source_target_pairs={{0,6},{1,7},{2,4},{3,5},{4,2},{5,3},{6,0},{7,1},{8,14},{9,15},{10,... | collective-permute-start | bytes 196616 | tf_op jit(solution)/shard_map/ppermute | solution.py:22
  27.4 6.9 %collective-permute-start.8 = (bf16[128,256]{1,0:T(8,128)(2,1)S(1)}, bf16[128,256]{1,0:T(8,128)(2,1)S(1)}, u32[]{:S(2)}, u32[]{:S(2)}) collective-permute-start(bf16[128,256]{1,0:T(8,128)(2,1)S(1)} %pad_maximum_fusion.2), channel_id=1, source_target_pairs={{0,2},{1,3},{2,0},{3,1},{4,6},{5,7},{6,4},{7,5},{8,10},{9,11},{10,... | collective-permute-start | bytes 196616 | tf_op jit(solution)/shard_map/ppermute | solution.py:22
  28.0 7.3 %collective-permute-start.9 = (bf16[128,256]{1,0:T(8,128)(2,1)S(1)}, bf16[128,256]{1,0:T(8,128)(2,1)S(1)}, u32[]{:S(2)}, u32[]{:S(2)}) collective-permute-start(bf16[128,256]{1,0:T(8,128)(2,1)S(1)} %pad_maximum_fusion.2), channel_id=1, source_target_pairs={{0,4},{1,5},{2,6},{3,7},{4,0},{5,1},{6,2},{7,3},{8,12},{9,13},{10,... | collective-permute-start | bytes 196616 | tf_op jit(solution)/shard_map/ppermute | solution.py:22
  29.0 6.9 %collective-permute-start.6 = (f32[72,256]{1,0:T(8,128)S(1)}, f32[72,256]{1,0:T(8,128)S(1)}, u32[]{:S(2)}, u32[]{:S(2)}) collective-permute-start(f32[72,256]{1,0:T(8,128)S(1)} %constant_dynamic-slice_fusion.4), channel_id=1, source_target_pairs={{0,8},{1,9},{2,10},{3,11},{4,12},{5,13},{6,14},{7,15},{8,0},{9,1},... | collective-permute-start | bytes 221192 | tf_op jit(solution)/shard_map/ppermute | solution.py:22
  33.0 8.3 %collective-permute-start.15 = (f32[72,256]{1,0:T(8,128)S(1)}, f32[72,256]{1,0:T(8,128)S(1)}, u32[]{:S(2)}, u32[]{:S(2)}) collective-permute-start(f32[72,256]{1,0:T(8,128)S(1)} %constant_dynamic-slice_fusion), channel_id=1, source_target_pairs={{0,8},{1,9},{2,10},{3,11},{4,12},{5,13},{6,14},{7,15},{8,0},{9,1},... | collective-permute-start | bytes 221192 | tf_op jit(solution)/shard_map/ppermute | solution.py:22
  35.9 7.3 %collective-permute-start.7 = (f32[72,256]{1,0:T(8,128)S(1)}, f32[72,256]{1,0:T(8,128)S(1)}, u32[]{:S(2)}, u32[]{:S(2)}) collective-permute-start(f32[72,256]{1,0:T(8,128)S(1)} %dynamic-slice_add_fusion.3), channel_id=1, source_target_pairs={{0,8},{1,9},{2,10},{3,11},{4,12},{5,13},{6,14},{7,15},{8,0},{9,1},... | collective-permute-start | bytes 221192 | tf_op jit(solution)/shard_map/ppermute | solution.py:22
  41.3 5.8 %collective-permute-start.16 = (f32[72,256]{1,0:T(8,128)S(1)}, f32[72,256]{1,0:T(8,128)S(1)}, u32[]{:S(2)}, u32[]{:S(2)}) collective-permute-start(f32[72,256]{1,0:T(8,128)S(1)} %dynamic-slice_add_fusion.2), channel_id=1, source_target_pairs={{0,8},{1,9},{2,10},{3,11},{4,12},{5,13},{6,14},{7,15},{8,0},{9,1},... | collective-permute-start | bytes 221192 | tf_op jit(solution)/shard_map/ppermute | solution.py:22
  43.2 6.6 %collective-permute-start.21 = (f32[144,256]{1,0:T(8,128)S(1)}, f32[144,256]{1,0:T(8,128)S(1)}, u32[]{:S(2)}, u32[]{:S(2)}) collective-permute-start(f32[144,256]{1,0:T(8,128)S(1)} %maximum_select_fusion.2), channel_id=1, source_target_pairs={{0,2},{1,3},{2,0},{3,1},{4,6},{5,7},{6,4},{7,5},{8,10},{9,11},{10,... | collective-permute-start | bytes 442376 | tf_op jit(solution)/shard_map/ppermute | solution.py:22
  44.1 7.3 %collective-permute-start.22 = (f32[144,256]{1,0:T(8,128)S(1)}, f32[144,256]{1,0:T(8,128)S(1)}, u32[]{:S(2)}, u32[]{:S(2)}) collective-permute-start(f32[144,256]{1,0:T(8,128)S(1)} %maximum_select_fusion.2), channel_id=1, source_target_pairs={{0,4},{1,5},{2,6},{3,7},{4,0},{5,1},{6,2},{7,3},{8,12},{9,13},{10,... | collective-permute-start | bytes 442376 | tf_op jit(solution)/shard_map/ppermute | solution.py:22
  45.4 7.8 %collective-permute-start.23 = (f32[144,256]{1,0:T(8,128)S(1)}, f32[144,256]{1,0:T(8,128)S(1)}, u32[]{:S(2)}, u32[]{:S(2)}) collective-permute-start(f32[144,256]{1,0:T(8,128)S(1)} %maximum_select_fusion.2), channel_id=1, source_target_pairs={{0,6},{1,7},{2,4},{3,5},{4,2},{5,3},{6,0},{7,1},{8,14},{9,15},{10,... | collective-permute-start | bytes 442376 | tf_op jit(solution)/shard_map/ppermute | solution.py:22
  47.2 7.1 %collective-permute-start.17 = (f32[144,256]{1,0:T(8,128)S(1)}, f32[144,256]{1,0:T(8,128)S(1)}, u32[]{:S(2)}, u32[]{:S(2)}) collective-permute-start(f32[144,256]{1,0:T(8,128)S(1)} %get-tuple-element.19), channel_id=1, source_target_pairs={{0,2},{1,3},{2,0},{3,1},{4,6},{5,7},{6,4},{7,5},{8,10},{9,11},{10,... | collective-permute-start | bytes 442376 | tf_op jit(solution)/shard_map/ppermute | solution.py:22
  47.8 7.0 %collective-permute-start.18 = (f32[144,256]{1,0:T(8,128)S(1)}, f32[144,256]{1,0:T(8,128)S(1)}, u32[]{:S(2)}, u32[]{:S(2)}) collective-permute-start(f32[144,256]{1,0:T(8,128)S(1)} %get-tuple-element.19), channel_id=1, source_target_pairs={{0,4},{1,5},{2,6},{3,7},{4,0},{5,1},{6,2},{7,3},{8,12},{9,13},{10,... | collective-permute-start | bytes 442376 | tf_op jit(solution)/shard_map/ppermute | solution.py:22
  49.8 6.6 %collective-permute-start.19 = (f32[144,256]{1,0:T(8,128)S(1)}, f32[144,256]{1,0:T(8,128)S(1)}, u32[]{:S(2)}, u32[]{:S(2)}) collective-permute-start(f32[144,256]{1,0:T(8,128)S(1)} %get-tuple-element.19), channel_id=1, source_target_pairs={{0,6},{1,7},{2,4},{3,5},{4,2},{5,3},{6,0},{7,1},{8,14},{9,15},{10,... | collective-permute-start | bytes 442376 | tf_op jit(solution)/shard_map/ppermute | solution.py:22
  51.3 5.1 %collective-permute-start.11 = (bf16[512,256]{1,0:T(8,128)(2,1)S(1)}, bf16[512,256]{1,0:T(8,128)(2,1)S(1)}, u32[]{:S(2)}, u32[]{:S(2)}) collective-permute-start(bf16[512,256]{1,0:T(8,128)(2,1)S(1)} %pad_maximum_fusion.1), channel_id=1, source_target_pairs={{0,1},{1,0},{2,3},{3,2},{4,5},{5,4},{6,7},{7,6},{8,9},{9,8},{10,11... | collective-permute-start | bytes 786440 | tf_op jit(solution)/shard_map/ppermute | solution.py:22
  53.2 3.2 %collective-permute-start.24 = (f32[576,256]{1,0:T(8,128)S(1)}, f32[576,256]{1,0:T(8,128)S(1)}, u32[]{:S(2)}, u32[]{:S(2)}) collective-permute-start(f32[576,256]{1,0:T(8,128)S(1)} %constant_dynamic-update-slice_fusion), channel_id=1, source_target_pairs={{0,1},{1,0},{2,3},{3,2},{4,5},{5,4},{6,7},{7,6},{8,9},{9,8},{10,11... | collective-permute-start | bytes 1769480 | tf_op jit(solution)/shard_map/ppermute | solution.py:22
  56.3 2.1 %collective-permute-start.20 = (f32[576,256]{1,0:T(8,128)S(1)}, f32[576,256]{1,0:T(8,128)S(1)}, u32[]{:S(2)}, u32[]{:S(2)}) collective-permute-start(f32[576,256]{1,0:T(8,128)S(1)} %constant_dynamic-update-slice_fusion.4), channel_id=1, source_target_pairs={{0,1},{1,0},{2,3},{3,2},{4,5},{5,4},{6,7},{7,6},{8,9},{9,8},{10,11... | collective-permute-start | bytes 1769480 | tf_op jit(solution)/shard_map/ppermute | solution.py:22
  56.5 2.2 %copy-start.1 = (bf16[2048,1024]{1,0:T(8,128)(2,1)S(1)}, bf16[2048,1024]{1,0:T(8,128)(2,1)}, u32[]{:S(2)}) copy-start(bf16[2048,1024]{1,0:T(8,128)(2,1)} %a_hbm.1) | copy-start | bytes 12582916
